TPU v7x, 256 devices: a whole 4x4x8 slice. The times are simulated.
256 devices in a mesh: prompt: 16 (over x, z_hi), comp: 16 (over z_lo, y, core).
Axes of the slice: x: 4, y: 4, z: 8 (z_hi: 4, z_lo: 2; z = z_hi * 2 + z_lo), core: 2. Of those that a mesh axis runs over, the one named last changes fastest.
Arguments:
- normed_hidden_input: bfloat16 [16, 2048, 5120], P('comp', 'prompt'), may hold values from -6 to 6
- frozen_query_base: bfloat16 [16, 2048, 2560], P('comp', 'prompt'), may hold values from -5 to 5
- attention_output_grad: bfloat16 [16, 2048, 2560], P('comp', 'prompt'), may hold values from -6 to 6
- completion_keys: bfloat16 [16, 2048, 512], P('comp', 'prompt'), may hold values from -6 to 6
- completion_values: bfloat16 [16, 2048, 512], P('comp', 'prompt'), may hold values from -6 to 6
- owner_prompt_keys: bfloat16 [16, 2048, 512], P('comp', 'prompt'), may hold values from -5 to 5
- owner_prompt_values: bfloat16 [16, 2048, 512], P('comp', 'prompt'), may hold values from -6 to 6
- adapter_down_weight: bfloat16 [5120, 64], replicated, may hold values from -0.078125 to 0.078125
- adapter_up_weight: bfloat16 [64, 2560], replicated, may hold values from -0.75 to 0.75
- adapter_rank: int32 [1], replicated, may hold values from 16 to 64
- route: int32 [16, 16, 16], P('comp', 'prompt'), may hold values from 0 to 15, each once within a row
- lengths: int32 [16, 16, 16], P('comp', 'prompt'), may hold values from 1 to 8, as said below
Outputs:
- grad_query: bfloat16 [16, 2048, 2560], P('comp', 'prompt')
- grad_self_keys: bfloat16 [16, 2048, 512], P('comp', 'prompt')
- grad_self_values: bfloat16 [16, 2048, 512], P('comp', 'prompt')
- grad_prompt_keys: bfloat16 [16, 2048, 512], P('comp', 'prompt')
- grad_prompt_values: bfloat16 [16, 2048, 512], P('comp', 'prompt')
- grad_down: float32 [5120, 64], replicated
- grad_up: float32 [64, 2560], replicated
Inputs may be any that keep to these rules, and one draw needn't show every extreme that they name: `route`: each device's 16 entries name every owner of its group once. `lengths`: every device holds a completion of full length 8.
All inputs are finite; a program needn't handle non-finite values.
Results may differ from a plain program's by a relative error of at most 0.013.
The roundings to bfloat16 on the way count: a program that leaves them out, or rounds other values in their place, can miss the bound.
Values may be sent and summed in bfloat16 or wider, within the bound.
No kernel may reach another device: no remote copies, remote signals or barrier semaphores. Data moves between devices by JAX's collectives and lax.ppermute only.
A program may use at most 64 MiB of HBM per device.

v0:
```python
import math

import jax
import jax.numpy as jnp
from jax import lax
from jax.sharding import PartitionSpec as P

KEY_VALUE_HEADS = 4
GROUP = 5
HEAD_SIZE = 128
PLEN = 128
CL = 8


adapter_strength = 32.0
masked_score = -1e30


def merge_stats(top_a, total_a, top_b, total_b):
    top = jnp.maximum(top_a, top_b)
    return top + jnp.log(total_a * jnp.exp(top_a - top) + total_b * jnp.exp(top_b - top))


def per_device(
    normed_hidden_input,
    frozen_query_base,
    attention_output_grad,
    completion_keys,
    completion_values,
    owner_prompt_keys,
    owner_prompt_values,
    adapter_down_weight,
    adapter_up_weight,
    adapter_rank,
    route,
    lengths,
):
    count = lax.axis_size("prompt")
    token_rows = count * CL
    inv_sqrt = 1.0 / math.sqrt(HEAD_SIZE)
    hidden_rows = normed_hidden_input[0]
    owner_order = route[0, 0]
    length_list = lengths[0, 0]
    rank_value = adapter_rank[0]
    keep_mask = (jnp.arange(adapter_down_weight.shape[1]) < rank_value).astype(jnp.float32)
    adapter_scale = adapter_strength / rank_value.astype(jnp.float32)
    low_rank_rows = (
        jnp.dot(hidden_rows, adapter_down_weight, preferred_element_type=jnp.float32) * keep_mask
    ).astype(jnp.bfloat16)
    query = (
        frozen_query_base[0].astype(jnp.float32)
        + adapter_scale
        * jnp.dot(low_rank_rows, adapter_up_weight, preferred_element_type=jnp.float32)
    ).astype(jnp.bfloat16)
    q_slots = query.reshape(count, CL, KEY_VALUE_HEADS, GROUP, HEAD_SIZE)
    sk_slots = completion_keys[0].reshape(count, CL, KEY_VALUE_HEADS, HEAD_SIZE)
    sv_slots = completion_values[0].reshape(count, CL, KEY_VALUE_HEADS, HEAD_SIZE)
    positions = jnp.arange(CL)
    causal = positions[None, :] <= positions[:, None]
    ss = (
        jnp.einsum("sqkgd,stkd->sqkgt", q_slots, sk_slots, preferred_element_type=jnp.float32)
        * inv_sqrt
    )
    ss = jnp.where(causal[None, :, None, None, :], ss, masked_score)
    self_top = jnp.max(ss, -1)
    self_total = jnp.sum(jnp.exp(ss - self_top[..., None]), -1)
    live = (positions[None, :] < length_list[:, None]).reshape(token_rows)
    gmask = attention_output_grad[0] * live.astype(jnp.bfloat16)[:, None]
    g_slots = gmask.reshape(count, CL, KEY_VALUE_HEADS, GROUP, HEAD_SIZE)
    g_wide = g_slots.astype(jnp.float32)
    slot_ids = jnp.arange(count)
    inverse = jnp.sum(jnp.where(owner_order[:, None] == slot_ids[None, :], slot_ids[:, None], 0), 0)
    all_keys, all_vals = (
        lax.all_gather(owner_prompt_keys[0], "prompt", axis=0, tiled=True),
        lax.all_gather(owner_prompt_values[0], "prompt", axis=0, tiled=True),
    )
    sel_keys = jnp.take(
        all_keys.reshape(count, PLEN, KEY_VALUE_HEADS, HEAD_SIZE), owner_order, axis=0
    )
    sel_vals = jnp.take(
        all_vals.reshape(count, PLEN, KEY_VALUE_HEADS, HEAD_SIZE), owner_order, axis=0
    )
    sp = (
        jnp.einsum("sqkgd,spkd->sqkgp", q_slots, sel_keys, preferred_element_type=jnp.float32)
        * inv_sqrt
    )
    top_p = jnp.max(sp, -1)
    total_p = jnp.sum(jnp.exp(sp - top_p[..., None]), -1)
    lse_slots = merge_stats(top_p, total_p, self_top, self_total)
    pp = jnp.exp(sp - lse_slots[..., None])
    ppb = pp.astype(jnp.bfloat16)
    out_p = jnp.einsum("sqkgp,spkd->sqkgd", ppb, sel_vals, preferred_element_type=jnp.float32)
    ps = jnp.exp(ss - lse_slots[..., None])
    psb = ps.astype(jnp.bfloat16)
    out_s = jnp.einsum("sqkgt,stkd->sqkgd", psb, sv_slots, preferred_element_type=jnp.float32)
    ps, psb, out_s = (ps, psb, out_s)
    delta = jnp.sum(g_wide * (out_p + out_s), -1)
    dpp = jnp.einsum("sqkgd,spkd->sqkgp", g_slots, sel_vals, preferred_element_type=jnp.float32)
    dsp = (pp * (dpp - delta[..., None])).astype(jnp.bfloat16)
    dq_prompt = (
        jnp.einsum("sqkgp,spkd->sqkgd", dsp, sel_keys, preferred_element_type=jnp.float32)
        * inv_sqrt
    )
    part_k = (
        jnp.einsum("sqkgp,sqkgd->spkd", dsp, q_slots, preferred_element_type=jnp.float32) * inv_sqrt
    )
    part_v = jnp.einsum("sqkgp,sqkgd->spkd", ppb, g_slots, preferred_element_type=jnp.float32)
    by_owner_k = jnp.take(part_k, inverse, axis=0).reshape(
        count * PLEN, KEY_VALUE_HEADS * HEAD_SIZE
    )
    by_owner_v = jnp.take(part_v, inverse, axis=0).reshape(
        count * PLEN, KEY_VALUE_HEADS * HEAD_SIZE
    )
    summed_k, summed_v = (
        lax.psum_scatter(by_owner_k, "prompt", scatter_dimension=0, tiled=True),
        lax.psum_scatter(by_owner_v, "prompt", scatter_dimension=0, tiled=True),
    )
    dps = jnp.einsum("sqkgd,stkd->sqkgt", g_slots, sv_slots, preferred_element_type=jnp.float32)
    dss = (ps * (dps - delta[..., None])).astype(jnp.bfloat16)
    dq_self = (
        jnp.einsum("sqkgt,stkd->sqkgd", dss, sk_slots, preferred_element_type=jnp.float32)
        * inv_sqrt
    )
    self_key_grad = (
        (
            jnp.einsum("sqkgt,sqkgd->stkd", dss, q_slots, preferred_element_type=jnp.float32)
            * inv_sqrt
        )
        .reshape(token_rows, KEY_VALUE_HEADS * HEAD_SIZE)
        .astype(jnp.bfloat16)
    )
    self_value_grad = (
        jnp.einsum("sqkgt,sqkgd->stkd", psb, g_slots, preferred_element_type=jnp.float32)
        .reshape(token_rows, KEY_VALUE_HEADS * HEAD_SIZE)
        .astype(jnp.bfloat16)
    )
    dq_total = dq_prompt + dq_self
    query_grad_adapter = dq_total.reshape(token_rows, KEY_VALUE_HEADS * GROUP * HEAD_SIZE).astype(
        jnp.bfloat16
    )
    up_gradient = adapter_scale * jnp.dot(
        low_rank_rows.T, query_grad_adapter, preferred_element_type=jnp.float32
    )
    lifted_rows = (
        adapter_scale
        * jnp.dot(query_grad_adapter, adapter_up_weight.T, preferred_element_type=jnp.float32)
        * keep_mask
    ).astype(jnp.bfloat16)
    down_gradient = jnp.dot(hidden_rows.T, lifted_rows, preferred_element_type=jnp.float32)
    down_gradient, up_gradient = lax.psum((down_gradient, up_gradient), ("prompt", "comp"))
    return (
        query_grad_adapter[None],
        self_key_grad[None],
        self_value_grad[None],
        summed_k.astype(jnp.bfloat16)[None],
        summed_v.astype(jnp.bfloat16)[None],
        down_gradient,
        up_gradient,
    )


def solution(mesh):
    placed = (
        P("comp", "prompt", None),
        P("comp", "prompt", None),
        P("comp", "prompt", None),
        P("comp", "prompt", None),
        P("comp", "prompt", None),
        P("comp", "prompt", None),
        P("comp", "prompt", None),
        P(),
        P(),
        P(),
        P("comp", "prompt", None),
        P("comp", "prompt", None),
    )
    return jax.shard_map(
        per_device,
        mesh=mesh,
        in_specs=placed,
        out_specs=(
            P("comp", "prompt", None),
            P("comp", "prompt", None),
            P("comp", "prompt", None),
            P("comp", "prompt", None),
            P("comp", "prompt", None),
            P(),
            P(),
        ),
        check_vma=False,
    )
```

profile of v0, /device:TPU:1, one launch (start us, length us, event | category | flops | bytes accessed | tf_op | source)
XLA Modules:
  0.0 652.2 jit_solution(8461387529062394522)
XLA Ops:
  14.1 2.5 fusion.98
  19.8 53.7 %all-gather.5.cloned.1.call-done = bf16[1,2048,512]{2,1,0:T(8,128)(2,1)} async-done(((bf16[1,128,512]{2,1,0:T(8,128)(2,1)}), bf16[1,2048,512]{2,1,0:T(8,128)(2,1)}) %all-gather.5.cloned.1.call-update) | async-done | bytes 2097168 | tf_op jit(solution)/shard_map/all_gather | solution.py:74
  73.4 4.0 reshape.198
  77.4 3.5 copy.41
  80.9 52.4 %all-gather.7.cloned.1.call-done = bf16[1,2048,512]{2,1,0:T(8,128)(2,1)} async-done(((bf16[1,128,512]{2,1,0:T(8,128)(2,1)}), bf16[1,2048,512]{2,1,0:T(8,128)(2,1)}) %all-gather.7.cloned.1.call-update) | async-done | bytes 2097168 | tf_op jit(solution)/shard_map/all_gather | solution.py:75
  133.3 4.0 reshape.199
  137.3 3.5 copy.43
  140.8 3.8 gather_fusion
  144.5 3.8 gather_fusion.1
  148.3 3.3 fusion.99
  153.8 3.1 convolution_bitcast_fusion.1
  160.8 2.7 fusion
  163.5 5.1 gather_fusion.3
  168.6 5.1 gather_fusion.2
  173.7 6.8 %broadcast_select_fusion = (f32[16,128,4,128]{1,3,2,0:T(8,128)}, f32[16,128,4,128]{1,3,2,0:T(8,128)S(1)}) fusion(f32[16,128,4,128]{1,3,2,0:T(8,128)} %gather_fusion.3, pred[16]{0:T(512)(128)(4,1)} %compare_and_fusion, f32[16,128,4,128]{1,3,2,0:T(8,128)} %gather_fusion.2), kind=kLoop, calls=%fused_computation.22 | loop fusion | flops 2097152 | bytes 16777232 | tf_op jit(solution)/shard_map/jit(_take)/select_n | solution.py:111
  182.9 3.9 copy.71
  186.9 4.6 copy.48
  191.5 3.9 copy.70
  195.8 3.9 fusion.47
  203.3 3.2 convolution_bitcast_fusion
  209.9 71.2 %reduce-scatter.3.cloned.1.call-done = f32[128,512]{0,1:T(8,128)} async-done(((f32[2048,512]{0,1:T(8,128)}), f32[128,512]{0,1:T(8,128)}) %reduce-scatter.3.cloned.1.call-update) | async-done | bytes 262160 | tf_op jit(solution)/shard_map/reduce_scatter | solution.py:115
  282.8 95.0 %reduce-scatter.5.cloned.1.call-done = f32[128,512]{0,1:T(8,128)} async-done(((f32[2048,512]{0,1:T(8,128)}), f32[128,512]{0,1:T(8,128)}) %reduce-scatter.5.cloned.1.call-update) | async-done | bytes 262160 | tf_op jit(solution)/shard_map/reduce_scatter | solution.py:116
  379.5 262.7 %all-reduce.3.cloned.1.call-done = (f32[5120,64]{0,1:T(8,128)}, f32[64,2560]{1,0:T(8,128)}) async-done(((f32[5120,64]{0,1:T(8,128)}, f32[64,2560]{1,0:T(8,128)}), (f32[5120,64]{0,1:T(8,128)}, f32[64,2560]{1,0:T(8,128)})) %all-reduce.3.cloned.1.call-update) | async-done | bytes 1966096 | tf_op jit(solution)/shard_map/psum | solution.py:150
  642.2 2.5 copy.75
  (93 shorter events, 29.2 us)
Async XLA Ops:
  7.2 4.3 copy-start
  7.2 6.0 copy-start.9
  7.2 6.0 copy-start.11
  7.2 66.2 %all-gather.5.cloned.1.call-start = ((), (), s32[]{:S(2)}) async-start(), calls=%async_computation.4 | async-start | bytes 2228224 | tf_op jit(solution)/shard_map/all_gather | solution.py:74
  7.9 125.3 %all-gather.7.cloned.1.call-start = ((), (), s32[]{:S(2)}) async-start(), calls=%async_computation.5 | async-start | bytes 2228224 | tf_op jit(solution)/shard_map/all_gather | solution.py:75
  8.7 272.3 %reduce-scatter.3.cloned.1.call-start = ((), (), s32[]{:S(2)}) async-start(), calls=%async_computation.2 | async-start | bytes 4456448 | tf_op jit(solution)/shard_map/reduce_scatter | solution.py:115
  9.4 4.1 copy-start.19
  16.6 2.0 copy-start.21
  16.6 2.5 copy-start.20
  18.6 129.7 %copy-start.22 = (pred[16]{0:T(512)(128)(4,1)}, pred[16]{0:T(512)(128)(4,1)S(1)}, u32[]{:S(2)}) copy-start(pred[16]{0:T(512)(128)(4,1)S(1)} %compare_and_fusion.1) | copy-start | bytes 52
  151.5 1.1 copy-start.13
  152.7 1.1 copy-start.3
  152.7 1.1 copy-start.17
  153.8 3.1 copy-start.8
  153.8 3.1 copy-start.23
  157.9 2.0 copy-start.16
  186.9 190.9 %reduce-scatter.5.cloned.1.call-start = ((), (), s32[]{:S(2)}) async-start(), calls=%async_computation.3 | async-start | bytes 4456448 | tf_op jit(solution)/shard_map/reduce_scatter | solution.py:116
  195.5 446.7 %all-reduce.3.cloned.1.call-start = ((), (), s32[]{:S(2)}) async-start(), calls=%async_computation.6 | async-start | bytes 3932160 | tf_op jit(solution)/shard_map/psum | solution.py:150
  195.8 3.9 copy-start.7
  195.8 3.9 copy-start.24
  195.8 3.9 copy-start.26
  206.5 2.2 copy-start.18
  206.5 2.2 copy-start.4
  642.2 2.5 copy-start.12
  (8 other events, 7.2 us)
Sparse Core Ops, SparseCore 0:
  10.5 62.9 all-gather.4
  75.9 57.3 all-gather.6
  187.0 93.9 reduce-scatter.2
  285.0 92.7 reduce-scatter.4
  383.7 258.4 all-reduce.2
where the time goes:
time: 654 us; the launch traced here: 652 us
  waiting for transfers between devices  536 us (82%)
  local copies, waits for them, and re-layouts  56.3 us (9%)
  matrix products  29.9 us (5%)
  between operations  14.8 us (2%)
  other arithmetic  14.2 us (2%)
    psum x1, waiting for transfers between devices, per_device(): lax.psum((down_gradient, up_gradient), ('prompt', 'comp'))  263 us
    reduce_scatter x1, waiting for transfers between devices, per_device(): lax.psum_scatter(by_owner_v, 'prompt', scatter_dimension=0, tiled=True)  95 us
    reduce_scatter x1, waiting for transfers between devices, per_device(): lax.psum_scatter(by_owner_k, 'prompt', scatter_dimension=0, tiled=True)  71.2 us
    all_gather x1, waiting for transfers between devices, per_device(): lax.all_gather(owner_prompt_keys[0], 'prompt', axis=0, tiled=True)  53.7 us
    all_gather x1, waiting for transfers between devices, per_device(): lax.all_gather(owner_prompt_values[0], 'prompt', axis=0, tiled=True)  52.4 us
    unnamed x60, local copies, waits for them, and re-layouts  16.7 us
  transfers between devices with their start and end apart: 5, of which 5 were waited for; matrix products, arithmetic and copies ran while one was open for 6% of the time, Pallas kernels for 0%

commit v1 on v0

v1 whole, which is shorter than its diff:
```python
import math

import jax
import jax.numpy as jnp
from jax import lax
from jax.experimental import pallas as pl
from jax.experimental.pallas import tpu as pltpu
from jax.sharding import PartitionSpec as P

KEY_VALUE_HEADS = 4
GROUP = 5
HEAD_SIZE = 128
PLEN = 128
CL = 8
SLOTS = 16
TOKENS = SLOTS * CL
QUERY_HEADS = KEY_VALUE_HEADS * GROUP
PAIRS = QUERY_HEADS // 2
HALF = PAIRS * HEAD_SIZE
KV_HALF = KEY_VALUE_HEADS * HEAD_SIZE // 2
ROWS = 2 * TOKENS
MODEL_WIDTH = 5120
PADDED_RANK = 64
QUERY_WIDTH = QUERY_HEADS * HEAD_SIZE
SEND_WIDTH = 2 * HALF + 128
BACK_WIDTH = HALF + 128
DOWN_BLOCKS = MODEL_WIDTH // 128
GRAD_BLOCKS = (MODEL_WIDTH + QUERY_WIDTH) // 128

INV_SQRT = 1.0 / math.sqrt(HEAD_SIZE)
adapter_strength = 32.0
masked_score = -1e30

BF16 = jnp.bfloat16
F32 = jnp.float32


def dot(a, b, dims):
    return lax.dot_general(a, b, (dims, ((), ())), preferred_element_type=F32)


def nt(a, b):
    return dot(a, b, ((1,), (1,)))


def nn(a, b):
    return dot(a, b, ((1,), (0,)))


def tn(a, b):
    return dot(a, b, ((0,), (0,)))


def fold(wide):
    width = wide.shape[1] // 2
    left = wide[:, :width].reshape(SLOTS, 1, CL, width)
    right = wide[:, width:].reshape(SLOTS, 1, CL, width)
    return jnp.concatenate([left, right], axis=1).reshape(ROWS, width)


def unfold(rows):
    split = rows.reshape(SLOTS, 2, CL, rows.shape[1])
    return split[:, 0].reshape(TOKENS, -1), split[:, 1].reshape(TOKENS, -1)


def own_mask():
    key = lax.broadcasted_iota(jnp.int32, (ROWS, ROWS), 0)
    row = lax.broadcasted_iota(jnp.int32, (ROWS, ROWS), 1)
    return (key // CL == row // CL) & (key <= row)


def pack_stats(rows):
    value = jnp.concatenate(rows, axis=0)
    first = value.astype(BF16).astype(F32)
    rest = value - first
    second = rest.astype(BF16).astype(F32)
    third = rest - second
    pad = jnp.zeros((128 - 3 * len(rows), ROWS), F32)
    return jnp.concatenate([first, second, third, pad], axis=0).T.astype(BF16)


def unpack_stats(columns, count):
    parts = columns.astype(F32).T
    return parts[:count] + (parts[count : 2 * count] + parts[2 * count : 3 * count])


def prepare_kernel(
    rank_ref, route_ref, length_ref, x_ref, base_ref, g_ref, sk_ref, sv_ref, wd_ref, wu_ref,
    low_ref, send_ref, rows_ref,
):
    rank = rank_ref[0]
    scale = adapter_strength / rank.astype(F32)
    keep = lax.broadcasted_iota(jnp.int32, (TOKENS, PADDED_RANK), 1) < rank
    low = jnp.where(keep, nn(x_ref[...], wd_ref[...]), 0.0).astype(BF16)
    low_ref[...] = low
    query = base_ref[...].astype(F32) + scale * nn(low, wu_ref[...])
    rows_ref[:, :HALF] = fold(query).astype(BF16)
    position = lax.broadcasted_iota(jnp.int32, (CL, 128), 0)
    live = jnp.concatenate(
        [jnp.where(position < length_ref[0, 0, s], 1.0, 0.0) for s in range(SLOTS)], axis=0
    )
    for n in range(PAIRS):
        left, right = (g_ref[:, m * 128 : (m + 1) * 128].astype(F32) * live for m in (n, n + PAIRS))
        rows_ref[:, HALF + n * 128 : HALF + (n + 1) * 128] = fold(
            jnp.concatenate([left, right], axis=1)
        ).astype(BF16)
    keys = fold(sk_ref[...].astype(F32)).astype(BF16)
    values = fold(sv_ref[...].astype(F32)).astype(BF16)
    mask = own_mask()
    lses, deltas = [], []
    for b in range(PAIRS):
        h = b // GROUP
        q = rows_ref[:, b * 128 : (b + 1) * 128]
        g = rows_ref[:, HALF + b * 128 : HALF + (b + 1) * 128]
        scores = jnp.where(mask, nt(keys[:, h * 128 : (h + 1) * 128], q) * INV_SQRT, masked_score)
        top = jnp.max(scores, axis=0, keepdims=True)
        weight = jnp.exp(scores - top)
        total = jnp.sum(weight, axis=0, keepdims=True)
        dprob = nt(values[:, h * 128 : (h + 1) * 128], g)
        lses.append(top + jnp.log(total))
        deltas.append(jnp.sum(weight * dprob, axis=0, keepdims=True) / total)
    rows_ref[:, 2 * HALF :] = pack_stats(lses + deltas)
    for s in range(SLOTS):
        send_ref[route_ref[0, 0, s]] = rows_ref[s * 16 : (s + 1) * 16, :]


def owner_kernel(rows_ref, k_ref, v_ref, back_ref, dk_ref, dv_ref):
    lower = lax.broadcasted_iota(jnp.int32, (PLEN, ROWS), 1) // CL % 2 == 0
    stats = unpack_stats(rows_ref[:, 2 * HALF :], 2 * PAIRS)

    def stacked(ref, h):
        return jnp.concatenate(
            [ref[:, m * 128 : (m + 1) * 128] for m in (h, h + 2)], axis=0
        )

    def picked(both):
        return jnp.where(lower, both[:PLEN], both[PLEN:])

    def spread(one):
        return jnp.concatenate(
            [jnp.where(lower, one, 0.0), jnp.where(lower, 0.0, one)], axis=0
        ).astype(BF16)

    lses, deltas = [], []
    for h in range(2):
        keys, values = stacked(k_ref, h), stacked(v_ref, h)
        dk = jnp.zeros((2 * PLEN, HEAD_SIZE), F32)
        dv = jnp.zeros((2 * PLEN, HEAD_SIZE), F32)
        for b in range(h * GROUP, (h + 1) * GROUP):
            q = rows_ref[:, b * 128 : (b + 1) * 128]
            g = rows_ref[:, HALF + b * 128 : HALF + (b + 1) * 128]
            own_lse, own_delta = stats[b : b + 1], stats[PAIRS + b : PAIRS + b + 1]
            scores = picked(nt(keys, q)) * INV_SQRT
            dprob = picked(nt(values, g))
            top = jnp.max(scores, axis=0, keepdims=True)
            weight = jnp.exp(scores - top)
            prompt_lse = top + jnp.log(jnp.sum(weight, axis=0, keepdims=True))
            high = jnp.maximum(prompt_lse, own_lse)
            lse = high + jnp.log(jnp.exp(prompt_lse - high) + jnp.exp(own_lse - high))
            probs = weight * jnp.exp(top - lse)
            probs_b = probs.astype(BF16).astype(F32)
            delta = jnp.sum(probs_b * dprob, axis=0, keepdims=True) + own_delta * jnp.exp(own_lse - lse)
            probs_2 = spread(probs_b)
            dscore_2 = spread(probs * (dprob - delta))
            dv = dv + nn(probs_2, g)
            dk = dk + nn(dscore_2, q)
            back_ref[:, b * 128 : (b + 1) * 128] = (tn(dscore_2, keys) * INV_SQRT).astype(BF16)
            lses.append(lse)
            deltas.append(delta)
        for at, m in ((0, h), (PLEN, h + 2)):
            dk_ref[:, m * 128 : (m + 1) * 128] = (dk[at : at + PLEN] * INV_SQRT).astype(BF16)
            dv_ref[:, m * 128 : (m + 1) * 128] = dv[at : at + PLEN].astype(BF16)
    back_ref[:, HALF:] = pack_stats(lses + deltas)


def finish_kernel(
    rank_ref, route_ref, x_ref, sk_ref, sv_ref, wu_ref, low_ref, send_ref, back_ref,
    dq_ref, dsk_ref, dsv_ref, grads_ref, rows_ref, dq_rows_ref,
):
    rank = rank_ref[0]
    scale = adapter_strength / rank.astype(F32)
    for s in range(SLOTS):
        owner = route_ref[0, 0, s]
        rows_ref[s * 16 : (s + 1) * 16, :] = send_ref[owner]
        dq_rows_ref[s * 16 : (s + 1) * 16, :] = back_ref[owner]
    keys = fold(sk_ref[...].astype(F32)).astype(BF16)
    values = fold(sv_ref[...].astype(F32)).astype(BF16)
    stats = unpack_stats(dq_rows_ref[:, HALF:], 2 * PAIRS)
    mask = own_mask()
    for h in range(2):
        k2, v2 = keys[:, h * 128 : (h + 1) * 128], values[:, h * 128 : (h + 1) * 128]
        dsk = jnp.zeros((ROWS, HEAD_SIZE), F32)
        dsv = jnp.zeros((ROWS, HEAD_SIZE), F32)
        for b in range(h * GROUP, (h + 1) * GROUP):
            q = rows_ref[:, b * 128 : (b + 1) * 128]
            g = rows_ref[:, HALF + b * 128 : HALF + (b + 1) * 128]
            lse, delta = stats[b : b + 1], stats[PAIRS + b : PAIRS + b + 1]
            probs = jnp.exp(jnp.where(mask, nt(k2, q) * INV_SQRT - lse, masked_score))
            dscore = (probs * (nt(v2, g) - delta)).astype(BF16)
            dsv = dsv + nn(probs.astype(BF16), g)
            dsk = dsk + nn(dscore, q)
            dq = dq_rows_ref[:, b * 128 : (b + 1) * 128].astype(F32) + tn(dscore, k2) * INV_SQRT
            for at, part in zip((b, b + PAIRS), unfold(dq)):
                dq_ref[0, :, at * 128 : (at + 1) * 128] = part.astype(BF16)
        for at, k_part, v_part in zip((h, h + 2), unfold(dsk * INV_SQRT), unfold(dsv)):
            dsk_ref[0, :, at * 128 : (at + 1) * 128] = k_part.astype(BF16)
            dsv_ref[0, :, at * 128 : (at + 1) * 128] = v_part.astype(BF16)
    dq = dq_ref[0]
    keep = lax.broadcasted_iota(jnp.int32, (TOKENS, PADDED_RANK), 1) < rank
    lifted = jnp.where(keep, scale * nt(dq, wu_ref[...]), 0.0).astype(BF16)
    down = tn(lifted, x_ref[...])
    up = scale * tn(low_ref[...], dq)
    for c in range(GRAD_BLOCKS):
        part = (
            down[:, c * 128 : (c + 1) * 128]
            if c < DOWN_BLOCKS
            else up[:, (c - DOWN_BLOCKS) * 128 : (c - DOWN_BLOCKS + 1) * 128]
        )
        grads_ref[c * PADDED_RANK : (c + 1) * PADDED_RANK, :] = part.astype(BF16)


def spread_kernel(grads_ref, down_ref, up_ref):
    for c in range(GRAD_BLOCKS):
        part = grads_ref[c * PADDED_RANK : (c + 1) * PADDED_RANK, :].astype(F32)
        if c < DOWN_BLOCKS:
            down_ref[c * 128 : (c + 1) * 128, :] = part.T
        else:
            at = (c - DOWN_BLOCKS) * 128
            up_ref[:, at : at + 128] = part


VMEM = pl.BlockSpec(memory_space=pltpu.VMEM)
SMEM = pl.BlockSpec(memory_space=pltpu.SMEM)


def call(kernel, in_specs, outs, scratch=()):
    return pl.pallas_call(
        kernel,
        out_shape=[jax.ShapeDtypeStruct(shape, dtype) for shape, dtype in outs],
        in_specs=in_specs,
        out_specs=[VMEM] * len(outs),
        scratch_shapes=list(scratch),
        compiler_params=pltpu.CompilerParams(vmem_limit_bytes=48 * 1024 * 1024),
    )


def replicate(part, count):
    return jnp.broadcast_to(part[None], (count,) + part.shape)


def sum_all(grads):
    rows = GRAD_BLOCKS * PADDED_RANK
    parts = lax.all_to_all(grads.reshape(16, rows // 16, 128), "comp", 0, 0, tiled=True)
    total = jnp.sum(parts.astype(F32), axis=0)
    flips = (
        lambda i: i ^ 4,
        lambda i: (3 - i // 4) * 4 + i % 4,
        lambda i: i ^ 1,
        lambda i: i // 4 * 4 + 3 - i % 4,
    )
    for flip in flips:
        total = total + lax.ppermute(total, "prompt", [(i, flip(i)) for i in range(16)])
    whole = lax.all_to_all(replicate(total.astype(BF16), 16), "comp", 0, 0, tiled=True)
    return whole.reshape(rows, 128)


def per_device(
    normed_hidden_input,
    frozen_query_base,
    attention_output_grad,
    completion_keys,
    completion_values,
    owner_prompt_keys,
    owner_prompt_values,
    adapter_down_weight,
    adapter_up_weight,
    adapter_rank,
    route,
    lengths,
):
    hidden = normed_hidden_input[0]
    keys, values = completion_keys[0], completion_values[0]
    low, send = call(
        prepare_kernel,
        [SMEM] * 3 + [VMEM] * 7,
        [((TOKENS, PADDED_RANK), BF16), ((SLOTS, 16, SEND_WIDTH), BF16)],
        [pltpu.VMEM((ROWS, SEND_WIDTH), BF16)],
    )(
        adapter_rank, route, lengths, hidden, frozen_query_base[0], attention_output_grad[0],
        keys, values, adapter_down_weight, adapter_up_weight,
    )
    arrived = lax.all_to_all(send, "prompt", 0, 0, tiled=True)
    back, dk, dv = call(
        owner_kernel,
        [VMEM] * 3,
        [((ROWS, BACK_WIDTH), BF16)] + [((PLEN, KEY_VALUE_HEADS * HEAD_SIZE), BF16)] * 2,
    )(arrived.reshape(ROWS, SEND_WIDTH), owner_prompt_keys[0], owner_prompt_values[0])
    back = lax.all_to_all(back.reshape(SLOTS, 16, BACK_WIDTH), "prompt", 0, 0, tiled=True)
    dq, dsk, dsv, grads = call(
        finish_kernel,
        [SMEM] * 2 + [VMEM] * 7,
        [
            ((1, TOKENS, QUERY_WIDTH), BF16),
            ((1, TOKENS, KEY_VALUE_HEADS * HEAD_SIZE), BF16),
            ((1, TOKENS, KEY_VALUE_HEADS * HEAD_SIZE), BF16),
            ((GRAD_BLOCKS * PADDED_RANK, 128), BF16),
        ],
        [pltpu.VMEM((ROWS, SEND_WIDTH), BF16), pltpu.VMEM((ROWS, BACK_WIDTH), BF16)],
    )(adapter_rank, route, hidden, keys, values, adapter_up_weight, low, send, back)
    down, up = call(
        spread_kernel,
        [VMEM],
        [((MODEL_WIDTH, PADDED_RANK), F32), ((PADDED_RANK, QUERY_WIDTH), F32)],
    )(sum_all(grads))
    return dq, dsk, dsv, dk[None], dv[None], down, up


def solution(mesh):
    split = P("comp", "prompt", None)
    return jax.shard_map(
        per_device,
        mesh=mesh,
        in_specs=(split,) * 7 + (P(),) * 3 + (split,) * 2,
        out_specs=(split,) * 5 + (P(),) * 2,
        check_vma=False,
    )
```

time: 654 us -> 162 us (0.25)
  waiting for transfers between devices: 536 us -> 19.5 us
  blocking collectives: 0 us -> 119 us
  local copies, waits for them, and re-layouts: 56.3 us -> 5.8 us
  matrix products: 29.9 us -> 0 us
  other arithmetic: 14.2 us -> 0.2 us
  Pallas kernels: 0 us -> 13.5 us
  between operations: 14.8 us -> 1.59 us
    psum x1 -> x0, waiting for transfers between devices: 263 us -> none  [per_device(): lax.psum((down_gradient, up_gradient), ('prompt', 'comp'))]
    reduce_scatter x2 -> x0, waiting for transfers between devices: 166 us -> none  [the longest x1 95 us: per_device(): lax.psum_scatter(by_owner_v, 'prompt', scatter_dimension=0, tiled=True)]
    all_to_all x0 -> x4, blocking collectives: none -> 119 us  [the longest x1 45.9 us: per_device(): arrived = lax.all_to_all(send, 'prompt', 0, 0, tiled=True)]
    all_gather x2 -> x0, waiting for transfers between devices: 106 us -> none  [the longest x1 53.7 us: per_device(): lax.all_gather(owner_prompt_keys[0], 'prompt', axis=0, tiled=True)]
    dot_general x16 -> x0, matrix products: 29.9 us -> none  [the longest x1 3.91 us: per_device(): jnp.einsum('sqkgd,stkd->sqkgt', g_slots, sv_slots, preferred_element_type...]
    ppermute x0 -> x4, waiting for transfers between devices: none -> 19.5 us  [sum_all(): lax.ppermute(total, 'prompt', [(i, flip(i)) for i in range(16)])]
    gather x4 -> x0, local copies, waits for them, and re-layouts: 17.7 us -> none  [the longest x1 5.1 us: per_device(): jnp.take(part_v, inverse, axis=0)]
    reshape x4 -> x0, local copies, waits for them, and re-layouts: 14.9 us -> none  [the longest x2 7.47 us: per_device(): all_vals.reshape(count, PLEN, KEY_VALUE_HEADS, HEAD_SIZE)]
  transfers between devices with their start and end apart: 5 -> 4, of which waited for: 5 -> 4; matrix products, arithmetic and copies ran while one was open for 6% -> 0% of each run, Pallas kernels for 0% -> 0%
where the time goes in v1:
time: 162 us; the launch traced here: 161 us
  blocking collectives  119 us (73%)
  waiting for transfers between devices  19.5 us (12%)
  Pallas kernels  13.5 us (8%)
  local copies, waits for them, and re-layouts  5.8 us (4%)
    all_to_all x1, blocking collectives, per_device(): arrived = lax.all_to_all(send, 'prompt', 0, 0, tiled=True)  45.9 us
    all_to_all x1, blocking collectives, per_device(): lax.all_to_all(back.reshape(SLOTS, 16, BACK_WIDTH), 'prompt', 0, 0, tiled...  25.1 us
    all_to_all x1, blocking collectives, sum_all(): lax.all_to_all(replicate(total.astype(BF16), 16), 'comp', 0, 0, tiled=True)  24.7 us
    all_to_all x1, blocking collectives, sum_all(): lax.all_to_all(grads.reshape(16, rows // 16, 128), 'comp', 0, 0, tiled=True)  23.6 us
    ppermute x4, waiting for transfers between devices, sum_all(): lax.ppermute(total, 'prompt', [(i, flip(i)) for i in range(16)])  19.5 us
    unnamed x22, local copies, waits for them, and re-layouts  5.67 us
    pallas_call x1, Pallas kernels, per_device(): call(finish_kernel, [SMEM] * 2 + [VMEM] * 7, [((1, TOKENS, QUERY_WIDTH),...  5.27 us
    pallas_call x1, Pallas kernels, per_device(): call(owner_kernel, [VMEM] * 3, [((ROWS, BACK_WIDTH), BF16)] + [((PLEN, KE...  4.43 us
  transfers between devices with their start and end apart: 4, of which 4 were waited for; matrix products, arithmetic and copies ran while one was open for 0% of the time, Pallas kernels for 0%

profile of v1, /device:TPU:1, one launch (start us, length us, event | category | flops | bytes accessed | tf_op | source)
XLA Modules:
  0.0 161.3 jit_solution(1069459904831567139)
XLA Ops:
  1.5 1.7 %copy.19.wd_ref = bf16[5120,64]{1,0:T(8,128)(2,1)S(1)} copy(bf16[5120,64]{0,1:T(8,128)(2,1)} %param.19) | data formatting | bytes 1310720 | tf_op args[7]
  3.2 0.0 copy-start.2
  3.2 1.1 copy-done.2
  4.3 1.1 copy-done.3
  5.4 2.6 %shard_map.171 = (bf16[128,64]{1,0:T(8,128)(2,1)S(1)}, bf16[16,16,2688]{2,1,0:T(8,128)(2,1)S(1)}) custom-call(s32[1]{0:T(128)S(6)} %copy.21.rank_ref, s32[1,1,16]{2,1,0:T(1,128)S(1)} %copy-done.8, s32[1,1,16]{2,1,0:T(1,128)S(1)} %copy-done.9, bf16[128,5120]{1,0:T(8,128)(2,1)S(1)} %bitcast.14, bf16[128,2560]{1,0:T(8,128)(2,1)S(1)} %bitcast.19, ...), custom_call_target="tpu_custom_call" | custom-call | tf_op jit(solution)/shard_map/pallas_call | solution.py:283
  7.9 0.0 copy-start.6
  8.0 45.9 %all_to_all.20 = bf16[16,16,2688]{2,1,0:T(8,128)(2,1)S(1)} all-to-all(bf16[16,16,2688]{2,1,0:T(8,128)(2,1)S(1)} %get-tuple-element.19.send_ref), channel_id=1, replica_groups=mesh['prompt'=16,'comp'=16] {'prompt'}, dimensions={0} | all-to-all | bytes 2752512 | tf_op jit(solution)/shard_map/all_to_all | solution.py:292
  53.8 4.4 %shard_map.172 = (bf16[256,1408]{1,0:T(8,128)(2,1)S(1)}, bf16[128,512]{1,0:T(8,128)(2,1)}, bf16[128,512]{1,0:T(8,128)(2,1)}) custom-call(bf16[256,2688]{1,0:T(8,128)(2,1)S(1)} %bitcast.13, bf16[128,512]{1,0:T(8,128)(2,1)S(1)} %bitcast.25, bf16[128,512]{1,0:T(8,128)(2,1)S(1)} %bitcast.26), custom_call_target="tpu_custom_call" | custom-call | tf_op jit(solution)/shard_map/pallas_call | solution.py:293
  58.3 25.1 %all_to_all.21.back_ref = bf16[16,16,1408]{2,1,0:T(8,128)(2,1)S(1)} all-to-all(bf16[16,16,1408]{2,1,0:T(8,128)(2,1)S(1)} %bitcast.18), channel_id=1, replica_groups=mesh['prompt'=16,'comp'=16] {'prompt'}, dimensions={0} | all-to-all | bytes 1441792 | tf_op jit(solution)/shard_map/all_to_all | solution.py:298
  83.4 5.3 %shard_map.173 = (bf16[1,128,2560]{2,1,0:T(8,128)(2,1)}, bf16[1,128,512]{2,1,0:T(8,128)(2,1)}, bf16[1,128,512]{2,1,0:T(8,128)(2,1)}, bf16[3840,128]{1,0:T(8,128)(2,1)S(1)}) custom-call(s32[1]{0:T(128)S(6)} %copy.21.rank_ref, s32[1,1,16]{2,1,0:T(1,128)S(1)} %copy-done.8, bf16[128,5120]{1,0:T(8,128)(2,1)S(1)} %bitcast.15, bf16[128,512]{1,0:T(8,128)(2,1)S(1)} %bitcast.22, ...), custom_call_target="tpu_custom_call" | custom-call | tf_op jit(solution)/shard_map/pallas_call | solution.py:299
  88.7 23.6 %all_to_all.22 = bf16[16,240,128]{2,1,0:T(8,128)(2,1)S(1)} all-to-all(bf16[16,240,128]{2,1,0:T(8,128)(2,1)S(1)} %bitcast.17), channel_id=1, replica_groups=mesh['prompt'=16,'comp'=16] {'comp'}, dimensions={0} | all-to-all | bytes 1966080 | tf_op jit(solution)/shard_map/all_to_all | solution.py:253
  112.2 0.1 convert_reduce_fusion
  112.4 0.1 collective-permute-start
  112.5 3.7 %collective-permute-done = f32[240,128]{1,0:T(8,128)S(1)} collective-permute-done((f32[240,128]{1,0:T(8,128)S(1)}, f32[240,128]{1,0:T(8,128)S(1)}, u32[]{:S(2)}, u32[]{:S(2)}) %collective-permute-start) | collective-permute-done | bytes 122912 | tf_op jit(solution)/shard_map/ppermute | solution.py:262
  116.2 0.7 collective-permute-start.1
  116.9 4.4 %collective-permute-done.1 = f32[240,128]{1,0:T(8,128)S(1)} collective-permute-done((f32[240,128]{1,0:T(8,128)S(1)}, f32[240,128]{1,0:T(8,128)S(1)}, u32[]{:S(2)}, u32[]{:S(2)}) %collective-permute-start.1) | collective-permute-done | bytes 122912 | tf_op jit(solution)/shard_map/ppermute | solution.py:262
  121.2 0.5 collective-permute-start.2
  121.7 5.5 %collective-permute-done.2 = f32[240,128]{1,0:T(8,128)S(1)} collective-permute-done((f32[240,128]{1,0:T(8,128)S(1)}, f32[240,128]{1,0:T(8,128)S(1)}, u32[]{:S(2)}, u32[]{:S(2)}) %collective-permute-start.2) | collective-permute-done | bytes 122912 | tf_op jit(solution)/shard_map/ppermute | solution.py:262
  127.3 0.1 collective-permute-start.3
  127.4 5.9 %collective-permute-done.3 = f32[240,128]{1,0:T(8,128)S(1)} collective-permute-done((f32[240,128]{1,0:T(8,128)S(1)}, f32[240,128]{1,0:T(8,128)S(1)}, u32[]{:S(2)}, u32[]{:S(2)}) %collective-permute-start.3) | collective-permute-done | bytes 122912 | tf_op jit(solution)/shard_map/ppermute | solution.py:262
  133.3 0.1 broadcast_in_dim.14
  133.5 24.7 %all_to_all.23 = bf16[16,240,128]{2,1,0:T(8,128)(2,1)S(1)} all-to-all(bf16[16,240,128]{2,1,0:T(8,128)(2,1)S(1)} %broadcast_in_dim.14), channel_id=1, replica_groups=mesh['prompt'=16,'comp'=16] {'comp'}, dimensions={0} | all-to-all | bytes 1966080 | tf_op jit(solution)/shard_map/all_to_all | solution.py:263
  158.2 1.3 shard_map.174
  159.5 1.8 %copy.20 = f32[5120,64]{0,1:T(8,128)} copy(f32[5120,64]{1,0:T(8,128)S(1)} %get-tuple-element.34) | data formatting | bytes 2621440
  (20 shorter events, 0.1 us)
Async XLA Ops:
  0.6 2.5 %copy-start.8 = (s32[1,1,16]{2,1,0:T(1,128)S(1)}, s32[1,1,16]{2,1,0:T(1,128)}, u32[]{:S(2)}) copy-start(s32[1,1,16]{2,1,0:T(1,128)} %route_ref.3) | copy-start | bytes 196
  0.6 2.5 %copy-start.1 = (bf16[64,2560]{1,0:T(8,128)(2,1)S(1)}, bf16[64,2560]{1,0:T(8,128)(2,1)}, u32[]{:S(2)}) copy-start(bf16[64,2560]{1,0:T(8,128)(2,1)} %wu_ref.3) | copy-start | bytes 983044
  0.7 2.5 %copy-start.9 = (s32[1,1,16]{2,1,0:T(1,128)S(1)}, s32[1,1,16]{2,1,0:T(1,128)}, u32[]{:S(2)}) copy-start(s32[1,1,16]{2,1,0:T(1,128)} %length_ref.1) | copy-start | bytes 196
  0.7 2.5 %copy-start.5 = (bf16[1,128,512]{2,1,0:T(8,128)(2,1)S(1)}, bf16[1,128,512]{2,1,0:T(8,128)(2,1)}, u32[]{:S(2)}) copy-start(bf16[1,128,512]{2,1,0:T(8,128)(2,1)} %param.16) | copy-start | bytes 393220
  0.7 2.5 %copy-start.4 = (bf16[1,128,512]{2,1,0:T(8,128)(2,1)S(1)}, bf16[1,128,512]{2,1,0:T(8,128)(2,1)}, u32[]{:S(2)}) copy-start(bf16[1,128,512]{2,1,0:T(8,128)(2,1)} %param.15) | copy-start | bytes 393220
  0.7 2.5 %copy-start = (bf16[1,128,5120]{2,1,0:T(8,128)(2,1)S(1)}, bf16[1,128,5120]{2,1,0:T(8,128)(2,1)}, u32[]{:S(2)}) copy-start(bf16[1,128,5120]{2,1,0:T(8,128)(2,1)} %param.12) | copy-start | bytes 3932164
  3.2 1.1 copy-start.2
  4.3 1.1 copy-start.3
  7.9 45.9 %copy-start.6 = (bf16[1,128,512]{2,1,0:T(8,128)(2,1)S(1)}, bf16[1,128,512]{2,1,0:T(8,128)(2,1)}, u32[]{:S(2)}) copy-start(bf16[1,128,512]{2,1,0:T(8,128)(2,1)} %param.17) | copy-start | bytes 393220
  7.9 45.9 %copy-start.7 = (bf16[1,128,512]{2,1,0:T(8,128)(2,1)S(1)}, bf16[1,128,512]{2,1,0:T(8,128)(2,1)}, u32[]{:S(2)}) copy-start(bf16[1,128,512]{2,1,0:T(8,128)(2,1)} %param.18) | copy-start | bytes 393220
  112.4 3.8 %collective-permute-start = (f32[240,128]{1,0:T(8,128)S(1)}, f32[240,128]{1,0:T(8,128)S(1)}, u32[]{:S(2)}, u32[]{:S(2)}) collective-permute-start(f32[240,128]{1,0:T(8,128)S(1)} %convert_reduce_fusion), channel_id=1, source_target_pairs={{0,64},{16,80},{32,96},{48,112},{64,0},{80,16},{96,32},{112,48},{1... | collective-permute-start | bytes 368648 | tf_op jit(solution)/shard_map/ppermute | solution.py:262
  116.2 5.0 %collective-permute-start.1 = (f32[240,128]{1,0:T(8,128)S(1)}, f32[240,128]{1,0:T(8,128)S(1)}, u32[]{:S(2)}, u32[]{:S(2)}) collective-permute-start(f32[240,128]{1,0:T(8,128)S(1)} %add.12), channel_id=1, source_target_pairs={{0,192},{16,208},{32,224},{48,240},{64,128},{80,144},{96,160},{112... | collective-permute-start | bytes 368648 | tf_op jit(solution)/shard_map/ppermute | solution.py:262
  121.2 6.0 %collective-permute-start.2 = (f32[240,128]{1,0:T(8,128)S(1)}, f32[240,128]{1,0:T(8,128)S(1)}, u32[]{:S(2)}, u32[]{:S(2)}) collective-permute-start(f32[240,128]{1,0:T(8,128)S(1)} %add.13), channel_id=1, source_target_pairs={{0,16},{16,0},{32,48},{48,32},{64,80},{80,64},{96,112},{112,96},{1... | collective-permute-start | bytes 368648 | tf_op jit(solution)/shard_map/ppermute | solution.py:262
  127.3 6.0 %collective-permute-start.3 = (f32[240,128]{1,0:T(8,128)S(1)}, f32[240,128]{1,0:T(8,128)S(1)}, u32[]{:S(2)}, u32[]{:S(2)}) collective-permute-start(f32[240,128]{1,0:T(8,128)S(1)} %add.14), channel_id=1, source_target_pairs={{0,48},{16,32},{32,16},{48,0},{64,112},{80,96},{96,80},{112,64},{1... | collective-permute-start | bytes 368648 | tf_op jit(solution)/shard_map/ppermute | solution.py:262

commit v2 on v1

--- a/solution.py
+++ b/solution.py
@@ -64,9 +64,21 @@
 
 
 def own_mask():
-    key = lax.broadcasted_iota(jnp.int32, (ROWS, ROWS), 0)
-    row = lax.broadcasted_iota(jnp.int32, (ROWS, ROWS), 1)
+    key = lax.broadcasted_iota(jnp.int32, (TOKENS, ROWS), 0)
+    row = lax.broadcasted_iota(jnp.int32, (TOKENS, ROWS), 1) % TOKENS
     return (key // CL == row // CL) & (key <= row)
+
+
+def own_scores(keys, rows):
+    return jnp.concatenate(
+        [nt(keys[at : at + TOKENS], rows[at : at + TOKENS]) for at in (0, TOKENS)], axis=1
+    )
+
+
+def own_product(scores, rows, product):
+    return jnp.concatenate(
+        [product(scores[:, at : at + TOKENS], rows[at : at + TOKENS]) for at in (0, TOKENS)], axis=0
+    )
 
 
 def pack_stats(rows):
@@ -85,38 +97,60 @@
 
 
 def prepare_kernel(
-    rank_ref, route_ref, length_ref, x_ref, base_ref, g_ref, sk_ref, sv_ref, wd_ref, wu_ref,
+    rank_ref, route_ref, length_ref, x_hbm, base_hbm, g_hbm, sk_hbm, sv_hbm, wd_hbm, wu_hbm,
     low_ref, send_ref, rows_ref,
+    x_ref, base_ref, g_ref, sk_ref, sv_ref, wd_ref, wu_ref, sems,
 ):
+    sources = (g_hbm, sv_hbm, sk_hbm, wd_hbm, x_hbm, wu_hbm, base_hbm)
+    targets = (g_ref, sv_ref, sk_ref, wd_ref, x_ref, wu_ref, base_ref)
+    copies = [
+        pltpu.make_async_copy(source, target, sems.at[i])
+        for i, (source, target) in enumerate(zip(sources, targets))
+    ]
+    for copy in copies:
+        copy.start()
     rank = rank_ref[0]
     scale = adapter_strength / rank.astype(F32)
-    keep = lax.broadcasted_iota(jnp.int32, (TOKENS, PADDED_RANK), 1) < rank
-    low = jnp.where(keep, nn(x_ref[...], wd_ref[...]), 0.0).astype(BF16)
-    low_ref[...] = low
-    query = base_ref[...].astype(F32) + scale * nn(low, wu_ref[...])
-    rows_ref[:, :HALF] = fold(query).astype(BF16)
     position = lax.broadcasted_iota(jnp.int32, (CL, 128), 0)
     live = jnp.concatenate(
         [jnp.where(position < length_ref[0, 0, s], 1.0, 0.0) for s in range(SLOTS)], axis=0
     )
+    mask = own_mask()
+    copies[0].wait()
     for n in range(PAIRS):
         left, right = (g_ref[:, m * 128 : (m + 1) * 128].astype(F32) * live for m in (n, n + PAIRS))
         rows_ref[:, HALF + n * 128 : HALF + (n + 1) * 128] = fold(
             jnp.concatenate([left, right], axis=1)
         ).astype(BF16)
+    copies[1].wait()
+    values = fold(sv_ref[...].astype(F32)).astype(BF16)
+    copies[2].wait()
     keys = fold(sk_ref[...].astype(F32)).astype(BF16)
-    values = fold(sv_ref[...].astype(F32)).astype(BF16)
-    mask = own_mask()
+    copies[3].wait()
+    copies[4].wait()
+    keep = lax.broadcasted_iota(jnp.int32, (TOKENS, PADDED_RANK), 1) < rank
+    low = jnp.where(keep, nt(x_ref[...], wd_ref[...]), 0.0).astype(BF16)
+    low_ref[...] = low
+    copies[5].wait()
+    copies[6].wait()
     lses, deltas = [], []
     for b in range(PAIRS):
         h = b // GROUP
-        q = rows_ref[:, b * 128 : (b + 1) * 128]
+        left, right = (
+            base_ref[:, m * 128 : (m + 1) * 128].astype(F32)
+            + scale * nn(low, wu_ref[:, m * 128 : (m + 1) * 128])
+            for m in (b, b + PAIRS)
+        )
+        q = fold(jnp.concatenate([left, right], axis=1)).astype(BF16)
+        rows_ref[:, b * 128 : (b + 1) * 128] = q
         g = rows_ref[:, HALF + b * 128 : HALF + (b + 1) * 128]
-        scores = jnp.where(mask, nt(keys[:, h * 128 : (h + 1) * 128], q) * INV_SQRT, masked_score)
+        scores = jnp.where(
+            mask, own_scores(keys[:, h * 128 : (h + 1) * 128], q) * INV_SQRT, masked_score
+        )
         top = jnp.max(scores, axis=0, keepdims=True)
         weight = jnp.exp(scores - top)
         total = jnp.sum(weight, axis=0, keepdims=True)
-        dprob = nt(values[:, h * 128 : (h + 1) * 128], g)
+        dprob = own_scores(values[:, h * 128 : (h + 1) * 128], g)
         lses.append(top + jnp.log(total))
         deltas.append(jnp.sum(weight * dprob, axis=0, keepdims=True) / total)
     rows_ref[:, 2 * HALF :] = pack_stats(lses + deltas)
@@ -125,64 +159,59 @@
 
 
 def owner_kernel(rows_ref, k_ref, v_ref, back_ref, dk_ref, dv_ref):
-    lower = lax.broadcasted_iota(jnp.int32, (PLEN, ROWS), 1) // CL % 2 == 0
+    lower = (lax.broadcasted_iota(jnp.int32, (ROWS, HEAD_SIZE), 0) // CL % 2 == 0).astype(F32)
+    lower, upper = lower.astype(BF16), (1.0 - lower).astype(BF16)
     stats = unpack_stats(rows_ref[:, 2 * HALF :], 2 * PAIRS)
 
-    def stacked(ref, h):
-        return jnp.concatenate(
-            [ref[:, m * 128 : (m + 1) * 128] for m in (h, h + 2)], axis=0
-        )
-
-    def picked(both):
-        return jnp.where(lower, both[:PLEN], both[PLEN:])
-
-    def spread(one):
-        return jnp.concatenate(
-            [jnp.where(lower, one, 0.0), jnp.where(lower, 0.0, one)], axis=0
-        ).astype(BF16)
+    def beside(ref, h):
+        return jnp.concatenate([ref[:, m * 128 : (m + 1) * 128] for m in (h, h + 2)], axis=1)
+
+    def apart(rows):
+        return jnp.concatenate([rows * lower, rows * upper], axis=1)
 
     lses, deltas = [], []
     for h in range(2):
-        keys, values = stacked(k_ref, h), stacked(v_ref, h)
-        dk = jnp.zeros((2 * PLEN, HEAD_SIZE), F32)
-        dv = jnp.zeros((2 * PLEN, HEAD_SIZE), F32)
+        keys, values = beside(k_ref, h), beside(v_ref, h)
+        dk = jnp.zeros((PLEN, 2 * HEAD_SIZE), F32)
+        dv = jnp.zeros((PLEN, 2 * HEAD_SIZE), F32)
         for b in range(h * GROUP, (h + 1) * GROUP):
-            q = rows_ref[:, b * 128 : (b + 1) * 128]
-            g = rows_ref[:, HALF + b * 128 : HALF + (b + 1) * 128]
+            q = apart(rows_ref[:, b * 128 : (b + 1) * 128])
+            g = apart(rows_ref[:, HALF + b * 128 : HALF + (b + 1) * 128])
             own_lse, own_delta = stats[b : b + 1], stats[PAIRS + b : PAIRS + b + 1]
-            scores = picked(nt(keys, q)) * INV_SQRT
-            dprob = picked(nt(values, g))
+            scores = nt(keys, q) * INV_SQRT
+            dprob = nt(values, g)
             top = jnp.max(scores, axis=0, keepdims=True)
             weight = jnp.exp(scores - top)
             prompt_lse = top + jnp.log(jnp.sum(weight, axis=0, keepdims=True))
             high = jnp.maximum(prompt_lse, own_lse)
             lse = high + jnp.log(jnp.exp(prompt_lse - high) + jnp.exp(own_lse - high))
             probs = weight * jnp.exp(top - lse)
-            probs_b = probs.astype(BF16).astype(F32)
-            delta = jnp.sum(probs_b * dprob, axis=0, keepdims=True) + own_delta * jnp.exp(own_lse - lse)
-            probs_2 = spread(probs_b)
-            dscore_2 = spread(probs * (dprob - delta))
-            dv = dv + nn(probs_2, g)
-            dk = dk + nn(dscore_2, q)
-            back_ref[:, b * 128 : (b + 1) * 128] = (tn(dscore_2, keys) * INV_SQRT).astype(BF16)
+            probs_b = probs.astype(BF16)
+            delta = jnp.sum(probs_b.astype(F32) * dprob, axis=0, keepdims=True) + own_delta * jnp.exp(
+                own_lse - lse
+            )
+            dscore = (probs * (dprob - delta)).astype(BF16)
+            dv = dv + nn(probs_b, g)
+            dk = dk + nn(dscore, q)
+            dq = (tn(dscore, keys) * INV_SQRT).reshape(SLOTS, 2, CL, 2 * HEAD_SIZE)
+            dq = jnp.concatenate([dq[:, :1, :, :HEAD_SIZE], dq[:, 1:, :, HEAD_SIZE:]], axis=1)
+            back_ref[:, b * 128 : (b + 1) * 128] = dq.reshape(ROWS, HEAD_SIZE).astype(BF16)
             lses.append(lse)
             deltas.append(delta)
-        for at, m in ((0, h), (PLEN, h + 2)):
-            dk_ref[:, m * 128 : (m + 1) * 128] = (dk[at : at + PLEN] * INV_SQRT).astype(BF16)
-            dv_ref[:, m * 128 : (m + 1) * 128] = dv[at : at + PLEN].astype(BF16)
+        for at, m in ((0, h), (HEAD_SIZE, h + 2)):
+            dk_ref[:, m * 128 : (m + 1) * 128] = (dk[:, at : at + HEAD_SIZE] * INV_SQRT).astype(BF16)
+            dv_ref[:, m * 128 : (m + 1) * 128] = dv[:, at : at + HEAD_SIZE].astype(BF16)
     back_ref[:, HALF:] = pack_stats(lses + deltas)
 
 
 def finish_kernel(
-    rank_ref, route_ref, x_ref, sk_ref, sv_ref, wu_ref, low_ref, send_ref, back_ref,
-    dq_ref, dsk_ref, dsv_ref, grads_ref, rows_ref, dq_rows_ref,
+    rank_ref, route_ref, x_ref, sk_ref, sv_ref, wu_ref, low_ref, rows_ref, back_ref,
+    dq_ref, dsk_ref, dsv_ref, grads_ref, dq_rows_ref,
 ):
     rank = rank_ref[0]
     scale = adapter_strength / rank.astype(F32)
     for s in range(SLOTS):
-        owner = route_ref[0, 0, s]
-        rows_ref[s * 16 : (s + 1) * 16, :] = send_ref[owner]
-        dq_rows_ref[s * 16 : (s + 1) * 16, :] = back_ref[owner]
+        dq_rows_ref[s * 16 : (s + 1) * 16, :] = back_ref[route_ref[0, 0, s]]
     keys = fold(sk_ref[...].astype(F32)).astype(BF16)
     values = fold(sv_ref[...].astype(F32)).astype(BF16)
     stats = unpack_stats(dq_rows_ref[:, HALF:], 2 * PAIRS)
@@ -195,11 +224,12 @@
             q = rows_ref[:, b * 128 : (b + 1) * 128]
             g = rows_ref[:, HALF + b * 128 : HALF + (b + 1) * 128]
             lse, delta = stats[b : b + 1], stats[PAIRS + b : PAIRS + b + 1]
-            probs = jnp.exp(jnp.where(mask, nt(k2, q) * INV_SQRT - lse, masked_score))
-            dscore = (probs * (nt(v2, g) - delta)).astype(BF16)
-            dsv = dsv + nn(probs.astype(BF16), g)
-            dsk = dsk + nn(dscore, q)
-            dq = dq_rows_ref[:, b * 128 : (b + 1) * 128].astype(F32) + tn(dscore, k2) * INV_SQRT
+            probs = jnp.exp(jnp.where(mask, own_scores(k2, q) * INV_SQRT - lse, masked_score))
+            dscore = (probs * (own_scores(v2, g) - delta)).astype(BF16)
+            dsv = dsv + own_product(probs.astype(BF16), g, nn)
+            dsk = dsk + own_product(dscore, q, nn)
+            dq = dq_rows_ref[:, b * 128 : (b + 1) * 128].astype(F32)
+            dq = dq + own_product(dscore, k2, tn) * INV_SQRT
             for at, part in zip((b, b + PAIRS), unfold(dq)):
                 dq_ref[0, :, at * 128 : (at + 1) * 128] = part.astype(BF16)
         for at, k_part, v_part in zip((h, h + 2), unfold(dsk * INV_SQRT), unfold(dsv)):
@@ -208,14 +238,13 @@
     dq = dq_ref[0]
     keep = lax.broadcasted_iota(jnp.int32, (TOKENS, PADDED_RANK), 1) < rank
     lifted = jnp.where(keep, scale * nt(dq, wu_ref[...]), 0.0).astype(BF16)
-    down = tn(lifted, x_ref[...])
-    up = scale * tn(low_ref[...], dq)
+    low = low_ref[...]
     for c in range(GRAD_BLOCKS):
-        part = (
-            down[:, c * 128 : (c + 1) * 128]
-            if c < DOWN_BLOCKS
-            else up[:, (c - DOWN_BLOCKS) * 128 : (c - DOWN_BLOCKS + 1) * 128]
-        )
+        if c < DOWN_BLOCKS:
+            part = tn(lifted, x_ref[:, c * 128 : (c + 1) * 128])
+        else:
+            at = (c - DOWN_BLOCKS) * 128
+            part = scale * tn(low, dq[:, at : at + 128])
         grads_ref[c * PADDED_RANK : (c + 1) * PADDED_RANK, :] = part.astype(BF16)
 
 
@@ -223,7 +252,7 @@
     for c in range(GRAD_BLOCKS):
         part = grads_ref[c * PADDED_RANK : (c + 1) * PADDED_RANK, :].astype(F32)
         if c < DOWN_BLOCKS:
-            down_ref[c * 128 : (c + 1) * 128, :] = part.T
+            down_ref[:, c * 128 : (c + 1) * 128] = part
         else:
             at = (c - DOWN_BLOCKS) * 128
             up_ref[:, at : at + 128] = part
@@ -231,6 +260,7 @@
 
 VMEM = pl.BlockSpec(memory_space=pltpu.VMEM)
 SMEM = pl.BlockSpec(memory_space=pltpu.SMEM)
+HBM = pl.BlockSpec(memory_space=pltpu.HBM)
 
 
 def call(kernel, in_specs, outs, scratch=()):
@@ -280,15 +310,20 @@
 ):
     hidden = normed_hidden_input[0]
     keys, values = completion_keys[0], completion_values[0]
-    low, send = call(
+    arrays = (
+        hidden, frozen_query_base[0], attention_output_grad[0], keys, values,
+        adapter_down_weight.T, adapter_up_weight,
+    )
+    low, send, rows = call(
         prepare_kernel,
-        [SMEM] * 3 + [VMEM] * 7,
-        [((TOKENS, PADDED_RANK), BF16), ((SLOTS, 16, SEND_WIDTH), BF16)],
-        [pltpu.VMEM((ROWS, SEND_WIDTH), BF16)],
-    )(
-        adapter_rank, route, lengths, hidden, frozen_query_base[0], attention_output_grad[0],
-        keys, values, adapter_down_weight, adapter_up_weight,
-    )
+        [SMEM] * 3 + [HBM] * 7,
+        [
+            ((TOKENS, PADDED_RANK), BF16),
+            ((SLOTS, 16, SEND_WIDTH), BF16),
+            ((ROWS, SEND_WIDTH), BF16),
+        ],
+        [pltpu.VMEM(a.shape, BF16) for a in arrays] + [pltpu.SemaphoreType.DMA((7,))],
+    )(adapter_rank, route, lengths, *arrays)
     arrived = lax.all_to_all(send, "prompt", 0, 0, tiled=True)
     back, dk, dv = call(
         owner_kernel,
@@ -305,14 +340,14 @@
             ((1, TOKENS, KEY_VALUE_HEADS * HEAD_SIZE), BF16),
             ((GRAD_BLOCKS * PADDED_RANK, 128), BF16),
         ],
-        [pltpu.VMEM((ROWS, SEND_WIDTH), BF16), pltpu.VMEM((ROWS, BACK_WIDTH), BF16)],
-    )(adapter_rank, route, hidden, keys, values, adapter_up_weight, low, send, back)
+        [pltpu.VMEM((ROWS, BACK_WIDTH), BF16)],
+    )(adapter_rank, route, hidden, keys, values, adapter_up_weight, low, rows, back)
     down, up = call(
         spread_kernel,
         [VMEM],
-        [((MODEL_WIDTH, PADDED_RANK), F32), ((PADDED_RANK, QUERY_WIDTH), F32)],
+        [((PADDED_RANK, MODEL_WIDTH), F32), ((PADDED_RANK, QUERY_WIDTH), F32)],
     )(sum_all(grads))
-    return dq, dsk, dsv, dk[None], dv[None], down, up
+    return dq, dsk, dsv, dk[None], dv[None], down.T, up
 
 
 def solution(mesh):

time: 162 us -> 168 us (1.037)
  Pallas kernels: 13.5 us -> 16.8 us
  local copies, waits for them, and re-layouts: 5.8 us -> 8.83 us
    pallas_call x2, Pallas kernels: 3.81 us -> 8.04 us  [the longest x1 6.68 us: per_device(): call(prepare_kernel, [SMEM] * 3 + [HBM] * 7, [((TOKENS, PADDED_RANK), BF1...]
    unnamed x22 -> x34, local copies, waits for them, and re-layouts: 5.67 us -> 8.71 us
where the time goes in v2:
time: 168 us
  blocking collectives  119 us (71%)
  waiting for transfers between devices  19.5 us (12%)
  Pallas kernels  16.8 us (10%)
  local copies, waits for them, and re-layouts  8.83 us (5%)
    all_to_all x1, blocking collectives, per_device(): arrived = lax.all_to_all(send, 'prompt', 0, 0, tiled=True)  46.2 us
    all_to_all x1, blocking collectives, per_device(): lax.all_to_all(back.reshape(SLOTS, 16, BACK_WIDTH), 'prompt', 0, 0, tiled...  24.8 us
    all_to_all x1, blocking collectives, sum_all(): lax.all_to_all(replicate(total.astype(BF16), 16), 'comp', 0, 0, tiled=True)  24.7 us
    all_to_all x1, blocking collectives, sum_all(): lax.all_to_all(grads.reshape(16, rows // 16, 128), 'comp', 0, 0, tiled=True)  23.5 us
    ppermute x4, waiting for transfers between devices, sum_all(): lax.ppermute(total, 'prompt', [(i, flip(i)) for i in range(16)])  19.5 us
    unnamed x34, local copies, waits for them, and re-layouts  8.71 us
    pallas_call x1, Pallas kernels, per_device(): call(prepare_kernel, [SMEM] * 3 + [HBM] * 7, [((TOKENS, PADDED_RANK), BF1...  6.68 us
    pallas_call x1, Pallas kernels, per_device(): call(finish_kernel, [SMEM] * 2 + [VMEM] * 7, [((1, TOKENS, QUERY_WIDTH),...  4.66 us
  transfers between devices with their start and end apart: 4, of which 4 were waited for; matrix products, arithmetic and copies ran while one was open for 0% of the time, Pallas kernels for 0%

profile of v2, /device:TPU:1, one launch (start us, length us, event | category | flops | bytes accessed | tf_op | source)
XLA Modules:
  0.0 167.5 jit_solution(359781929671758363)
XLA Ops:
  1.3 1.3 copy-done
  2.6 1.0 copy-done.3
  3.6 1.1 copy-done.5
  4.7 1.1 copy-done.6
  5.8 1.1 copy-done.7
  6.8 0.9 copy-done.8
  7.7 0.9 copy-done.10
  8.6 0.7 copy-done.14
  9.3 0.7 copy-done.16
  10.0 6.7 %shard_map.171 = (bf16[128,64]{1,0:T(8,128)(2,1)S(1)}, bf16[16,16,2688]{2,1,0:T(8,128)(2,1)S(1)}, bf16[256,2688]{1,0:T(8,128)(2,1)}) custom-call(s32[1]{0:T(128)S(6)} %copy.19.rank_ref, s32[1,1,16]{2,1,0:T(1,128)S(1)} %copy-done.14, s32[1,1,16]{2,1,0:T(1,128)S(1)} %copy-done.16, bf16[128,5120]{1,0:T(8,128)(2,1)S(1)} %bitcast.16, ...), custom_call_target="tpu_custom_call" | custom-call | tf_op jit(solution)/shard_map/pallas_call | solution.py:317
  16.7 46.2 %all_to_all.20 = bf16[16,16,2688]{2,1,0:T(8,128)(2,1)S(1)} all-to-all(bf16[16,16,2688]{2,1,0:T(8,128)(2,1)S(1)} %get-tuple-element.21), channel_id=1, replica_groups=mesh['prompt'=16,'comp'=16] {'prompt'}, dimensions={0} | all-to-all | bytes 2752512 | tf_op jit(solution)/shard_map/all_to_all | solution.py:327
  63.0 4.1 %shard_map.172 = (bf16[256,1408]{1,0:T(8,128)(2,1)S(1)}, bf16[128,512]{1,0:T(8,128)(2,1)}, bf16[128,512]{1,0:T(8,128)(2,1)}) custom-call(bf16[256,2688]{1,0:T(8,128)(2,1)S(1)} %bitcast.15, bf16[128,512]{1,0:T(8,128)(2,1)S(1)} %bitcast.28, bf16[128,512]{1,0:T(8,128)(2,1)S(1)} %bitcast.29), custom_call_target="tpu_custom_call" | custom-call | tf_op jit(solution)/shard_map/pallas_call | solution.py:328
  67.1 24.8 %all_to_all.21.back_ref = bf16[16,16,1408]{2,1,0:T(8,128)(2,1)S(1)} all-to-all(bf16[16,16,1408]{2,1,0:T(8,128)(2,1)S(1)} %bitcast.20), channel_id=1, replica_groups=mesh['prompt'=16,'comp'=16] {'prompt'}, dimensions={0} | all-to-all | bytes 1441792 | tf_op jit(solution)/shard_map/all_to_all | solution.py:333
  92.0 4.7 %shard_map.173 = (bf16[1,128,2560]{2,1,0:T(8,128)(2,1)}, bf16[1,128,512]{2,1,0:T(8,128)(2,1)}, bf16[1,128,512]{2,1,0:T(8,128)(2,1)}, bf16[3840,128]{1,0:T(8,128)(2,1)S(1)}) custom-call(s32[1]{0:T(128)S(6)} %copy.19.rank_ref, s32[1,1,16]{2,1,0:T(1,128)S(1)} %copy-done.15, bf16[128,5120]{1,0:T(8,128)(2,1)S(1)} %bitcast.17, bf16[128,512]{1,0:T(8,128)(2,1)S(1)} %bitcast.25, ...), custom_call_target="tpu_custom_call" | custom-call | tf_op jit(solution)/shard_map/pallas_call | solution.py:334
  96.6 23.5 %all_to_all.22 = bf16[16,240,128]{2,1,0:T(8,128)(2,1)S(1)} all-to-all(bf16[16,240,128]{2,1,0:T(8,128)(2,1)S(1)} %bitcast.19), channel_id=1, replica_groups=mesh['prompt'=16,'comp'=16] {'comp'}, dimensions={0} | all-to-all | bytes 1966080 | tf_op jit(solution)/shard_map/all_to_all | solution.py:283
  120.2 0.1 convert_reduce_fusion
  120.4 3.7 %collective-permute-done = f32[240,128]{1,0:T(8,128)S(1)} collective-permute-done((f32[240,128]{1,0:T(8,128)S(1)}, f32[240,128]{1,0:T(8,128)S(1)}, u32[]{:S(2)}, u32[]{:S(2)}) %collective-permute-start) | collective-permute-done | bytes 122912 | tf_op jit(solution)/shard_map/ppermute | solution.py:292
  124.1 0.7 collective-permute-start.1
  124.8 4.4 %collective-permute-done.1 = f32[240,128]{1,0:T(8,128)S(1)} collective-permute-done((f32[240,128]{1,0:T(8,128)S(1)}, f32[240,128]{1,0:T(8,128)S(1)}, u32[]{:S(2)}, u32[]{:S(2)}) %collective-permute-start.1) | collective-permute-done | bytes 122912 | tf_op jit(solution)/shard_map/ppermute | solution.py:292
  129.2 0.5 collective-permute-start.2
  129.7 5.5 %collective-permute-done.2 = f32[240,128]{1,0:T(8,128)S(1)} collective-permute-done((f32[240,128]{1,0:T(8,128)S(1)}, f32[240,128]{1,0:T(8,128)S(1)}, u32[]{:S(2)}, u32[]{:S(2)}) %collective-permute-start.2) | collective-permute-done | bytes 122912 | tf_op jit(solution)/shard_map/ppermute | solution.py:292
  135.3 5.9 %collective-permute-done.3 = f32[240,128]{1,0:T(8,128)S(1)} collective-permute-done((f32[240,128]{1,0:T(8,128)S(1)}, f32[240,128]{1,0:T(8,128)S(1)}, u32[]{:S(2)}, u32[]{:S(2)}) %collective-permute-start.3) | collective-permute-done | bytes 122912 | tf_op jit(solution)/shard_map/ppermute | solution.py:292
  141.4 24.7 %all_to_all.23 = bf16[16,240,128]{2,1,0:T(8,128)(2,1)S(1)} all-to-all(bf16[16,240,128]{2,1,0:T(8,128)(2,1)S(1)} %broadcast_in_dim.14), channel_id=1, replica_groups=mesh['prompt'=16,'comp'=16] {'comp'}, dimensions={0} | all-to-all | bytes 1966080 | tf_op jit(solution)/shard_map/all_to_all | solution.py:293
  166.1 1.4 shard_map.174
  (32 shorter events, 0.4 us)
Async XLA Ops:
  1.3 1.3 copy-start
  2.6 1.0 copy-start.3
  3.6 1.1 copy-start.5
  4.7 1.1 copy-start.6
  5.7 1.1 copy-start.7
  6.8 0.9 copy-start.8
  7.7 0.9 copy-start.10
  8.6 0.7 copy-start.14
  9.3 0.7 copy-start.16
  16.7 46.3 %copy-start.12 = (bf16[1,128,512]{2,1,0:T(8,128)(2,1)S(1)}, bf16[1,128,512]{2,1,0:T(8,128)(2,1)}, u32[]{:S(2)}) copy-start(bf16[1,128,512]{2,1,0:T(8,128)(2,1)} %param.17) | copy-start | bytes 393220
  16.7 46.3 %copy-start.13 = (bf16[1,128,512]{2,1,0:T(8,128)(2,1)S(1)}, bf16[1,128,512]{2,1,0:T(8,128)(2,1)}, u32[]{:S(2)}) copy-start(bf16[1,128,512]{2,1,0:T(8,128)(2,1)} %param.18) | copy-start | bytes 393220
  16.7 75.3 %copy-start.9 = (bf16[1,128,512]{2,1,0:T(8,128)(2,1)S(1)}, bf16[1,128,512]{2,1,0:T(8,128)(2,1)}, u32[]{:S(2)}) copy-start(bf16[1,128,512]{2,1,0:T(8,128)(2,1)} %param.15) | copy-start | bytes 393220
  16.7 75.2 %copy-start.11 = (bf16[1,128,512]{2,1,0:T(8,128)(2,1)S(1)}, bf16[1,128,512]{2,1,0:T(8,128)(2,1)}, u32[]{:S(2)}) copy-start(bf16[1,128,512]{2,1,0:T(8,128)(2,1)} %param.16) | copy-start | bytes 393220
  62.9 29.0 %copy-start.1 = (bf16[1,128,5120]{2,1,0:T(8,128)(2,1)S(1)}, bf16[1,128,5120]{2,1,0:T(8,128)(2,1)}, u32[]{:S(2)}) copy-start(bf16[1,128,5120]{2,1,0:T(8,128)(2,1)} %param.12) | copy-start | bytes 3932164
  62.9 29.0 %copy-start.2 = (bf16[256,2688]{1,0:T(8,128)(2,1)S(1)}, bf16[256,2688]{1,0:T(8,128)(2,1)}, u32[]{:S(2)}) copy-start(bf16[256,2688]{1,0:T(8,128)(2,1)} %get-tuple-element.20.rows_ref) | copy-start | bytes 4128772
  62.9 29.0 %copy-start.4 = (bf16[64,2560]{1,0:T(8,128)(2,1)S(1)}, bf16[64,2560]{1,0:T(8,128)(2,1)}, u32[]{:S(2)}) copy-start(bf16[64,2560]{1,0:T(8,128)(2,1)} %wu_ref.1) | copy-start | bytes 983044
  62.9 29.0 %copy-start.15 = (s32[1,1,16]{2,1,0:T(1,128)S(1)}, s32[1,1,16]{2,1,0:T(1,128)}, u32[]{:S(2)}) copy-start(s32[1,1,16]{2,1,0:T(1,128)} %route_ref.3) | copy-start | bytes 196
  120.3 3.8 %collective-permute-start = (f32[240,128]{1,0:T(8,128)S(1)}, f32[240,128]{1,0:T(8,128)S(1)}, u32[]{:S(2)}, u32[]{:S(2)}) collective-permute-start(f32[240,128]{1,0:T(8,128)S(1)} %convert_reduce_fusion), channel_id=1, source_target_pairs={{0,64},{16,80},{32,96},{48,112},{64,0},{80,16},{96,32},{112,48},{1... | collective-permute-start | bytes 368648 | tf_op jit(solution)/shard_map/ppermute | solution.py:292
  124.1 5.0 %collective-permute-start.1 = (f32[240,128]{1,0:T(8,128)S(1)}, f32[240,128]{1,0:T(8,128)S(1)}, u32[]{:S(2)}, u32[]{:S(2)}) collective-permute-start(f32[240,128]{1,0:T(8,128)S(1)} %add.12), channel_id=1, source_target_pairs={{0,192},{16,208},{32,224},{48,240},{64,128},{80,144},{96,160},{112... | collective-permute-start | bytes 368648 | tf_op jit(solution)/shard_map/ppermute | solution.py:292
  129.2 6.0 %collective-permute-start.2 = (f32[240,128]{1,0:T(8,128)S(1)}, f32[240,128]{1,0:T(8,128)S(1)}, u32[]{:S(2)}, u32[]{:S(2)}) collective-permute-start(f32[240,128]{1,0:T(8,128)S(1)} %add.13), channel_id=1, source_target_pairs={{0,16},{16,0},{32,48},{48,32},{64,80},{80,64},{96,112},{112,96},{1... | collective-permute-start | bytes 368648 | tf_op jit(solution)/shard_map/ppermute | solution.py:292
  135.2 6.0 %collective-permute-start.3 = (f32[240,128]{1,0:T(8,128)S(1)}, f32[240,128]{1,0:T(8,128)S(1)}, u32[]{:S(2)}, u32[]{:S(2)}) collective-permute-start(f32[240,128]{1,0:T(8,128)S(1)} %add.14), channel_id=1, source_target_pairs={{0,48},{16,32},{32,16},{48,0},{64,112},{80,96},{96,80},{112,64},{1... | collective-permute-start | bytes 368648 | tf_op jit(solution)/shard_map/ppermute | solution.py:292

commit v3 on v2

--- a/solution.py
+++ b/solution.py
@@ -98,8 +98,8 @@
 
 def prepare_kernel(
     rank_ref, route_ref, length_ref, x_hbm, base_hbm, g_hbm, sk_hbm, sv_hbm, wd_hbm, wu_hbm,
-    low_ref, send_ref, rows_ref,
-    x_ref, base_ref, g_ref, sk_ref, sv_ref, wd_ref, wu_ref, sems,
+    low_ref, send_hbm,
+    x_ref, base_ref, g_ref, sk_ref, sv_ref, wd_ref, wu_ref, rows_ref, sems,
 ):
     sources = (g_hbm, sv_hbm, sk_hbm, wd_hbm, x_hbm, wu_hbm, base_hbm)
     targets = (g_ref, sv_ref, sk_ref, wd_ref, x_ref, wu_ref, base_ref)
@@ -154,8 +154,16 @@
         lses.append(top + jnp.log(total))
         deltas.append(jnp.sum(weight * dprob, axis=0, keepdims=True) / total)
     rows_ref[:, 2 * HALF :] = pack_stats(lses + deltas)
-    for s in range(SLOTS):
-        send_ref[route_ref[0, 0, s]] = rows_ref[s * 16 : (s + 1) * 16, :]
+    sends = [
+        pltpu.make_async_copy(
+            rows_ref.at[pl.ds(s * 16, 16)], send_hbm.at[route_ref[0, 0, s]], sems.at[7 + s]
+        )
+        for s in range(SLOTS)
+    ]
+    for copy in sends:
+        copy.start()
+    for copy in sends:
+        copy.wait()
 
 
 def owner_kernel(rows_ref, k_ref, v_ref, back_ref, dk_ref, dv_ref):
@@ -205,13 +213,15 @@
 
 
 def finish_kernel(
-    rank_ref, route_ref, x_ref, sk_ref, sv_ref, wu_ref, low_ref, rows_ref, back_ref,
-    dq_ref, dsk_ref, dsv_ref, grads_ref, dq_rows_ref,
+    rank_ref, route_ref, x_ref, sk_ref, sv_ref, wu_ref, low_ref, send_ref, back_ref,
+    dq_ref, dsk_ref, dsv_ref, grads_ref, rows_ref, dq_rows_ref,
 ):
     rank = rank_ref[0]
     scale = adapter_strength / rank.astype(F32)
     for s in range(SLOTS):
-        dq_rows_ref[s * 16 : (s + 1) * 16, :] = back_ref[route_ref[0, 0, s]]
+        owner = route_ref[0, 0, s]
+        rows_ref[s * 16 : (s + 1) * 16, :] = send_ref[owner]
+        dq_rows_ref[s * 16 : (s + 1) * 16, :] = back_ref[owner]
     keys = fold(sk_ref[...].astype(F32)).astype(BF16)
     values = fold(sv_ref[...].astype(F32)).astype(BF16)
     stats = unpack_stats(dq_rows_ref[:, HALF:], 2 * PAIRS)
@@ -263,14 +273,14 @@
 HBM = pl.BlockSpec(memory_space=pltpu.HBM)
 
 
-def call(kernel, in_specs, outs, scratch=()):
+def call(kernel, in_specs, outs, scratch=(), out_specs=None, vmem_mib=40):
     return pl.pallas_call(
         kernel,
         out_shape=[jax.ShapeDtypeStruct(shape, dtype) for shape, dtype in outs],
         in_specs=in_specs,
-        out_specs=[VMEM] * len(outs),
+        out_specs=out_specs or [VMEM] * len(outs),
         scratch_shapes=list(scratch),
-        compiler_params=pltpu.CompilerParams(vmem_limit_bytes=48 * 1024 * 1024),
+        compiler_params=pltpu.CompilerParams(vmem_limit_bytes=vmem_mib * 1024 * 1024),
     )
 
 
@@ -314,15 +324,14 @@
         hidden, frozen_query_base[0], attention_output_grad[0], keys, values,
         adapter_down_weight.T, adapter_up_weight,
     )
-    low, send, rows = call(
+    low, send = call(
         prepare_kernel,
         [SMEM] * 3 + [HBM] * 7,
-        [
-            ((TOKENS, PADDED_RANK), BF16),
-            ((SLOTS, 16, SEND_WIDTH), BF16),
-            ((ROWS, SEND_WIDTH), BF16),
-        ],
-        [pltpu.VMEM(a.shape, BF16) for a in arrays] + [pltpu.SemaphoreType.DMA((7,))],
+        [((TOKENS, PADDED_RANK), BF16), ((SLOTS, 16, SEND_WIDTH), BF16)],
+        [pltpu.VMEM(a.shape, BF16) for a in arrays]
+        + [pltpu.VMEM((ROWS, SEND_WIDTH), BF16), pltpu.SemaphoreType.DMA((7 + SLOTS,))],
+        [VMEM, HBM],
+        60,
     )(adapter_rank, route, lengths, *arrays)
     arrived = lax.all_to_all(send, "prompt", 0, 0, tiled=True)
     back, dk, dv = call(
@@ -340,8 +349,8 @@
             ((1, TOKENS, KEY_VALUE_HEADS * HEAD_SIZE), BF16),
             ((GRAD_BLOCKS * PADDED_RANK, 128), BF16),
         ],
-        [pltpu.VMEM((ROWS, BACK_WIDTH), BF16)],
-    )(adapter_rank, route, hidden, keys, values, adapter_up_weight, low, rows, back)
+        [pltpu.VMEM((ROWS, SEND_WIDTH), BF16), pltpu.VMEM((ROWS, BACK_WIDTH), BF16)],
+    )(adapter_rank, route, hidden, keys, values, adapter_up_weight, low, send, back)
     down, up = call(
         spread_kernel,
         [VMEM],

time: 168 us -> 161 us (0.958)
  local copies, waits for them, and re-layouts: 8.83 us -> 0.18 us
    unnamed x34 -> x18, local copies, waits for them, and re-layouts: 8.71 us -> 0.05 us
where the time goes in v3:
time: 161 us; the launch traced here: 160 us
  blocking collectives  120 us (75%)
  waiting for transfers between devices  19.5 us (12%)
  Pallas kernels  18.1 us (11%)
    all_to_all x1, blocking collectives, per_device(): arrived = lax.all_to_all(send, 'prompt', 0, 0, tiled=True)  46.2 us
    all_to_all x1, blocking collectives, per_device(): lax.all_to_all(back.reshape(SLOTS, 16, BACK_WIDTH), 'prompt', 0, 0, tiled...  25 us
    all_to_all x1, blocking collectives, sum_all(): lax.all_to_all(replicate(total.astype(BF16), 16), 'comp', 0, 0, tiled=True)  24.7 us
    all_to_all x1, blocking collectives, sum_all(): lax.all_to_all(grads.reshape(16, rows // 16, 128), 'comp', 0, 0, tiled=True)  23.6 us
    ppermute x4, waiting for transfers between devices, sum_all(): lax.ppermute(total, 'prompt', [(i, flip(i)) for i in range(16)])  19.5 us
    pallas_call x1, Pallas kernels, per_device(): call(prepare_kernel, [SMEM] * 3 + [HBM] * 7, [((TOKENS, PADDED_RANK), BF1...  7.97 us
    pallas_call x1, Pallas kernels, per_device(): call(finish_kernel, [SMEM] * 2 + [VMEM] * 7, [((1, TOKENS, QUERY_WIDTH),...  4.68 us
    pallas_call x1, Pallas kernels, per_device(): call(owner_kernel, [VMEM] * 3, [((ROWS, BACK_WIDTH), BF16)] + [((PLEN, KE...  4.14 us
  transfers between devices with their start and end apart: 4, of which 4 were waited for; matrix products, arithmetic and copies ran while one was open for 0% of the time, Pallas kernels for 0%

profile of v3, /device:TPU:1, one launch (start us, length us, event | category | flops | bytes accessed | tf_op | source)
XLA Modules:
  0.0 160.4 jit_solution(6864077214279887250)
XLA Ops:
  1.3 8.0 %shard_map.171 = (bf16[128,64]{1,0:T(8,128)(2,1)}, bf16[16,16,2688]{2,1,0:T(8,128)(2,1)}) custom-call(s32[1]{0:T(128)S(6)} %copy.19.rank_ref, s32[1,1,16]{2,1,0:T(1,128)} %route_ref.3, s32[1,1,16]{2,1,0:T(1,128)} %length_ref.1, bf16[128,5120]{1,0:T(8,128)(2,1)} %bitcast.16, bf16[128,2560]{1,0:T(8,128)(2,1)} %bitcast.27, bf16[128,2560]{1,0:T(8,128)(2,1)} %bitcast.28, ...), custom_call_target="tpu_custom_call" | custom-call | tf_op jit(solution)/shard_map/pallas_call | solution.py:327
  9.3 0.0 copy-start.5
  9.3 0.0 copy-start.6
  9.3 0.0 copy-start.3
  9.3 0.0 copy-start.4
  9.3 46.2 %all_to_all.20 = bf16[16,16,2688]{2,1,0:T(8,128)(2,1)S(1)} all-to-all(bf16[16,16,2688]{2,1,0:T(8,128)(2,1)} %get-tuple-element.19.send_ref), channel_id=1, replica_groups=mesh['prompt'=16,'comp'=16] {'prompt'}, dimensions={0} | all-to-all | bytes 2752512 | tf_op jit(solution)/shard_map/all_to_all | solution.py:336
  55.5 0.0 copy-start.2
  55.5 0.0 copy-start.7
  55.5 4.1 %shard_map.172 = (bf16[256,1408]{1,0:T(8,128)(2,1)S(1)}, bf16[128,512]{1,0:T(8,128)(2,1)}, bf16[128,512]{1,0:T(8,128)(2,1)}) custom-call(bf16[256,2688]{1,0:T(8,128)(2,1)S(1)} %bitcast.15, bf16[128,512]{1,0:T(8,128)(2,1)S(1)} %bitcast.25, bf16[128,512]{1,0:T(8,128)(2,1)S(1)} %bitcast.26), custom_call_target="tpu_custom_call" | custom-call | tf_op jit(solution)/shard_map/pallas_call | solution.py:337
  59.7 25.0 %all_to_all.21.back_ref = bf16[16,16,1408]{2,1,0:T(8,128)(2,1)S(1)} all-to-all(bf16[16,16,1408]{2,1,0:T(8,128)(2,1)S(1)} %bitcast.20), channel_id=1, replica_groups=mesh['prompt'=16,'comp'=16] {'prompt'}, dimensions={0} | all-to-all | bytes 1441792 | tf_op jit(solution)/shard_map/all_to_all | solution.py:342
  84.8 4.7 %shard_map.173 = (bf16[1,128,2560]{2,1,0:T(8,128)(2,1)}, bf16[1,128,512]{2,1,0:T(8,128)(2,1)}, bf16[1,128,512]{2,1,0:T(8,128)(2,1)}, bf16[3840,128]{1,0:T(8,128)(2,1)S(1)}) custom-call(s32[1]{0:T(128)S(6)} %copy.19.rank_ref, s32[1,1,16]{2,1,0:T(1,128)S(1)} %copy-done.8, bf16[128,5120]{1,0:T(8,128)(2,1)S(1)} %bitcast.17, bf16[128,512]{1,0:T(8,128)(2,1)S(1)} %bitcast.22, ...), custom_call_target="tpu_custom_call" | custom-call | tf_op jit(solution)/shard_map/pallas_call | solution.py:343
  89.4 23.6 %all_to_all.22 = bf16[16,240,128]{2,1,0:T(8,128)(2,1)S(1)} all-to-all(bf16[16,240,128]{2,1,0:T(8,128)(2,1)S(1)} %bitcast.19), channel_id=1, replica_groups=mesh['prompt'=16,'comp'=16] {'comp'}, dimensions={0} | all-to-all | bytes 1966080 | tf_op jit(solution)/shard_map/all_to_all | solution.py:293
  113.1 0.1 convert_reduce_fusion
  113.2 0.1 collective-permute-start
  113.3 3.7 %collective-permute-done = f32[240,128]{1,0:T(8,128)S(1)} collective-permute-done((f32[240,128]{1,0:T(8,128)S(1)}, f32[240,128]{1,0:T(8,128)S(1)}, u32[]{:S(2)}, u32[]{:S(2)}) %collective-permute-start) | collective-permute-done | bytes 122912 | tf_op jit(solution)/shard_map/ppermute | solution.py:302
  117.0 0.7 collective-permute-start.1
  117.7 4.4 %collective-permute-done.1 = f32[240,128]{1,0:T(8,128)S(1)} collective-permute-done((f32[240,128]{1,0:T(8,128)S(1)}, f32[240,128]{1,0:T(8,128)S(1)}, u32[]{:S(2)}, u32[]{:S(2)}) %collective-permute-start.1) | collective-permute-done | bytes 122912 | tf_op jit(solution)/shard_map/ppermute | solution.py:302
  122.1 0.5 collective-permute-start.2
  122.6 5.5 %collective-permute-done.2 = f32[240,128]{1,0:T(8,128)S(1)} collective-permute-done((f32[240,128]{1,0:T(8,128)S(1)}, f32[240,128]{1,0:T(8,128)S(1)}, u32[]{:S(2)}, u32[]{:S(2)}) %collective-permute-start.2) | collective-permute-done | bytes 122912 | tf_op jit(solution)/shard_map/ppermute | solution.py:302
  128.1 0.1 collective-permute-start.3
  128.2 5.9 %collective-permute-done.3 = f32[240,128]{1,0:T(8,128)S(1)} collective-permute-done((f32[240,128]{1,0:T(8,128)S(1)}, f32[240,128]{1,0:T(8,128)S(1)}, u32[]{:S(2)}, u32[]{:S(2)}) %collective-permute-start.3) | collective-permute-done | bytes 122912 | tf_op jit(solution)/shard_map/ppermute | solution.py:302
  134.2 0.1 broadcast_in_dim.14
  134.3 24.7 %all_to_all.23 = bf16[16,240,128]{2,1,0:T(8,128)(2,1)S(1)} all-to-all(bf16[16,240,128]{2,1,0:T(8,128)(2,1)S(1)} %broadcast_in_dim.14), channel_id=1, replica_groups=mesh['prompt'=16,'comp'=16] {'comp'}, dimensions={0} | all-to-all | bytes 1966080 | tf_op jit(solution)/shard_map/all_to_all | solution.py:303
  159.1 1.4 shard_map.174
  (16 shorter events, 0.1 us)
Async XLA Ops:
  9.3 46.2 %copy-start.5 = (bf16[1,128,512]{2,1,0:T(8,128)(2,1)S(1)}, bf16[1,128,512]{2,1,0:T(8,128)(2,1)}, u32[]{:S(2)}) copy-start(bf16[1,128,512]{2,1,0:T(8,128)(2,1)} %param.17) | copy-start | bytes 393220
  9.3 46.2 %copy-start.6 = (bf16[1,128,512]{2,1,0:T(8,128)(2,1)S(1)}, bf16[1,128,512]{2,1,0:T(8,128)(2,1)}, u32[]{:S(2)}) copy-start(bf16[1,128,512]{2,1,0:T(8,128)(2,1)} %param.18) | copy-start | bytes 393220
  9.3 75.4 %copy-start.3 = (bf16[1,128,512]{2,1,0:T(8,128)(2,1)S(1)}, bf16[1,128,512]{2,1,0:T(8,128)(2,1)}, u32[]{:S(2)}) copy-start(bf16[1,128,512]{2,1,0:T(8,128)(2,1)} %param.15) | copy-start | bytes 393220
  9.3 75.4 %copy-start.4 = (bf16[1,128,512]{2,1,0:T(8,128)(2,1)S(1)}, bf16[1,128,512]{2,1,0:T(8,128)(2,1)}, u32[]{:S(2)}) copy-start(bf16[1,128,512]{2,1,0:T(8,128)(2,1)} %param.16) | copy-start | bytes 393220
  55.5 29.2 %copy-start = (bf16[16,16,2688]{2,1,0:T(8,128)(2,1)S(1)}, bf16[16,16,2688]{2,1,0:T(8,128)(2,1)}, u32[]{:S(2)}) copy-start(bf16[16,16,2688]{2,1,0:T(8,128)(2,1)} %get-tuple-element.19.send_ref) | copy-start | bytes 4128772
  55.5 29.2 %copy-start.1 = (bf16[1,128,5120]{2,1,0:T(8,128)(2,1)S(1)}, bf16[1,128,5120]{2,1,0:T(8,128)(2,1)}, u32[]{:S(2)}) copy-start(bf16[1,128,5120]{2,1,0:T(8,128)(2,1)} %param.12) | copy-start | bytes 3932164
  55.5 29.2 %copy-start.2 = (bf16[64,2560]{1,0:T(8,128)(2,1)S(1)}, bf16[64,2560]{1,0:T(8,128)(2,1)}, u32[]{:S(2)}) copy-start(bf16[64,2560]{1,0:T(8,128)(2,1)} %wu_ref.1) | copy-start | bytes 983044
  55.5 29.2 %copy-start.7 = (bf16[128,64]{1,0:T(8,128)(2,1)S(1)}, bf16[128,64]{1,0:T(8,128)(2,1)}, u32[]{:S(2)}) copy-start(bf16[128,64]{1,0:T(8,128)(2,1)} %get-tuple-element.18.low_ref) | copy-start | bytes 49156
  55.5 29.2 %copy-start.8 = (s32[1,1,16]{2,1,0:T(1,128)S(1)}, s32[1,1,16]{2,1,0:T(1,128)}, u32[]{:S(2)}) copy-start(s32[1,1,16]{2,1,0:T(1,128)} %route_ref.3) | copy-start | bytes 196
  113.2 3.8 %collective-permute-start = (f32[240,128]{1,0:T(8,128)S(1)}, f32[240,128]{1,0:T(8,128)S(1)}, u32[]{:S(2)}, u32[]{:S(2)}) collective-permute-start(f32[240,128]{1,0:T(8,128)S(1)} %convert_reduce_fusion), channel_id=1, source_target_pairs={{0,64},{16,80},{32,96},{48,112},{64,0},{80,16},{96,32},{112,48},{1... | collective-permute-start | bytes 368648 | tf_op jit(solution)/shard_map/ppermute | solution.py:302
  117.0 5.0 %collective-permute-start.1 = (f32[240,128]{1,0:T(8,128)S(1)}, f32[240,128]{1,0:T(8,128)S(1)}, u32[]{:S(2)}, u32[]{:S(2)}) collective-permute-start(f32[240,128]{1,0:T(8,128)S(1)} %add.12), channel_id=1, source_target_pairs={{0,192},{16,208},{32,224},{48,240},{64,128},{80,144},{96,160},{112... | collective-permute-start | bytes 368648 | tf_op jit(solution)/shard_map/ppermute | solution.py:302
  122.1 6.0 %collective-permute-start.2 = (f32[240,128]{1,0:T(8,128)S(1)}, f32[240,128]{1,0:T(8,128)S(1)}, u32[]{:S(2)}, u32[]{:S(2)}) collective-permute-start(f32[240,128]{1,0:T(8,128)S(1)} %add.13), channel_id=1, source_target_pairs={{0,16},{16,0},{32,48},{48,32},{64,80},{80,64},{96,112},{112,96},{1... | collective-permute-start | bytes 368648 | tf_op jit(solution)/shard_map/ppermute | solution.py:302
  128.1 6.0 %collective-permute-start.3 = (f32[240,128]{1,0:T(8,128)S(1)}, f32[240,128]{1,0:T(8,128)S(1)}, u32[]{:S(2)}, u32[]{:S(2)}) collective-permute-start(f32[240,128]{1,0:T(8,128)S(1)} %add.14), channel_id=1, source_target_pairs={{0,48},{16,32},{32,16},{48,0},{64,112},{80,96},{96,80},{112,64},{1... | collective-permute-start | bytes 368648 | tf_op jit(solution)/shard_map/ppermute | solution.py:302

commit v4 on v3

--- a/solution.py
+++ b/solution.py
@@ -1,3 +1,4 @@
+import functools
 import math
 
 import jax
@@ -26,6 +27,8 @@
 BACK_WIDTH = HALF + 128
 DOWN_BLOCKS = MODEL_WIDTH // 128
 GRAD_BLOCKS = (MODEL_WIDTH + QUERY_WIDTH) // 128
+CORE_BLOCKS = 32
+CORE_ROWS = CORE_BLOCKS * PADDED_RANK
 
 INV_SQRT = 1.0 / math.sqrt(HEAD_SIZE)
 adapter_strength = 32.0
@@ -213,8 +216,8 @@
 
 
 def finish_kernel(
-    rank_ref, route_ref, x_ref, sk_ref, sv_ref, wu_ref, low_ref, send_ref, back_ref,
-    dq_ref, dsk_ref, dsv_ref, grads_ref, rows_ref, dq_rows_ref,
+    rank_ref, route_ref, core_ref, x_ref, sk_ref, sv_ref, wu_ref, low_ref, send_ref, back_ref,
+    dq_ref, dsk_ref, dsv_ref, mine_ref, other_ref, rows_ref, dq_rows_ref,
 ):
     rank = rank_ref[0]
     scale = adapter_strength / rank.astype(F32)
@@ -249,18 +252,30 @@
     keep = lax.broadcasted_iota(jnp.int32, (TOKENS, PADDED_RANK), 1) < rank
     lifted = jnp.where(keep, scale * nt(dq, wu_ref[...]), 0.0).astype(BF16)
     low = low_ref[...]
+
+    def block(c):
+        if c < DOWN_BLOCKS:
+            return tn(lifted, x_ref[:, c * 128 : (c + 1) * 128])
+        if c < GRAD_BLOCKS:
+            at = (c - DOWN_BLOCKS) * 128
+            return scale * tn(low, dq[:, at : at + 128])
+        return jnp.zeros((PADDED_RANK, 128), F32)
+
+    first = core_ref[0] == 0
+    for c in range(CORE_BLOCKS):
+        lower, upper = block(c), block(c + CORE_BLOCKS)
+        at = slice(c * PADDED_RANK, (c + 1) * PADDED_RANK)
+        mine_ref[at, :] = jnp.where(first, lower, upper).astype(BF16)
+        other_ref[at, :] = jnp.where(first, upper, lower).astype(BF16)
+
+
+def spread_kernel(core_ref, mine_ref, other_ref, down_ref, up_ref):
+    first = core_ref[0] == 0
     for c in range(GRAD_BLOCKS):
-        if c < DOWN_BLOCKS:
-            part = tn(lifted, x_ref[:, c * 128 : (c + 1) * 128])
-        else:
-            at = (c - DOWN_BLOCKS) * 128
-            part = scale * tn(low, dq[:, at : at + 128])
-        grads_ref[c * PADDED_RANK : (c + 1) * PADDED_RANK, :] = part.astype(BF16)
-
-
-def spread_kernel(grads_ref, down_ref, up_ref):
-    for c in range(GRAD_BLOCKS):
-        part = grads_ref[c * PADDED_RANK : (c + 1) * PADDED_RANK, :].astype(F32)
+        at = c % CORE_BLOCKS * PADDED_RANK
+        mine = mine_ref[at : at + PADDED_RANK, :].astype(F32)
+        other = other_ref[at : at + PADDED_RANK, :].astype(F32)
+        part = jnp.where(first, mine, other) if c < CORE_BLOCKS else jnp.where(first, other, mine)
         if c < DOWN_BLOCKS:
             down_ref[:, c * 128 : (c + 1) * 128] = part
         else:
@@ -284,24 +299,31 @@
     )
 
 
-def replicate(part, count):
-    return jnp.broadcast_to(part[None], (count,) + part.shape)
-
-
-def sum_all(grads):
-    rows = GRAD_BLOCKS * PADDED_RANK
-    parts = lax.all_to_all(grads.reshape(16, rows // 16, 128), "comp", 0, 0, tiled=True)
-    total = jnp.sum(parts.astype(F32), axis=0)
-    flips = (
-        lambda i: i ^ 4,
-        lambda i: (3 - i // 4) * 4 + i % 4,
-        lambda i: i ^ 1,
-        lambda i: i // 4 * 4 + 3 - i % 4,
-    )
-    for flip in flips:
+def by_core(part):
+    return lax.ppermute(part, "comp", [(i, i ^ 1) for i in range(16)])
+
+
+def layer_groups():
+    return [
+        [(x * 4 + z_hi) * 16 + zy * 2 + core for x in range(4) for zy in range(8)]
+        for z_hi in range(4)
+        for core in range(2)
+    ]
+
+
+def sum_all(mine, other):
+    rows = CORE_ROWS // 32
+    swap = functools.partial(
+        lax.all_to_all, axis_name=("prompt", "comp"), split_axis=0, concat_axis=0,
+        axis_index_groups=layer_groups(), tiled=True,
+    )
+    pair = (mine.astype(F32) + by_core(other).astype(F32)).astype(BF16)
+    total = jnp.sum(swap(pair.reshape(32, rows, 128)).astype(F32), axis=0)
+    for flip in (lambda i: i ^ 1, lambda i: i // 4 * 4 + 3 - i % 4):
         total = total + lax.ppermute(total, "prompt", [(i, flip(i)) for i in range(16)])
-    whole = lax.all_to_all(replicate(total.astype(BF16), 16), "comp", 0, 0, tiled=True)
-    return whole.reshape(rows, 128)
+    total = total.astype(BF16)
+    half = swap(jnp.broadcast_to(total[None], (32, rows, 128))).reshape(CORE_ROWS, 128)
+    return half, by_core(half)
 
 
 def per_device(
@@ -340,22 +362,24 @@
         [((ROWS, BACK_WIDTH), BF16)] + [((PLEN, KEY_VALUE_HEADS * HEAD_SIZE), BF16)] * 2,
     )(arrived.reshape(ROWS, SEND_WIDTH), owner_prompt_keys[0], owner_prompt_values[0])
     back = lax.all_to_all(back.reshape(SLOTS, 16, BACK_WIDTH), "prompt", 0, 0, tiled=True)
-    dq, dsk, dsv, grads = call(
+    core = (lax.axis_index("comp") % 2).astype(jnp.int32)[None]
+    dq, dsk, dsv, mine, other = call(
         finish_kernel,
-        [SMEM] * 2 + [VMEM] * 7,
+        [SMEM] * 3 + [VMEM] * 7,
         [
             ((1, TOKENS, QUERY_WIDTH), BF16),
             ((1, TOKENS, KEY_VALUE_HEADS * HEAD_SIZE), BF16),
             ((1, TOKENS, KEY_VALUE_HEADS * HEAD_SIZE), BF16),
-            ((GRAD_BLOCKS * PADDED_RANK, 128), BF16),
+            ((CORE_ROWS, 128), BF16),
+            ((CORE_ROWS, 128), BF16),
         ],
         [pltpu.VMEM((ROWS, SEND_WIDTH), BF16), pltpu.VMEM((ROWS, BACK_WIDTH), BF16)],
-    )(adapter_rank, route, hidden, keys, values, adapter_up_weight, low, send, back)
+    )(adapter_rank, route, core, hidden, keys, values, adapter_up_weight, low, send, back)
     down, up = call(
         spread_kernel,
-        [VMEM],
+        [SMEM] + [VMEM] * 2,
         [((PADDED_RANK, MODEL_WIDTH), F32), ((PADDED_RANK, QUERY_WIDTH), F32)],
-    )(sum_all(grads))
+    )(core, *sum_all(mine, other))
     return dq, dsk, dsv, dk[None], dv[None], down.T, up
 
 

time: 161 us -> 146 us (0.907)
  blocking collectives: 120 us -> 75.9 us
  starting transfers between devices: 1.34 us -> 15.6 us
  waiting for transfers between devices: 19.5 us -> 29.9 us
  local copies, waits for them, and re-layouts: 0.18 us -> 3.63 us
    all_to_all x3 -> x2, blocking collectives: 73.4 us -> 29.6 us  [the longest x1 16.5 us: sum_all(): total = jnp.sum(swap(pair.reshape(32, rows, 128)).astype(F32), axis=0)]
    all_to_all x0 -> x1, waiting for transfers between devices: none -> 19.2 us  [per_device(): lax.all_to_all(back.reshape(SLOTS, 16, BACK_WIDTH), 'prompt', 0, 0, tiled...]
    ppermute x4 -> x2, waiting for transfers between devices: 19.5 us -> 7.59 us  [sum_all(): lax.ppermute(total, 'prompt', [(i, flip(i)) for i in range(16)])]
    ppermute x0 -> x2, starting transfers between devices: none -> 8.95 us  [by_core(): return lax.ppermute(part, 'comp', [(i, i ^ 1) for i in range(16)])]
    all_to_all x0 -> x1, starting transfers between devices: none -> 5.25 us  [per_device(): lax.all_to_all(back.reshape(SLOTS, 16, BACK_WIDTH), 'prompt', 0, 0, tiled...]
    unnamed x18 -> x20, local copies, waits for them, and re-layouts: 0.05 us -> 3.52 us
    ppermute x0 -> x2, waiting for transfers between devices: none -> 3.07 us  [by_core(): return lax.ppermute(part, 'comp', [(i, i ^ 1) for i in range(16)])]
  transfers between devices with their start and end apart: 4 -> 5, of which waited for: 4 -> 5; matrix products, arithmetic and copies ran while one was open for 0% -> 0% of each run, Pallas kernels for 0% -> 0%
where the time goes in v4:
time: 146 us; the launch traced here: 145 us
  blocking collectives  75.9 us (52%)
  waiting for transfers between devices  29.9 us (20%)
  Pallas kernels  18.9 us (13%)
  starting transfers between devices  15.6 us (11%)
  local copies, waits for them, and re-layouts  3.63 us (2%)
    all_to_all x1, blocking collectives, per_device(): arrived = lax.all_to_all(send, 'prompt', 0, 0, tiled=True)  46.2 us
    all_to_all x1, waiting for transfers between devices, per_device(): lax.all_to_all(back.reshape(SLOTS, 16, BACK_WIDTH), 'prompt', 0, 0, tiled...  19.2 us
    all_to_all x1, blocking collectives, sum_all(): total = jnp.sum(swap(pair.reshape(32, rows, 128)).astype(F32), axis=0)  16.5 us
    all_to_all x1, blocking collectives, sum_all(): swap(jnp.broadcast_to(total[None], (32, rows, 128))).reshape(CORE_ROWS, 128)  13.1 us
    ppermute x2, starting transfers between devices, by_core(): return lax.ppermute(part, 'comp', [(i, i ^ 1) for i in range(16)])  8.95 us
    pallas_call x1, Pallas kernels, per_device(): call(prepare_kernel, [SMEM] * 3 + [HBM] * 7, [((TOKENS, PADDED_RANK), BF1...  7.97 us
    ppermute x2, waiting for transfers between devices, sum_all(): lax.ppermute(total, 'prompt', [(i, flip(i)) for i in range(16)])  7.59 us
    pallas_call x1, Pallas kernels, per_device(): call(finish_kernel, [SMEM] * 3 + [VMEM] * 7, [((1, TOKENS, QUERY_WIDTH),...  5.38 us
  transfers between devices with their start and end apart: 5, of which 5 were waited for; matrix products, arithmetic and copies ran while one was open for 0% of the time, Pallas kernels for 0%

profile of v4, /device:TPU:1, one launch (start us, length us, event | category | flops | bytes accessed | tf_op | source)
XLA Modules:
  0.0 145.5 jit_solution(4747357636918029565)
XLA Ops:
  1.3 8.0 %shard_map.171 = (bf16[128,64]{1,0:T(8,128)(2,1)}, bf16[16,16,2688]{2,1,0:T(8,128)(2,1)}) custom-call(s32[1]{0:T(128)S(6)} %copy.19.rank_ref, s32[1,1,16]{2,1,0:T(1,128)} %route_ref.3, s32[1,1,16]{2,1,0:T(1,128)} %length_ref.1, bf16[128,5120]{1,0:T(8,128)(2,1)} %bitcast.17, bf16[128,2560]{1,0:T(8,128)(2,1)} %bitcast.29, bf16[128,2560]{1,0:T(8,128)(2,1)} %bitcast.30, ...), custom_call_target="tpu_custom_call" | custom-call | tf_op jit(solution)/shard_map/pallas_call | solution.py:349
  9.3 46.2 %all_to_all.20 = bf16[16,16,2688]{2,1,0:T(8,128)(2,1)S(1)} all-to-all(bf16[16,16,2688]{2,1,0:T(8,128)(2,1)} %get-tuple-element.20.send_ref), channel_id=1, replica_groups=mesh['prompt'=16,'comp'=16] {'prompt'}, dimensions={0} | all-to-all | bytes 2752512 | tf_op jit(solution)/shard_map/all_to_all | solution.py:358
  55.5 4.1 %shard_map.172 = (bf16[256,1408]{1,0:T(8,128)(2,1)S(1)}, bf16[128,512]{1,0:T(8,128)(2,1)}, bf16[128,512]{1,0:T(8,128)(2,1)}) custom-call(bf16[256,2688]{1,0:T(8,128)(2,1)S(1)} %bitcast.16, bf16[128,512]{1,0:T(8,128)(2,1)S(1)} %bitcast.26, bf16[128,512]{1,0:T(8,128)(2,1)S(1)} %bitcast.27), custom_call_target="tpu_custom_call" | custom-call | tf_op jit(solution)/shard_map/pallas_call | solution.py:359
  59.7 0.9 copy-done.3
  60.5 5.3 %all-to-all-start.1 = ((bf16[16,16,1408]{2,1,0:T(8,128)(2,1)}), bf16[16,16,1408]{2,1,0:T(8,128)(2,1)S(1)}, u32[]{:S(2)}, u32[]{:S(2)}) async-start(bf16[16,16,1408]{2,1,0:T(8,128)(2,1)} %bitcast.21), calls=%async_computation.1 | async-start | bytes 1441792 | tf_op jit(solution)/shard_map/all_to_all | solution.py:364
  65.8 19.2 %all-to-all-done.1.back_ref = bf16[16,16,1408]{2,1,0:T(8,128)(2,1)S(1)} async-done(((bf16[16,16,1408]{2,1,0:T(8,128)(2,1)}), bf16[16,16,1408]{2,1,0:T(8,128)(2,1)S(1)}, u32[]{:S(2)}, u32[]{:S(2)}) %all-to-all-start.1) | async-done | bytes 720928 | tf_op jit(solution)/shard_map/all_to_all | solution.py:364
  85.0 1.0 copy-done.2
  86.0 0.9 copy-done.5
  86.9 0.8 copy-done.8
  87.7 5.4 %shard_map.173 = (bf16[1,128,2560]{2,1,0:T(8,128)(2,1)}, bf16[1,128,512]{2,1,0:T(8,128)(2,1)}, bf16[1,128,512]{2,1,0:T(8,128)(2,1)}, bf16[2048,128]{1,0:T(8,128)(2,1)S(1)}, bf16[2048,128]{1,0:T(8,128)(2,1)S(1)}) custom-call(s32[1]{0:T(128)S(6)} %copy.19.rank_ref, s32[1,1,16]{2,1,0:T(1,128)S(1)} %copy-done.9, s32[1]{0:T(128)} %bitcast.core_ref, ...), custom_call_target="tpu_custom_call" | custom-call | tf_op jit(solution)/shard_map/pallas_call | solution.py:366
  93.0 3.7 %collective-permute-start = (bf16[2048,128]{1,0:T(8,128)(2,1)S(1)}, bf16[2048,128]{1,0:T(8,128)(2,1)S(1)}, u32[]{:S(2)}, u32[]{:S(2)}) collective-permute-start(bf16[2048,128]{1,0:T(8,128)(2,1)S(1)} %get-tuple-element.28), channel_id=1, source_target_pairs={{0,1},{1,0},{2,3},{3,2},{4,5},{5,4},{6,7},{7,6},{8,9},{9,8},{10,11... | collective-permute-start | bytes 1572872 | tf_op jit(solution)/shard_map/ppermute | solution.py:303
  96.8 1.5 %collective-permute-done = bf16[2048,128]{1,0:T(8,128)(2,1)S(1)} collective-permute-done((bf16[2048,128]{1,0:T(8,128)(2,1)S(1)}, bf16[2048,128]{1,0:T(8,128)(2,1)S(1)}, u32[]{:S(2)}, u32[]{:S(2)}) %collective-permute-start) | collective-permute-done | bytes 524320 | tf_op jit(solution)/shard_map/ppermute | solution.py:303
  98.3 0.1 add_convert_fusion
  98.5 16.5 %all_to_all.21 = bf16[32,64,128]{2,1,0:T(8,128)(2,1)S(1)} all-to-all(bf16[32,64,128]{2,1,0:T(8,128)(2,1)S(1)} %bitcast.28), channel_id=1, replica_groups={{0,2,4,6,8,10,12,14,64,66,68,70,72,74,76,78,128,130,132,134,136,138,140..., dimensions={0} | all-to-all | bytes 1048576 | tf_op jit(solution)/shard_map/all_to_all | solution.py:321
  115.0 0.1 convert_reduce_fusion
  115.1 0.3 collective-permute-start.1
  115.4 3.8 %collective-permute-done.1 = f32[64,128]{1,0:T(8,128)S(1)} collective-permute-done((f32[64,128]{1,0:T(8,128)S(1)}, f32[64,128]{1,0:T(8,128)S(1)}, u32[]{:S(2)}, u32[]{:S(2)}) %collective-permute-start.1) | collective-permute-done | bytes 32800 | tf_op jit(solution)/shard_map/ppermute | solution.py:323
  119.2 1.1 collective-permute-start.2
  120.3 3.8 %collective-permute-done.2 = f32[64,128]{1,0:T(8,128)S(1)} collective-permute-done((f32[64,128]{1,0:T(8,128)S(1)}, f32[64,128]{1,0:T(8,128)S(1)}, u32[]{:S(2)}, u32[]{:S(2)}) %collective-permute-start.2) | collective-permute-done | bytes 32800 | tf_op jit(solution)/shard_map/ppermute | solution.py:323
  124.1 0.1 broadcast_in_dim.18
  124.2 13.1 %all_to_all.22 = bf16[32,64,128]{2,1,0:T(8,128)(2,1)S(1)} all-to-all(bf16[32,64,128]{2,1,0:T(8,128)(2,1)S(1)} %broadcast_in_dim.18), channel_id=1, replica_groups={{0,2,4,6,8,10,12,14,64,66,68,70,72,74,76,78,128,130,132,134,136,138,140..., dimensions={0} | all-to-all | bytes 1048576 | tf_op jit(solution)/shard_map/all_to_all | solution.py:325
  137.3 5.2 %collective-permute-start.3 = (bf16[2048,128]{1,0:T(8,128)(2,1)S(1)}, bf16[2048,128]{1,0:T(8,128)(2,1)S(1)}, u32[]{:S(2)}, u32[]{:S(2)}) collective-permute-start(bf16[2048,128]{1,0:T(8,128)(2,1)S(1)} %bitcast.19), channel_id=1, source_target_pairs={{0,1},{1,0},{2,3},{3,2},{4,5},{5,4},{6,7},{7,6},{8,9},{9,8},{10,11... | collective-permute-start | bytes 1572872 | tf_op jit(solution)/shard_map/ppermute | solution.py:303
  142.5 1.5 %collective-permute-done.3.other_ref = bf16[2048,128]{1,0:T(8,128)(2,1)S(1)} collective-permute-done((bf16[2048,128]{1,0:T(8,128)(2,1)S(1)}, bf16[2048,128]{1,0:T(8,128)(2,1)S(1)}, u32[]{:S(2)}, u32[]{:S(2)}) %collective-permute-start.3) | collective-permute-done | bytes 524320 | tf_op jit(solution)/shard_map/ppermute | solution.py:303
  144.0 1.4 shard_map.174
  (18 shorter events, 0.1 us)
Async XLA Ops:
  9.3 46.3 %copy-start.6 = (bf16[1,128,512]{2,1,0:T(8,128)(2,1)S(1)}, bf16[1,128,512]{2,1,0:T(8,128)(2,1)}, u32[]{:S(2)}) copy-start(bf16[1,128,512]{2,1,0:T(8,128)(2,1)} %param.17) | copy-start | bytes 393220
  9.3 46.2 %copy-start.7 = (bf16[1,128,512]{2,1,0:T(8,128)(2,1)S(1)}, bf16[1,128,512]{2,1,0:T(8,128)(2,1)}, u32[]{:S(2)}) copy-start(bf16[1,128,512]{2,1,0:T(8,128)(2,1)} %param.18) | copy-start | bytes 393220
  55.5 29.5 %copy-start = (bf16[16,16,2688]{2,1,0:T(8,128)(2,1)S(1)}, bf16[16,16,2688]{2,1,0:T(8,128)(2,1)}, u32[]{:S(2)}) copy-start(bf16[16,16,2688]{2,1,0:T(8,128)(2,1)} %get-tuple-element.20.send_ref) | copy-start | bytes 4128772
  55.5 29.5 %copy-start.1 = (bf16[1,128,5120]{2,1,0:T(8,128)(2,1)S(1)}, bf16[1,128,5120]{2,1,0:T(8,128)(2,1)}, u32[]{:S(2)}) copy-start(bf16[1,128,5120]{2,1,0:T(8,128)(2,1)} %param.12) | copy-start | bytes 3932164
  55.5 29.5 %copy-start.4 = (bf16[1,128,512]{2,1,0:T(8,128)(2,1)S(1)}, bf16[1,128,512]{2,1,0:T(8,128)(2,1)}, u32[]{:S(2)}) copy-start(bf16[1,128,512]{2,1,0:T(8,128)(2,1)} %param.15) | copy-start | bytes 393220
  55.5 29.5 %copy-start.9 = (s32[1,1,16]{2,1,0:T(1,128)S(1)}, s32[1,1,16]{2,1,0:T(1,128)}, u32[]{:S(2)}) copy-start(s32[1,1,16]{2,1,0:T(1,128)} %route_ref.3) | copy-start | bytes 196
  59.7 0.9 copy-start.3
  60.5 24.5 %all-to-all-start.1 = ((bf16[16,16,1408]{2,1,0:T(8,128)(2,1)}), bf16[16,16,1408]{2,1,0:T(8,128)(2,1)S(1)}, u32[]{:S(2)}, u32[]{:S(2)}) async-start(bf16[16,16,1408]{2,1,0:T(8,128)(2,1)} %bitcast.21), calls=%async_computation.1 | async-start | bytes 1441792 | tf_op jit(solution)/shard_map/all_to_all | solution.py:364
  85.0 1.0 copy-start.2
  86.0 0.9 copy-start.5
  86.9 0.8 copy-start.8
  93.0 5.3 %collective-permute-start = (bf16[2048,128]{1,0:T(8,128)(2,1)S(1)}, bf16[2048,128]{1,0:T(8,128)(2,1)S(1)}, u32[]{:S(2)}, u32[]{:S(2)}) collective-permute-start(bf16[2048,128]{1,0:T(8,128)(2,1)S(1)} %get-tuple-element.28), channel_id=1, source_target_pairs={{0,1},{1,0},{2,3},{3,2},{4,5},{5,4},{6,7},{7,6},{8,9},{9,8},{10,11... | collective-permute-start | bytes 1572872 | tf_op jit(solution)/shard_map/ppermute | solution.py:303
  115.1 4.1 %collective-permute-start.1 = (f32[64,128]{1,0:T(8,128)S(1)}, f32[64,128]{1,0:T(8,128)S(1)}, u32[]{:S(2)}, u32[]{:S(2)}) collective-permute-start(f32[64,128]{1,0:T(8,128)S(1)} %convert_reduce_fusion), channel_id=1, source_target_pairs={{0,16},{16,0},{32,48},{48,32},{64,80},{80,64},{96,112},{112,96},{1... | collective-permute-start | bytes 98312 | tf_op jit(solution)/shard_map/ppermute | solution.py:323
  119.2 4.9 %collective-permute-start.2 = (f32[64,128]{1,0:T(8,128)S(1)}, f32[64,128]{1,0:T(8,128)S(1)}, u32[]{:S(2)}, u32[]{:S(2)}) collective-permute-start(f32[64,128]{1,0:T(8,128)S(1)} %add.15), channel_id=1, source_target_pairs={{0,48},{16,32},{32,16},{48,0},{64,112},{80,96},{96,80},{112,64},{1... | collective-permute-start | bytes 98312 | tf_op jit(solution)/shard_map/ppermute | solution.py:323
  137.3 6.8 %collective-permute-start.3 = (bf16[2048,128]{1,0:T(8,128)(2,1)S(1)}, bf16[2048,128]{1,0:T(8,128)(2,1)S(1)}, u32[]{:S(2)}, u32[]{:S(2)}) collective-permute-start(bf16[2048,128]{1,0:T(8,128)(2,1)S(1)} %bitcast.19), channel_id=1, source_target_pairs={{0,1},{1,0},{2,3},{3,2},{4,5},{5,4},{6,7},{7,6},{8,9},{9,8},{10,11... | collective-permute-start | bytes 1572872 | tf_op jit(solution)/shard_map/ppermute | solution.py:303

commit v5 on v4

--- a/solution.py
+++ b/solution.py
@@ -24,6 +24,8 @@
 PADDED_RANK = 64
 QUERY_WIDTH = QUERY_HEADS * HEAD_SIZE
 SEND_WIDTH = 2 * HALF + 128
+X_PARTS = 4
+X_PART = MODEL_WIDTH // X_PARTS
 BACK_WIDTH = HALF + 128
 DOWN_BLOCKS = MODEL_WIDTH // 128
 GRAD_BLOCKS = (MODEL_WIDTH + QUERY_WIDTH) // 128
@@ -91,7 +93,7 @@
     second = rest.astype(BF16).astype(F32)
     third = rest - second
     pad = jnp.zeros((128 - 3 * len(rows), ROWS), F32)
-    return jnp.concatenate([first, second, third, pad], axis=0).T.astype(BF16)
+    return jnp.concatenate([first, second, third, pad], axis=0).T
 
 
 def unpack_stats(columns, count):
@@ -100,18 +102,35 @@
 
 
 def prepare_kernel(
-    rank_ref, route_ref, length_ref, x_hbm, base_hbm, g_hbm, sk_hbm, sv_hbm, wd_hbm, wu_hbm,
-    low_ref, send_hbm,
-    x_ref, base_ref, g_ref, sk_ref, sv_ref, wd_ref, wu_ref, rows_ref, sems,
+    rank_hbm, route_hbm, length_hbm, x_hbm, base_hbm, g_hbm, sk_hbm, sv_hbm, wd_hbm, wu_hbm,
+    send_hbm,
+    rank_ref, route_ref, length_ref, x_ref, base_ref, g_ref, sk_ref, sv_ref, wd_ref, wu_ref, rows_ref, sems,
 ):
-    sources = (g_hbm, sv_hbm, sk_hbm, wd_hbm, x_hbm, wu_hbm, base_hbm)
-    targets = (g_ref, sv_ref, sk_ref, wd_ref, x_ref, wu_ref, base_ref)
-    copies = [
+    columns = [slice(i * X_PART, (i + 1) * X_PART) for i in range(X_PARTS)]
+    pairs = [(rank_hbm, rank_ref), (length_hbm, length_ref), (route_hbm, route_ref)]
+    pairs += [(wd_hbm, wd_ref)] + [(x_hbm.at[:, c], x_ref.at[:, c]) for c in columns]
+    pairs += [
+        (g_hbm, g_ref), (sv_hbm, sv_ref), (sk_hbm, sk_ref), (wu_hbm, wu_ref), (base_hbm, base_ref)
+    ]
+    loads = [
         pltpu.make_async_copy(source, target, sems.at[i])
-        for i, (source, target) in enumerate(zip(sources, targets))
-    ]
-    for copy in copies:
+        for i, (source, target) in enumerate(pairs)
+    ]
+    for copy in loads:
         copy.start()
+
+    def sends(start, width, sem):
+        return [
+            pltpu.make_async_copy(
+                rows_ref.at[pl.ds(s * 16, 16), pl.ds(start, width)],
+                send_hbm.at[route_ref[0, 0, s], :, pl.ds(start, width)],
+                sems.at[sem + s],
+            )
+            for s in range(SLOTS)
+        ]
+
+    for copy in loads[:3]:
+        copy.wait()
     rank = rank_ref[0]
     scale = adapter_strength / rank.astype(F32)
     position = lax.broadcasted_iota(jnp.int32, (CL, 128), 0)
@@ -119,53 +138,58 @@
         [jnp.where(position < length_ref[0, 0, s], 1.0, 0.0) for s in range(SLOTS)], axis=0
     )
     mask = own_mask()
-    copies[0].wait()
+    loads[3].wait()
+    low = jnp.zeros((TOKENS, PADDED_RANK), F32)
+    for i, c in enumerate(columns):
+        loads[4 + i].wait()
+        low = low + nt(x_ref[:, c], wd_ref[:, c])
+    rest = 4 + X_PARTS
+    loads[rest].wait()
     for n in range(PAIRS):
         left, right = (g_ref[:, m * 128 : (m + 1) * 128].astype(F32) * live for m in (n, n + PAIRS))
-        rows_ref[:, HALF + n * 128 : HALF + (n + 1) * 128] = fold(
+        rows_ref[:, n * 128 : (n + 1) * 128] = fold(
             jnp.concatenate([left, right], axis=1)
         ).astype(BF16)
-    copies[1].wait()
+    early = sends(0, HALF, rest + 5)
+    for copy in early:
+        copy.start()
+    for copy in loads[rest + 1 :]:
+        copy.wait()
     values = fold(sv_ref[...].astype(F32)).astype(BF16)
-    copies[2].wait()
     keys = fold(sk_ref[...].astype(F32)).astype(BF16)
-    copies[3].wait()
-    copies[4].wait()
     keep = lax.broadcasted_iota(jnp.int32, (TOKENS, PADDED_RANK), 1) < rank
-    low = jnp.where(keep, nt(x_ref[...], wd_ref[...]), 0.0).astype(BF16)
-    low_ref[...] = low
-    copies[5].wait()
-    copies[6].wait()
+    low = jnp.where(keep, low, 0.0).astype(BF16)
+    query = base_ref[...].astype(F32) + scale * nn(low, wu_ref[...])
+    rows_ref[:, HALF : 2 * HALF] = fold(query).astype(BF16)
+
+    def products(b):
+        h = b // GROUP
+        g = rows_ref[:, b * 128 : (b + 1) * 128]
+        q = rows_ref[:, HALF + b * 128 : HALF + (b + 1) * 128]
+        return (
+            own_scores(keys[:, h * 128 : (h + 1) * 128], q),
+            own_scores(values[:, h * 128 : (h + 1) * 128], g),
+        )
+
     lses, deltas = [], []
+    ready = products(0)
     for b in range(PAIRS):
-        h = b // GROUP
-        left, right = (
-            base_ref[:, m * 128 : (m + 1) * 128].astype(F32)
-            + scale * nn(low, wu_ref[:, m * 128 : (m + 1) * 128])
-            for m in (b, b + PAIRS)
-        )
-        q = fold(jnp.concatenate([left, right], axis=1)).astype(BF16)
-        rows_ref[:, b * 128 : (b + 1) * 128] = q
-        g = rows_ref[:, HALF + b * 128 : HALF + (b + 1) * 128]
-        scores = jnp.where(
-            mask, own_scores(keys[:, h * 128 : (h + 1) * 128], q) * INV_SQRT, masked_score
-        )
+        scores, dprob = ready
+        if b + 1 < PAIRS:
+            ready = products(b + 1)
+        scores = jnp.where(mask, scores * INV_SQRT, masked_score)
         top = jnp.max(scores, axis=0, keepdims=True)
         weight = jnp.exp(scores - top)
         total = jnp.sum(weight, axis=0, keepdims=True)
-        dprob = own_scores(values[:, h * 128 : (h + 1) * 128], g)
         lses.append(top + jnp.log(total))
         deltas.append(jnp.sum(weight * dprob, axis=0, keepdims=True) / total)
-    rows_ref[:, 2 * HALF :] = pack_stats(lses + deltas)
-    sends = [
-        pltpu.make_async_copy(
-            rows_ref.at[pl.ds(s * 16, 16)], send_hbm.at[route_ref[0, 0, s]], sems.at[7 + s]
-        )
-        for s in range(SLOTS)
-    ]
-    for copy in sends:
+    none = jnp.zeros((TOKENS, PADDED_RANK), F32)
+    low_rows = fold(jnp.concatenate([none, low.astype(F32), none, none], axis=1))
+    rows_ref[:, 2 * HALF :] = (pack_stats(lses + deltas) + low_rows).astype(BF16)
+    late = sends(HALF, SEND_WIDTH - HALF, rest + 5 + SLOTS)
+    for copy in late:
         copy.start()
-    for copy in sends:
+    for copy in early + late:
         copy.wait()
 
 
@@ -180,17 +204,26 @@
     def apart(rows):
         return jnp.concatenate([rows * lower, rows * upper], axis=1)
 
+    sides = [(beside(k_ref, h), beside(v_ref, h)) for h in range(2)]
+
+    def products(b):
+        g = apart(rows_ref[:, b * 128 : (b + 1) * 128])
+        q = apart(rows_ref[:, HALF + b * 128 : HALF + (b + 1) * 128])
+        keys, values = sides[b // GROUP]
+        return q, g, nt(keys, q), nt(values, g)
+
     lses, deltas = [], []
+    ready = products(0)
     for h in range(2):
-        keys, values = beside(k_ref, h), beside(v_ref, h)
+        keys = sides[h][0]
         dk = jnp.zeros((PLEN, 2 * HEAD_SIZE), F32)
         dv = jnp.zeros((PLEN, 2 * HEAD_SIZE), F32)
         for b in range(h * GROUP, (h + 1) * GROUP):
-            q = apart(rows_ref[:, b * 128 : (b + 1) * 128])
-            g = apart(rows_ref[:, HALF + b * 128 : HALF + (b + 1) * 128])
+            q, g, scores, dprob = ready
+            if b + 1 < PAIRS:
+                ready = products(b + 1)
             own_lse, own_delta = stats[b : b + 1], stats[PAIRS + b : PAIRS + b + 1]
-            scores = nt(keys, q) * INV_SQRT
-            dprob = nt(values, g)
+            scores = scores * INV_SQRT
             top = jnp.max(scores, axis=0, keepdims=True)
             weight = jnp.exp(scores - top)
             prompt_lse = top + jnp.log(jnp.sum(weight, axis=0, keepdims=True))
@@ -212,46 +245,91 @@
         for at, m in ((0, h), (HEAD_SIZE, h + 2)):
             dk_ref[:, m * 128 : (m + 1) * 128] = (dk[:, at : at + HEAD_SIZE] * INV_SQRT).astype(BF16)
             dv_ref[:, m * 128 : (m + 1) * 128] = dv[:, at : at + HEAD_SIZE].astype(BF16)
-    back_ref[:, HALF:] = pack_stats(lses + deltas)
+    back_ref[:, HALF:] = pack_stats(lses + deltas).astype(BF16)
 
 
 def finish_kernel(
-    rank_ref, route_ref, core_ref, x_ref, sk_ref, sv_ref, wu_ref, low_ref, send_ref, back_ref,
-    dq_ref, dsk_ref, dsv_ref, mine_ref, other_ref, rows_ref, dq_rows_ref,
+    route_hbm, rank_hbm, core_hbm, sk_hbm, sv_hbm, wu_hbm, x_hbm, send_hbm, back_hbm,
+    dq_hbm, dsk_hbm, dsv_hbm, mine_ref, other_ref,
+    route_ref, rank_ref, core_ref, sk_ref, sv_ref, wu_ref, x_ref, rows_ref, dq_rows_ref,
+    dq_ref, dsk_ref, dsv_ref, sems,
 ):
+    pairs = [
+        (route_hbm, route_ref), (rank_hbm, rank_ref), (core_hbm, core_ref), (sk_hbm, sk_ref),
+        (sv_hbm, sv_ref), (wu_hbm, wu_ref), (x_hbm, x_ref),
+    ]
+    loads = [
+        pltpu.make_async_copy(source, target, sems.at[i])
+        for i, (source, target) in enumerate(pairs)
+    ]
+    for copy in loads[:6]:
+        copy.start()
+    loads[0].wait()
+    blocks = []
+    for s in range(SLOTS):
+        owner, at = route_ref[0, 0, s], pl.ds(s * 16, 16)
+        blocks += [
+            pltpu.make_async_copy(send_hbm.at[owner], rows_ref.at[at], sems.at[7 + 2 * s]),
+            pltpu.make_async_copy(back_hbm.at[owner], dq_rows_ref.at[at], sems.at[8 + 2 * s]),
+        ]
+    for copy in blocks:
+        copy.start()
+    loads[6].start()
+    for copy in loads[1:6]:
+        copy.wait()
     rank = rank_ref[0]
     scale = adapter_strength / rank.astype(F32)
-    for s in range(SLOTS):
-        owner = route_ref[0, 0, s]
-        rows_ref[s * 16 : (s + 1) * 16, :] = send_ref[owner]
-        dq_rows_ref[s * 16 : (s + 1) * 16, :] = back_ref[owner]
+    mask = own_mask()
     keys = fold(sk_ref[...].astype(F32)).astype(BF16)
     values = fold(sv_ref[...].astype(F32)).astype(BF16)
+    for copy in blocks:
+        copy.wait()
     stats = unpack_stats(dq_rows_ref[:, HALF:], 2 * PAIRS)
-    mask = own_mask()
+
+    def products(b):
+        h = b // GROUP
+        g = rows_ref[:, b * 128 : (b + 1) * 128]
+        q = rows_ref[:, HALF + b * 128 : HALF + (b + 1) * 128]
+        return (
+            q, g,
+            own_scores(keys[:, h * 128 : (h + 1) * 128], q),
+            own_scores(values[:, h * 128 : (h + 1) * 128], g),
+        )
+
+    ready = products(0)
     for h in range(2):
-        k2, v2 = keys[:, h * 128 : (h + 1) * 128], values[:, h * 128 : (h + 1) * 128]
+        k2 = keys[:, h * 128 : (h + 1) * 128]
         dsk = jnp.zeros((ROWS, HEAD_SIZE), F32)
         dsv = jnp.zeros((ROWS, HEAD_SIZE), F32)
         for b in range(h * GROUP, (h + 1) * GROUP):
-            q = rows_ref[:, b * 128 : (b + 1) * 128]
-            g = rows_ref[:, HALF + b * 128 : HALF + (b + 1) * 128]
+            q, g, scores, dprob = ready
+            if b + 1 < PAIRS:
+                ready = products(b + 1)
             lse, delta = stats[b : b + 1], stats[PAIRS + b : PAIRS + b + 1]
-            probs = jnp.exp(jnp.where(mask, own_scores(k2, q) * INV_SQRT - lse, masked_score))
-            dscore = (probs * (own_scores(v2, g) - delta)).astype(BF16)
+            probs = jnp.exp(jnp.where(mask, scores * INV_SQRT - lse, masked_score))
+            dscore = (probs * (dprob - delta)).astype(BF16)
             dsv = dsv + own_product(probs.astype(BF16), g, nn)
             dsk = dsk + own_product(dscore, q, nn)
             dq = dq_rows_ref[:, b * 128 : (b + 1) * 128].astype(F32)
             dq = dq + own_product(dscore, k2, tn) * INV_SQRT
             for at, part in zip((b, b + PAIRS), unfold(dq)):
-                dq_ref[0, :, at * 128 : (at + 1) * 128] = part.astype(BF16)
+                dq_ref[:, at * 128 : (at + 1) * 128] = part.astype(BF16)
         for at, k_part, v_part in zip((h, h + 2), unfold(dsk * INV_SQRT), unfold(dsv)):
-            dsk_ref[0, :, at * 128 : (at + 1) * 128] = k_part.astype(BF16)
-            dsv_ref[0, :, at * 128 : (at + 1) * 128] = v_part.astype(BF16)
-    dq = dq_ref[0]
+            dsk_ref[:, at * 128 : (at + 1) * 128] = k_part.astype(BF16)
+            dsv_ref[:, at * 128 : (at + 1) * 128] = v_part.astype(BF16)
+    stores = [
+        pltpu.make_async_copy(source, target.at[0], sems.at[7 + 2 * SLOTS + i])
+        for i, (source, target) in enumerate(
+            [(dq_ref, dq_hbm), (dsk_ref, dsk_hbm), (dsv_ref, dsv_hbm)]
+        )
+    ]
+    for copy in stores:
+        copy.start()
+    dq = dq_ref[...]
     keep = lax.broadcasted_iota(jnp.int32, (TOKENS, PADDED_RANK), 1) < rank
     lifted = jnp.where(keep, scale * nt(dq, wu_ref[...]), 0.0).astype(BF16)
-    low = low_ref[...]
+    low = unfold(rows_ref[:, 2 * HALF :].astype(F32))[0][:, PADDED_RANK:].astype(BF16)
+    loads[6].wait()
 
     def block(c):
         if c < DOWN_BLOCKS:
@@ -267,6 +345,8 @@
         at = slice(c * PADDED_RANK, (c + 1) * PADDED_RANK)
         mine_ref[at, :] = jnp.where(first, lower, upper).astype(BF16)
         other_ref[at, :] = jnp.where(first, upper, lower).astype(BF16)
+    for copy in stores:
+        copy.wait()
 
 
 def spread_kernel(core_ref, mine_ref, other_ref, down_ref, up_ref):
@@ -297,6 +377,69 @@
         scratch_shapes=list(scratch),
         compiler_params=pltpu.CompilerParams(vmem_limit_bytes=vmem_mib * 1024 * 1024),
     )
+
+
+def like(arrays):
+    return [
+        (pltpu.SMEM if a.dtype == jnp.int32 else pltpu.VMEM)(a.shape, a.dtype) for a in arrays
+    ]
+
+
+def run_prepare(*arrays):
+    return call(
+        prepare_kernel,
+        [HBM] * len(arrays),
+        [((SLOTS, 16, SEND_WIDTH), BF16)],
+        like(arrays)
+        + [
+            pltpu.VMEM((ROWS, SEND_WIDTH), BF16),
+            pltpu.SemaphoreType.DMA((9 + X_PARTS + 2 * SLOTS,)),
+        ],
+        [HBM],
+        60,
+    )(*arrays)[0]
+
+
+def run_owner(rows, keys, values):
+    return call(
+        owner_kernel,
+        [VMEM] * 3,
+        [((ROWS, BACK_WIDTH), BF16)] + [((PLEN, KEY_VALUE_HEADS * HEAD_SIZE), BF16)] * 2,
+    )(rows, keys, values)
+
+
+def run_finish(*arrays):
+    kv_width = KEY_VALUE_HEADS * HEAD_SIZE
+    return call(
+        finish_kernel,
+        [HBM] * len(arrays),
+        [
+            ((1, TOKENS, QUERY_WIDTH), BF16),
+            ((1, TOKENS, kv_width), BF16),
+            ((1, TOKENS, kv_width), BF16),
+            ((CORE_ROWS, 128), BF16),
+            ((CORE_ROWS, 128), BF16),
+        ],
+        like(arrays[:7])
+        + [
+            pltpu.VMEM((ROWS, SEND_WIDTH), BF16),
+            pltpu.VMEM((ROWS, BACK_WIDTH), BF16),
+            pltpu.VMEM((TOKENS, QUERY_WIDTH), BF16),
+            pltpu.VMEM((TOKENS, kv_width), BF16),
+            pltpu.VMEM((TOKENS, kv_width), BF16),
+            pltpu.SemaphoreType.DMA((10 + 2 * SLOTS,)),
+        ],
+        [HBM] * 3 + [VMEM] * 2,
+        60,
+    )(*arrays)
+
+
+def run_spread(core, mine, other):
+    return call(
+        spread_kernel,
+        [SMEM] + [VMEM] * 2,
+        [((PADDED_RANK, MODEL_WIDTH), F32), ((PADDED_RANK, QUERY_WIDTH), F32)],
+    )(core, mine, other)
 
 
 def by_core(part):
@@ -342,44 +485,20 @@
 ):
     hidden = normed_hidden_input[0]
     keys, values = completion_keys[0], completion_values[0]
-    arrays = (
-        hidden, frozen_query_base[0], attention_output_grad[0], keys, values,
-        adapter_down_weight.T, adapter_up_weight,
-    )
-    low, send = call(
-        prepare_kernel,
-        [SMEM] * 3 + [HBM] * 7,
-        [((TOKENS, PADDED_RANK), BF16), ((SLOTS, 16, SEND_WIDTH), BF16)],
-        [pltpu.VMEM(a.shape, BF16) for a in arrays]
-        + [pltpu.VMEM((ROWS, SEND_WIDTH), BF16), pltpu.SemaphoreType.DMA((7 + SLOTS,))],
-        [VMEM, HBM],
-        60,
-    )(adapter_rank, route, lengths, *arrays)
+    send = run_prepare(
+        adapter_rank, route, lengths, hidden, frozen_query_base[0], attention_output_grad[0],
+        keys, values, adapter_down_weight.T, adapter_up_weight,
+    )
     arrived = lax.all_to_all(send, "prompt", 0, 0, tiled=True)
-    back, dk, dv = call(
-        owner_kernel,
-        [VMEM] * 3,
-        [((ROWS, BACK_WIDTH), BF16)] + [((PLEN, KEY_VALUE_HEADS * HEAD_SIZE), BF16)] * 2,
-    )(arrived.reshape(ROWS, SEND_WIDTH), owner_prompt_keys[0], owner_prompt_values[0])
+    back, dk, dv = run_owner(
+        arrived.reshape(ROWS, SEND_WIDTH), owner_prompt_keys[0], owner_prompt_values[0]
+    )
     back = lax.all_to_all(back.reshape(SLOTS, 16, BACK_WIDTH), "prompt", 0, 0, tiled=True)
     core = (lax.axis_index("comp") % 2).astype(jnp.int32)[None]
-    dq, dsk, dsv, mine, other = call(
-        finish_kernel,
-        [SMEM] * 3 + [VMEM] * 7,
-        [
-            ((1, TOKENS, QUERY_WIDTH), BF16),
-            ((1, TOKENS, KEY_VALUE_HEADS * HEAD_SIZE), BF16),
-            ((1, TOKENS, KEY_VALUE_HEADS * HEAD_SIZE), BF16),
-            ((CORE_ROWS, 128), BF16),
-            ((CORE_ROWS, 128), BF16),
-        ],
-        [pltpu.VMEM((ROWS, SEND_WIDTH), BF16), pltpu.VMEM((ROWS, BACK_WIDTH), BF16)],
-    )(adapter_rank, route, core, hidden, keys, values, adapter_up_weight, low, send, back)
-    down, up = call(
-        spread_kernel,
-        [SMEM] + [VMEM] * 2,
-        [((PADDED_RANK, MODEL_WIDTH), F32), ((PADDED_RANK, QUERY_WIDTH), F32)],
-    )(core, *sum_all(mine, other))
+    dq, dsk, dsv, mine, other = run_finish(
+        route, adapter_rank, core, keys, values, adapter_up_weight, hidden, send, back
+    )
+    down, up = run_spread(core, *sum_all(mine, other))
     return dq, dsk, dsv, dk[None], dv[None], down.T, up
 
 

time: 146 us -> 142 us (0.973)
  local copies, waits for them, and re-layouts: 3.63 us -> 0.98 us
  Pallas kernels: 18.9 us -> 16.3 us
  waiting for transfers between devices: 29.9 us -> 31.8 us
    unnamed x20 -> x6, local copies, waits for them, and re-layouts: 3.52 us -> 0.87 us
    pallas_call x4, Pallas kernels: 18.9 us -> 16.3 us  [the longest x1 6.61 us: run_finish(): call(finish_kernel, [HBM] * len(arrays), [((1, TOKENS, QUERY_WIDTH), BF16...]
where the time goes in v5:
time: 142 us
  blocking collectives  75.4 us (53%)
  waiting for transfers between devices  31.8 us (22%)
  Pallas kernels  16.3 us (11%)
  starting transfers between devices  14.4 us (10%)
    all_to_all x1, blocking collectives, per_device(): arrived = lax.all_to_all(send, 'prompt', 0, 0, tiled=True)  46.6 us
    all_to_all x1, waiting for transfers between devices, per_device(): lax.all_to_all(back.reshape(SLOTS, 16, BACK_WIDTH), 'prompt', 0, 0, tiled...  20.4 us
    all_to_all x1, blocking collectives, sum_all(): total = jnp.sum(swap(pair.reshape(32, rows, 128)).astype(F32), axis=0)  15.7 us
    all_to_all x1, blocking collectives, sum_all(): swap(jnp.broadcast_to(total[None], (32, rows, 128))).reshape(CORE_ROWS, 128)  13.1 us
    ppermute x2, starting transfers between devices, by_core(): return lax.ppermute(part, 'comp', [(i, i ^ 1) for i in range(16)])  8.59 us
    ppermute x2, waiting for transfers between devices, sum_all(): lax.ppermute(total, 'prompt', [(i, flip(i)) for i in range(16)])  8.14 us
    pallas_call x1, Pallas kernels, run_finish(): call(finish_kernel, [HBM] * len(arrays), [((1, TOKENS, QUERY_WIDTH), BF16...  6.61 us
    pallas_call x1, Pallas kernels, run_prepare(): call(prepare_kernel, [HBM] * len(arrays), [((SLOTS, 16, SEND_WIDTH), BF16...  5.18 us
  transfers between devices with their start and end apart: 5, of which 5 were waited for; matrix products, arithmetic and copies ran while one was open for 0% of the time, Pallas kernels for 0%

profile of v5, /device:TPU:1, one launch (start us, length us, event | category | flops | bytes accessed | tf_op | source)
XLA Modules:
  0.0 141.6 jit_solution(15783945397361707227)
XLA Ops:
  1.3 5.2 %shard_map.171.send_hbm = bf16[16,16,2688]{2,1,0:T(8,128)(2,1)} custom-call(s32[1]{0:T(128)S(6)} %copy.19.rank_hbm, s32[1,1,16]{2,1,0:T(1,128)} %route_hbm.3, s32[1,1,16]{2,1,0:T(1,128)} %length_hbm.1, bf16[128,5120]{1,0:T(8,128)(2,1)} %bitcast.21, bf16[128,2560]{1,0:T(8,128)(2,1)} %bitcast.24, bf16[128,2560]{1,0:T(8,128)(2,1)} %bitcast.25, ...), custom_call_target="tpu_custom_call" | custom-call | tf_op jit(solution)/shard_map/pallas_call | solution.py:389
  6.5 0.0 copy-start
  6.5 0.0 copy-start.1
  6.5 46.6 %all_to_all.20 = bf16[16,16,2688]{2,1,0:T(8,128)(2,1)S(1)} all-to-all(bf16[16,16,2688]{2,1,0:T(8,128)(2,1)} %shard_map.171.send_hbm), channel_id=1, replica_groups=mesh['prompt'=16,'comp'=16] {'prompt'}, dimensions={0} | all-to-all | bytes 2752512 | tf_op jit(solution)/shard_map/all_to_all | solution.py:492
  53.1 0.0 copy-done.1
  53.1 3.1 %shard_map.172 = (bf16[256,1408]{1,0:T(8,128)(2,1)}, bf16[128,512]{1,0:T(8,128)(2,1)}, bf16[128,512]{1,0:T(8,128)(2,1)}) custom-call(bf16[256,2688]{1,0:T(8,128)(2,1)S(1)} %bitcast.16, bf16[128,512]{1,0:T(8,128)(2,1)S(1)} %bitcast.19, bf16[128,512]{1,0:T(8,128)(2,1)S(1)} %bitcast.20), custom_call_target="tpu_custom_call" | custom-call | tf_op jit(solution)/shard_map/pallas_call | solution.py:404
  56.2 5.0 %all-to-all-start.1 = ((bf16[16,16,1408]{2,1,0:T(8,128)(2,1)}), bf16[16,16,1408]{2,1,0:T(8,128)(2,1)S(1)}, u32[]{:S(2)}, u32[]{:S(2)}) async-start(bf16[16,16,1408]{2,1,0:T(8,128)(2,1)} %bitcast.10), calls=%async_computation.1 | async-start | bytes 1441792 | tf_op jit(solution)/shard_map/all_to_all | solution.py:496
  61.2 20.4 %all-to-all-done.1.back_hbm = bf16[16,16,1408]{2,1,0:T(8,128)(2,1)S(1)} async-done(((bf16[16,16,1408]{2,1,0:T(8,128)(2,1)}), bf16[16,16,1408]{2,1,0:T(8,128)(2,1)S(1)}, u32[]{:S(2)}, u32[]{:S(2)}) %all-to-all-start.1) | async-done | bytes 720928 | tf_op jit(solution)/shard_map/all_to_all | solution.py:496
  81.6 0.9 copy-done.2
  82.5 6.6 %shard_map.173 = (bf16[1,128,2560]{2,1,0:T(8,128)(2,1)}, bf16[1,128,512]{2,1,0:T(8,128)(2,1)}, bf16[1,128,512]{2,1,0:T(8,128)(2,1)}, bf16[2048,128]{1,0:T(8,128)(2,1)}, bf16[2048,128]{1,0:T(8,128)(2,1)}) custom-call(s32[1,1,16]{2,1,0:T(1,128)} %route_hbm.3, s32[1]{0:T(128)S(6)} %copy.19.rank_hbm, s32[1]{0:T(128)} %bitcast.core_hbm.core_ref, ...), custom_call_target="tpu_custom_call" | custom-call | tf_op jit(solution)/shard_map/pallas_call | solution.py:413
  89.1 3.4 %collective-permute-start = (bf16[2048,128]{1,0:T(8,128)(2,1)}, bf16[2048,128]{1,0:T(8,128)(2,1)S(1)}, u32[]{:S(2)}, u32[]{:S(2)}) collective-permute-start(bf16[2048,128]{1,0:T(8,128)(2,1)} %get-tuple-element.24), channel_id=1, source_target_pairs={{0,1},{1,0},{2,3},{3,2},{4,5},{5,4},{6,7},{7,6},{8,9},{9,8},{10,11... | collective-permute-start | bytes 1572872 | tf_op jit(solution)/shard_map/ppermute | solution.py:446
  92.5 1.7 %collective-permute-done = bf16[2048,128]{1,0:T(8,128)(2,1)S(1)} collective-permute-done((bf16[2048,128]{1,0:T(8,128)(2,1)}, bf16[2048,128]{1,0:T(8,128)(2,1)S(1)}, u32[]{:S(2)}, u32[]{:S(2)}) %collective-permute-start) | collective-permute-done | bytes 524320 | tf_op jit(solution)/shard_map/ppermute | solution.py:446
  94.2 1.2 add_convert_fusion
  95.4 15.7 %all_to_all.21 = bf16[32,64,128]{2,1,0:T(8,128)(2,1)S(1)} all-to-all(bf16[32,64,128]{2,1,0:T(8,128)(2,1)S(1)} %bitcast.23), channel_id=1, replica_groups={{0,2,4,6,8,10,12,14,64,66,68,70,72,74,76,78,128,130,132,134,136,138,140..., dimensions={0} | all-to-all | bytes 1048576 | tf_op jit(solution)/shard_map/all_to_all | solution.py:464
  111.1 0.1 convert_reduce_fusion
  111.2 0.2 collective-permute-start.1
  111.4 3.9 %collective-permute-done.1 = f32[64,128]{1,0:T(8,128)S(1)} collective-permute-done((f32[64,128]{1,0:T(8,128)S(1)}, f32[64,128]{1,0:T(8,128)S(1)}, u32[]{:S(2)}, u32[]{:S(2)}) %collective-permute-start.1) | collective-permute-done | bytes 32800 | tf_op jit(solution)/shard_map/ppermute | solution.py:466
  115.3 0.7 collective-permute-start.2
  115.9 4.2 %collective-permute-done.2 = f32[64,128]{1,0:T(8,128)S(1)} collective-permute-done((f32[64,128]{1,0:T(8,128)S(1)}, f32[64,128]{1,0:T(8,128)S(1)}, u32[]{:S(2)}, u32[]{:S(2)}) %collective-permute-start.2) | collective-permute-done | bytes 32800 | tf_op jit(solution)/shard_map/ppermute | solution.py:466
  120.2 0.1 broadcast_in_dim.18
  120.3 13.1 %all_to_all.22 = bf16[32,64,128]{2,1,0:T(8,128)(2,1)S(1)} all-to-all(bf16[32,64,128]{2,1,0:T(8,128)(2,1)S(1)} %broadcast_in_dim.18), channel_id=1, replica_groups={{0,2,4,6,8,10,12,14,64,66,68,70,72,74,76,78,128,130,132,134,136,138,140..., dimensions={0} | all-to-all | bytes 1048576 | tf_op jit(solution)/shard_map/all_to_all | solution.py:468
  133.4 5.2 %collective-permute-start.3 = (bf16[2048,128]{1,0:T(8,128)(2,1)S(1)}, bf16[2048,128]{1,0:T(8,128)(2,1)S(1)}, u32[]{:S(2)}, u32[]{:S(2)}) collective-permute-start(bf16[2048,128]{1,0:T(8,128)(2,1)S(1)} %bitcast.17), channel_id=1, source_target_pairs={{0,1},{1,0},{2,3},{3,2},{4,5},{5,4},{6,7},{7,6},{8,9},{9,8},{10,11... | collective-permute-start | bytes 1572872 | tf_op jit(solution)/shard_map/ppermute | solution.py:446
  138.6 1.5 %collective-permute-done.3.other_ref = bf16[2048,128]{1,0:T(8,128)(2,1)S(1)} collective-permute-done((bf16[2048,128]{1,0:T(8,128)(2,1)S(1)}, bf16[2048,128]{1,0:T(8,128)(2,1)S(1)}, u32[]{:S(2)}, u32[]{:S(2)}) %collective-permute-start.3) | collective-permute-done | bytes 524320 | tf_op jit(solution)/shard_map/ppermute | solution.py:446
  140.1 1.4 shard_map.174
  (4 shorter events, 0.0 us)
Async XLA Ops:
  6.5 46.6 %copy-start = (bf16[1,128,512]{2,1,0:T(8,128)(2,1)S(1)}, bf16[1,128,512]{2,1,0:T(8,128)(2,1)}, u32[]{:S(2)}) copy-start(bf16[1,128,512]{2,1,0:T(8,128)(2,1)} %param.17) | copy-start | bytes 393220
  6.5 46.6 %copy-start.1 = (bf16[1,128,512]{2,1,0:T(8,128)(2,1)S(1)}, bf16[1,128,512]{2,1,0:T(8,128)(2,1)}, u32[]{:S(2)}) copy-start(bf16[1,128,512]{2,1,0:T(8,128)(2,1)} %param.18) | copy-start | bytes 393220
  56.2 25.4 %all-to-all-start.1 = ((bf16[16,16,1408]{2,1,0:T(8,128)(2,1)}), bf16[16,16,1408]{2,1,0:T(8,128)(2,1)S(1)}, u32[]{:S(2)}, u32[]{:S(2)}) async-start(bf16[16,16,1408]{2,1,0:T(8,128)(2,1)} %bitcast.10), calls=%async_computation.1 | async-start | bytes 1441792 | tf_op jit(solution)/shard_map/all_to_all | solution.py:496
  81.6 0.9 copy-start.2
  89.1 5.1 %collective-permute-start = (bf16[2048,128]{1,0:T(8,128)(2,1)}, bf16[2048,128]{1,0:T(8,128)(2,1)S(1)}, u32[]{:S(2)}, u32[]{:S(2)}) collective-permute-start(bf16[2048,128]{1,0:T(8,128)(2,1)} %get-tuple-element.24), channel_id=1, source_target_pairs={{0,1},{1,0},{2,3},{3,2},{4,5},{5,4},{6,7},{7,6},{8,9},{9,8},{10,11... | collective-permute-start | bytes 1572872 | tf_op jit(solution)/shard_map/ppermute | solution.py:446
  111.2 4.1 %collective-permute-start.1 = (f32[64,128]{1,0:T(8,128)S(1)}, f32[64,128]{1,0:T(8,128)S(1)}, u32[]{:S(2)}, u32[]{:S(2)}) collective-permute-start(f32[64,128]{1,0:T(8,128)S(1)} %convert_reduce_fusion), channel_id=1, source_target_pairs={{0,16},{16,0},{32,48},{48,32},{64,80},{80,64},{96,112},{112,96},{1... | collective-permute-start | bytes 98312 | tf_op jit(solution)/shard_map/ppermute | solution.py:466
  115.3 4.9 %collective-permute-start.2 = (f32[64,128]{1,0:T(8,128)S(1)}, f32[64,128]{1,0:T(8,128)S(1)}, u32[]{:S(2)}, u32[]{:S(2)}) collective-permute-start(f32[64,128]{1,0:T(8,128)S(1)} %add.15), channel_id=1, source_target_pairs={{0,48},{16,32},{32,16},{48,0},{64,112},{80,96},{96,80},{112,64},{1... | collective-permute-start | bytes 98312 | tf_op jit(solution)/shard_map/ppermute | solution.py:466
  133.4 6.8 %collective-permute-start.3 = (bf16[2048,128]{1,0:T(8,128)(2,1)S(1)}, bf16[2048,128]{1,0:T(8,128)(2,1)S(1)}, u32[]{:S(2)}, u32[]{:S(2)}) collective-permute-start(bf16[2048,128]{1,0:T(8,128)(2,1)S(1)} %bitcast.17), channel_id=1, source_target_pairs={{0,1},{1,0},{2,3},{3,2},{4,5},{5,4},{6,7},{7,6},{8,9},{9,8},{10,11... | collective-permute-start | bytes 1572872 | tf_op jit(solution)/shard_map/ppermute | solution.py:446

commit v6 on v5

--- a/solution.py
+++ b/solution.py
@@ -248,43 +248,52 @@
     back_ref[:, HALF:] = pack_stats(lses + deltas).astype(BF16)
 
 
-def finish_kernel(
-    route_hbm, rank_hbm, core_hbm, sk_hbm, sv_hbm, wu_hbm, x_hbm, send_hbm, back_hbm,
-    dq_hbm, dsk_hbm, dsv_hbm, mine_ref, other_ref,
-    route_ref, rank_ref, core_ref, sk_ref, sv_ref, wu_ref, x_ref, rows_ref, dq_rows_ref,
-    dq_ref, dsk_ref, dsv_ref, sems,
+def own_kernel(
+    rank_ref, route_ref, core_ref, sk_hbm, sv_hbm, send_hbm,
+    rows_ref, keys_ref, values_ref, order_ref, factors_ref,
+    sk_ref, sv_ref, sems,
 ):
-    pairs = [
-        (route_hbm, route_ref), (rank_hbm, rank_ref), (core_hbm, core_ref), (sk_hbm, sk_ref),
-        (sv_hbm, sv_ref), (wu_hbm, wu_ref), (x_hbm, x_ref),
+    pairs = [(sk_hbm, sk_ref), (sv_hbm, sv_ref)]
+    pairs += [
+        (send_hbm.at[route_ref[0, 0, s]], rows_ref.at[pl.ds(s * 16, 16)]) for s in range(SLOTS)
     ]
     loads = [
         pltpu.make_async_copy(source, target, sems.at[i])
         for i, (source, target) in enumerate(pairs)
     ]
-    for copy in loads[:6]:
+    for copy in loads:
         copy.start()
-    loads[0].wait()
-    blocks = []
-    for s in range(SLOTS):
-        owner, at = route_ref[0, 0, s], pl.ds(s * 16, 16)
-        blocks += [
-            pltpu.make_async_copy(send_hbm.at[owner], rows_ref.at[at], sems.at[7 + 2 * s]),
-            pltpu.make_async_copy(back_hbm.at[owner], dq_rows_ref.at[at], sems.at[8 + 2 * s]),
-        ]
-    for copy in blocks:
-        copy.start()
-    loads[6].start()
-    for copy in loads[1:6]:
-        copy.wait()
     rank = rank_ref[0]
     scale = adapter_strength / rank.astype(F32)
+    block = (PADDED_RANK, 128)
+    keep = lax.broadcasted_iota(jnp.int32, block, 1) < rank
+    factors_ref[0] = jnp.full(block, scale, F32)
+    factors_ref[1] = jnp.where(keep, scale, 0.0)
+    factors_ref[2] = jnp.full(block, 1.0, F32) * (core_ref[0] == 0).astype(F32)
+    lane = lax.broadcasted_iota(jnp.int32, (16, ROWS), 1)
+    place = lax.broadcasted_iota(jnp.int32, (16, ROWS), 0)
+    for s in range(SLOTS):
+        at = (lane == route_ref[0, 0, s] * 16 + place).astype(F32)
+        order_ref[s * 16 : (s + 1) * 16, :] = at.astype(BF16)
+    for copy in loads:
+        copy.wait()
+    keys_ref[...] = fold(sk_ref[...].astype(F32)).astype(BF16)
+    values_ref[...] = fold(sv_ref[...].astype(F32)).astype(BF16)
+
+
+def finish_kernel(
+    x_hbm, wu_hbm, rows_ref, keys_ref, values_ref, order_ref, factors_ref, back_ref,
+    dq_hbm, dsk_hbm, dsv_hbm, mine_ref, other_ref,
+    x_ref, wu_ref, dq_rows_ref, dq_ref, dsk_ref, dsv_ref, sems,
+):
+    loads = [
+        pltpu.make_async_copy(wu_hbm, wu_ref, sems.at[3]),
+        pltpu.make_async_copy(x_hbm, x_ref, sems.at[4]),
+    ]
+    for copy in loads:
+        copy.start()
+    order = order_ref[...]
     mask = own_mask()
-    keys = fold(sk_ref[...].astype(F32)).astype(BF16)
-    values = fold(sv_ref[...].astype(F32)).astype(BF16)
-    for copy in blocks:
-        copy.wait()
-    stats = unpack_stats(dq_rows_ref[:, HALF:], 2 * PAIRS)
 
     def products(b):
         h = b // GROUP
@@ -292,13 +301,15 @@
         q = rows_ref[:, HALF + b * 128 : HALF + (b + 1) * 128]
         return (
             q, g,
-            own_scores(keys[:, h * 128 : (h + 1) * 128], q),
-            own_scores(values[:, h * 128 : (h + 1) * 128], g),
+            own_scores(keys_ref[:, h * 128 : (h + 1) * 128], q),
+            own_scores(values_ref[:, h * 128 : (h + 1) * 128], g),
         )
 
     ready = products(0)
+    stats = unpack_stats(nn(order, back_ref[:, HALF:]), 2 * PAIRS)
+    dq_rows_ref[...] = nn(order, back_ref[:, :HALF])
     for h in range(2):
-        k2 = keys[:, h * 128 : (h + 1) * 128]
+        k2 = keys_ref[:, h * 128 : (h + 1) * 128]
         dsk = jnp.zeros((ROWS, HEAD_SIZE), F32)
         dsv = jnp.zeros((ROWS, HEAD_SIZE), F32)
         for b in range(h * GROUP, (h + 1) * GROUP):
@@ -308,17 +319,16 @@
             lse, delta = stats[b : b + 1], stats[PAIRS + b : PAIRS + b + 1]
             probs = jnp.exp(jnp.where(mask, scores * INV_SQRT - lse, masked_score))
             dscore = (probs * (dprob - delta)).astype(BF16)
+            dq = dq_rows_ref[:, b * 128 : (b + 1) * 128] + own_product(dscore, k2, tn) * INV_SQRT
+            for at, part in zip((b, b + PAIRS), unfold(dq)):
+                dq_ref[:, at * 128 : (at + 1) * 128] = part.astype(BF16)
             dsv = dsv + own_product(probs.astype(BF16), g, nn)
             dsk = dsk + own_product(dscore, q, nn)
-            dq = dq_rows_ref[:, b * 128 : (b + 1) * 128].astype(F32)
-            dq = dq + own_product(dscore, k2, tn) * INV_SQRT
-            for at, part in zip((b, b + PAIRS), unfold(dq)):
-                dq_ref[:, at * 128 : (at + 1) * 128] = part.astype(BF16)
         for at, k_part, v_part in zip((h, h + 2), unfold(dsk * INV_SQRT), unfold(dsv)):
             dsk_ref[:, at * 128 : (at + 1) * 128] = k_part.astype(BF16)
             dsv_ref[:, at * 128 : (at + 1) * 128] = v_part.astype(BF16)
     stores = [
-        pltpu.make_async_copy(source, target.at[0], sems.at[7 + 2 * SLOTS + i])
+        pltpu.make_async_copy(source, target.at[0], sems.at[i])
         for i, (source, target) in enumerate(
             [(dq_ref, dq_hbm), (dsk_ref, dsk_hbm), (dsv_ref, dsv_hbm)]
         )
@@ -326,10 +336,11 @@
     for copy in stores:
         copy.start()
     dq = dq_ref[...]
-    keep = lax.broadcasted_iota(jnp.int32, (TOKENS, PADDED_RANK), 1) < rank
-    lifted = jnp.where(keep, scale * nt(dq, wu_ref[...]), 0.0).astype(BF16)
+    for copy in loads:
+        copy.wait()
+    lifted = (nt(dq, wu_ref[...]) * factors_ref[1, :1, :PADDED_RANK]).astype(BF16)
     low = unfold(rows_ref[:, 2 * HALF :].astype(F32))[0][:, PADDED_RANK:].astype(BF16)
-    loads[6].wait()
+    scale, first = factors_ref[0], factors_ref[2] > 0.5
 
     def block(c):
         if c < DOWN_BLOCKS:
@@ -339,7 +350,6 @@
             return scale * tn(low, dq[:, at : at + 128])
         return jnp.zeros((PADDED_RANK, 128), F32)
 
-    first = core_ref[0] == 0
     for c in range(CORE_BLOCKS):
         lower, upper = block(c), block(c + CORE_BLOCKS)
         at = slice(c * PADDED_RANK, (c + 1) * PADDED_RANK)
@@ -349,8 +359,8 @@
         copy.wait()
 
 
-def spread_kernel(core_ref, mine_ref, other_ref, down_ref, up_ref):
-    first = core_ref[0] == 0
+def spread_kernel(factors_ref, mine_ref, other_ref, down_ref, up_ref):
+    first = factors_ref[2] > 0.5
     for c in range(GRAD_BLOCKS):
         at = c % CORE_BLOCKS * PADDED_RANK
         mine = mine_ref[at : at + PADDED_RANK, :].astype(F32)
@@ -408,11 +418,30 @@
     )(rows, keys, values)
 
 
-def run_finish(*arrays):
+def run_own(rank, route, core, *arrays):
+    return call(
+        own_kernel,
+        [SMEM] * 3 + [HBM] * len(arrays),
+        [
+            ((ROWS, SEND_WIDTH), BF16),
+            ((ROWS, KV_HALF), BF16),
+            ((ROWS, KV_HALF), BF16),
+            ((ROWS, ROWS), BF16),
+            ((3, PADDED_RANK, 128), F32),
+        ],
+        like(arrays[:2]) + [pltpu.SemaphoreType.DMA((2 + SLOTS,))],
+    )(rank, route, core, *in_hbm(arrays))
+
+
+def in_hbm(arrays):
+    return [pltpu.with_memory_space_constraint(a, pltpu.HBM) for a in arrays]
+
+
+def run_finish(x, wu, *arrays):
     kv_width = KEY_VALUE_HEADS * HEAD_SIZE
     return call(
         finish_kernel,
-        [HBM] * len(arrays),
+        [HBM] * 2 + [VMEM] * len(arrays),
         [
             ((1, TOKENS, QUERY_WIDTH), BF16),
             ((1, TOKENS, kv_width), BF16),
@@ -420,26 +449,24 @@
             ((CORE_ROWS, 128), BF16),
             ((CORE_ROWS, 128), BF16),
         ],
-        like(arrays[:7])
+        like([x, wu])
         + [
-            pltpu.VMEM((ROWS, SEND_WIDTH), BF16),
-            pltpu.VMEM((ROWS, BACK_WIDTH), BF16),
+            pltpu.VMEM((ROWS, HALF), F32),
             pltpu.VMEM((TOKENS, QUERY_WIDTH), BF16),
             pltpu.VMEM((TOKENS, kv_width), BF16),
             pltpu.VMEM((TOKENS, kv_width), BF16),
-            pltpu.SemaphoreType.DMA((10 + 2 * SLOTS,)),
+            pltpu.SemaphoreType.DMA((5,)),
         ],
         [HBM] * 3 + [VMEM] * 2,
-        60,
-    )(*arrays)
-
-
-def run_spread(core, mine, other):
+    )(*in_hbm([x, wu]), *arrays)
+
+
+def run_spread(*arrays):
     return call(
         spread_kernel,
-        [SMEM] + [VMEM] * 2,
+        [VMEM] * len(arrays),
         [((PADDED_RANK, MODEL_WIDTH), F32), ((PADDED_RANK, QUERY_WIDTH), F32)],
-    )(core, mine, other)
+    )(*arrays)
 
 
 def by_core(part):
@@ -495,10 +522,11 @@
     )
     back = lax.all_to_all(back.reshape(SLOTS, 16, BACK_WIDTH), "prompt", 0, 0, tiled=True)
     core = (lax.axis_index("comp") % 2).astype(jnp.int32)[None]
+    own = run_own(adapter_rank, route, core, keys, values, send)
     dq, dsk, dsv, mine, other = run_finish(
-        route, adapter_rank, core, keys, values, adapter_up_weight, hidden, send, back
-    )
-    down, up = run_spread(core, *sum_all(mine, other))
+        hidden, adapter_up_weight, *own, back.reshape(ROWS, BACK_WIDTH)
+    )
+    down, up = run_spread(own[-1], *sum_all(mine, other))
     return dq, dsk, dsv, dk[None], dv[None], down.T, up
 
 

time: 142 us -> 138 us (0.972)
  waiting for transfers between devices: 31.8 us -> 28.3 us
    all_to_all x1, waiting for transfers between devices: 20.4 us -> 17.1 us  [per_device(): lax.all_to_all(back.reshape(SLOTS, 16, BACK_WIDTH), 'prompt', 0, 0, tiled...]
    pallas_call x2 -> x3, Pallas kernels: 8.03 us -> 8.4 us  [the longest x1 4.8 us: run_finish(): call(finish_kernel, [HBM] * 2 + [VMEM] * len(arrays), [((1, TOKENS, QUERY...]
  transfers between devices with their start and end apart: 5 -> 5, of which waited for: 5 -> 5; matrix products, arithmetic and copies ran while one was open for 0% -> 0% of each run, Pallas kernels for 0% -> 2%
where the time goes in v6:
time: 138 us
  blocking collectives  75.6 us (55%)
  waiting for transfers between devices  28.3 us (21%)
  Pallas kernels  16.8 us (12%)
  starting transfers between devices  15.3 us (11%)
    all_to_all x1, blocking collectives, per_device(): arrived = lax.all_to_all(send, 'prompt', 0, 0, tiled=True)  46.2 us
    all_to_all x1, waiting for transfers between devices, per_device(): lax.all_to_all(back.reshape(SLOTS, 16, BACK_WIDTH), 'prompt', 0, 0, tiled...  17.1 us
    all_to_all x1, blocking collectives, sum_all(): total = jnp.sum(swap(pair.reshape(32, rows, 128)).astype(F32), axis=0)  16.3 us
    all_to_all x1, blocking collectives, sum_all(): swap(jnp.broadcast_to(total[None], (32, rows, 128))).reshape(CORE_ROWS, 128)  13.1 us
    ppermute x2, starting transfers between devices, by_core(): return lax.ppermute(part, 'comp', [(i, i ^ 1) for i in range(16)])  9.13 us
    ppermute x2, waiting for transfers between devices, sum_all(): lax.ppermute(total, 'prompt', [(i, flip(i)) for i in range(16)])  8.08 us
    all_to_all x1, starting transfers between devices, per_device(): lax.all_to_all(back.reshape(SLOTS, 16, BACK_WIDTH), 'prompt', 0, 0, tiled...  5.24 us
    pallas_call x1, Pallas kernels, run_prepare(): call(prepare_kernel, [HBM] * len(arrays), [((SLOTS, 16, SEND_WIDTH), BF16...  5.23 us
  transfers between devices with their start and end apart: 5, of which 5 were waited for; matrix products, arithmetic and copies ran while one was open for 0% of the time, Pallas kernels for 2%

profile of v6, /device:TPU:1, one launch (start us, length us, event | category | flops | bytes accessed | tf_op | source)
XLA Modules:
  0.0 137.7 jit_solution(5805008326921014455)
XLA Ops:
  1.3 5.2 %shard_map.171.send_hbm = bf16[16,16,2688]{2,1,0:T(8,128)(2,1)} custom-call(s32[1]{0:T(128)S(6)} %copy.19.rank_hbm.rank_ref, s32[1,1,16]{2,1,0:T(1,128)} %route_ref.1, s32[1,1,16]{2,1,0:T(1,128)} %length_hbm.1, bf16[128,5120]{1,0:T(8,128)(2,1)} %bitcast.23, bf16[128,2560]{1,0:T(8,128)(2,1)} %bitcast.26, bf16[128,2560]{1,0:T(8,128)(2,1)} %bitcast.27, ...), custom_call_target="tpu_custom_call" | custom-call | tf_op jit(solution)/shard_map/pallas_call | solution.py:399
  6.5 0.0 copy-start
  6.5 0.0 copy-start.1
  6.5 46.2 %all_to_all.20 = bf16[16,16,2688]{2,1,0:T(8,128)(2,1)S(1)} all-to-all(bf16[16,16,2688]{2,1,0:T(8,128)(2,1)} %shard_map.171.send_hbm), channel_id=1, replica_groups=mesh['prompt'=16,'comp'=16] {'prompt'}, dimensions={0} | all-to-all | bytes 2752512 | tf_op jit(solution)/shard_map/all_to_all | solution.py:519
  52.8 3.1 %shard_map.173 = (bf16[256,1408]{1,0:T(8,128)(2,1)}, bf16[128,512]{1,0:T(8,128)(2,1)}, bf16[128,512]{1,0:T(8,128)(2,1)}) custom-call(bf16[256,2688]{1,0:T(8,128)(2,1)S(1)} %bitcast.17, bf16[128,512]{1,0:T(8,128)(2,1)S(1)} %bitcast.21, bf16[128,512]{1,0:T(8,128)(2,1)S(1)} %bitcast.22), custom_call_target="tpu_custom_call" | custom-call | tf_op jit(solution)/shard_map/pallas_call | solution.py:414
  55.9 5.2 %all-to-all-start.1 = ((bf16[16,16,1408]{2,1,0:T(8,128)(2,1)}), bf16[16,16,1408]{2,1,0:T(8,128)(2,1)S(1)}, u32[]{:S(2)}, u32[]{:S(2)}) async-start(bf16[16,16,1408]{2,1,0:T(8,128)(2,1)} %bitcast.10), calls=%async_computation.1 | async-start | bytes 1441792 | tf_op jit(solution)/shard_map/all_to_all | solution.py:523
  61.1 0.0 copy-done.2
  61.2 2.2 %shard_map.172 = (bf16[256,2688]{1,0:T(8,128)(2,1)S(1)}, bf16[256,256]{1,0:T(8,128)(2,1)S(1)}, bf16[256,256]{1,0:T(8,128)(2,1)S(1)}, bf16[256,256]{1,0:T(8,128)(2,1)S(1)}, f32[3,64,128]{2,1,0:T(8,128)S(1)}) custom-call(s32[1]{0:T(128)S(6)} %copy.19.rank_hbm.rank_ref, s32[1,1,16]{2,1,0:T(1,128)S(1)} %copy-done.2, s32[1]{0:T(128)} %bitcast.1.core_ref, ...), custom_call_target="tpu_custom_call" | custom-call | tf_op jit(solution)/shard_map/pallas_call | solution.py:422
  63.4 17.1 %all-to-all-done.1 = bf16[16,16,1408]{2,1,0:T(8,128)(2,1)S(1)} async-done(((bf16[16,16,1408]{2,1,0:T(8,128)(2,1)}), bf16[16,16,1408]{2,1,0:T(8,128)(2,1)S(1)}, u32[]{:S(2)}, u32[]{:S(2)}) %all-to-all-start.1) | async-done | bytes 720928 | tf_op jit(solution)/shard_map/all_to_all | solution.py:523
  80.5 4.8 %shard_map.174 = (bf16[1,128,2560]{2,1,0:T(8,128)(2,1)}, bf16[1,128,512]{2,1,0:T(8,128)(2,1)}, bf16[1,128,512]{2,1,0:T(8,128)(2,1)}, bf16[2048,128]{1,0:T(8,128)(2,1)S(1)}, bf16[2048,128]{1,0:T(8,128)(2,1)S(1)}) custom-call(bf16[128,5120]{1,0:T(8,128)(2,1)} %bitcast.24, bf16[64,2560]{1,0:T(8,128)(2,1)} %wu_hbm.3, ...), custom_call_target="tpu_custom_call" | custom-call | tf_op jit(solution)/shard_map/pallas_call | solution.py:442
  85.3 3.9 %collective-permute-start = (bf16[2048,128]{1,0:T(8,128)(2,1)S(1)}, bf16[2048,128]{1,0:T(8,128)(2,1)S(1)}, u32[]{:S(2)}, u32[]{:S(2)}) collective-permute-start(bf16[2048,128]{1,0:T(8,128)(2,1)S(1)} %get-tuple-element.34), channel_id=1, source_target_pairs={{0,1},{1,0},{2,3},{3,2},{4,5},{5,4},{6,7},{7,6},{8,9},{9,8},{10,11... | collective-permute-start | bytes 1572872 | tf_op jit(solution)/shard_map/ppermute | solution.py:473
  89.2 1.5 %collective-permute-done = bf16[2048,128]{1,0:T(8,128)(2,1)S(1)} collective-permute-done((bf16[2048,128]{1,0:T(8,128)(2,1)S(1)}, bf16[2048,128]{1,0:T(8,128)(2,1)S(1)}, u32[]{:S(2)}, u32[]{:S(2)}) %collective-permute-start) | collective-permute-done | bytes 524320 | tf_op jit(solution)/shard_map/ppermute | solution.py:473
  90.8 0.1 add_convert_fusion
  90.9 16.3 %all_to_all.21 = bf16[32,64,128]{2,1,0:T(8,128)(2,1)S(1)} all-to-all(bf16[32,64,128]{2,1,0:T(8,128)(2,1)S(1)} %bitcast.25), channel_id=1, replica_groups={{0,2,4,6,8,10,12,14,64,66,68,70,72,74,76,78,128,130,132,134,136,138,140..., dimensions={0} | all-to-all | bytes 1048576 | tf_op jit(solution)/shard_map/all_to_all | solution.py:491
  107.2 0.1 convert_reduce_fusion
  107.3 0.1 collective-permute-start.1
  107.4 4.0 %collective-permute-done.1 = f32[64,128]{1,0:T(8,128)S(1)} collective-permute-done((f32[64,128]{1,0:T(8,128)S(1)}, f32[64,128]{1,0:T(8,128)S(1)}, u32[]{:S(2)}, u32[]{:S(2)}) %collective-permute-start.1) | collective-permute-done | bytes 32800 | tf_op jit(solution)/shard_map/ppermute | solution.py:493
  111.4 0.8 collective-permute-start.2
  112.2 4.1 %collective-permute-done.2 = f32[64,128]{1,0:T(8,128)S(1)} collective-permute-done((f32[64,128]{1,0:T(8,128)S(1)}, f32[64,128]{1,0:T(8,128)S(1)}, u32[]{:S(2)}, u32[]{:S(2)}) %collective-permute-start.2) | collective-permute-done | bytes 32800 | tf_op jit(solution)/shard_map/ppermute | solution.py:493
  116.3 0.1 broadcast_in_dim.18
  116.4 13.1 %all_to_all.22 = bf16[32,64,128]{2,1,0:T(8,128)(2,1)S(1)} all-to-all(bf16[32,64,128]{2,1,0:T(8,128)(2,1)S(1)} %broadcast_in_dim.18), channel_id=1, replica_groups={{0,2,4,6,8,10,12,14,64,66,68,70,72,74,76,78,128,130,132,134,136,138,140..., dimensions={0} | all-to-all | bytes 1048576 | tf_op jit(solution)/shard_map/all_to_all | solution.py:495
  129.5 5.2 %collective-permute-start.3 = (bf16[2048,128]{1,0:T(8,128)(2,1)S(1)}, bf16[2048,128]{1,0:T(8,128)(2,1)S(1)}, u32[]{:S(2)}, u32[]{:S(2)}) collective-permute-start(bf16[2048,128]{1,0:T(8,128)(2,1)S(1)} %bitcast.19), channel_id=1, source_target_pairs={{0,1},{1,0},{2,3},{3,2},{4,5},{5,4},{6,7},{7,6},{8,9},{9,8},{10,11... | collective-permute-start | bytes 1572872 | tf_op jit(solution)/shard_map/ppermute | solution.py:473
  134.7 1.5 %collective-permute-done.3.other_ref = bf16[2048,128]{1,0:T(8,128)(2,1)S(1)} collective-permute-done((bf16[2048,128]{1,0:T(8,128)(2,1)S(1)}, bf16[2048,128]{1,0:T(8,128)(2,1)S(1)}, u32[]{:S(2)}, u32[]{:S(2)}) %collective-permute-start.3) | collective-permute-done | bytes 524320 | tf_op jit(solution)/shard_map/ppermute | solution.py:473
  136.3 1.4 %shard_map.175 = (f32[64,5120]{1,0:T(8,128)}, f32[64,2560]{1,0:T(8,128)}) custom-call(f32[3,64,128]{2,1,0:T(8,128)S(1)} %get-tuple-element.26.factors_ref, bf16[2048,128]{1,0:T(8,128)(2,1)S(1)} %bitcast.20, bf16[2048,128]{1,0:T(8,128)(2,1)S(1)} %collective-permute-done.3.other_ref), custom_call_target="tpu_custom_call" | custom-call | tf_op jit(solution)/shard_map/pallas_call | solution.py:465
  (5 shorter events, 0.0 us)
Async XLA Ops:
  6.5 46.2 %copy-start = (bf16[1,128,512]{2,1,0:T(8,128)(2,1)S(1)}, bf16[1,128,512]{2,1,0:T(8,128)(2,1)}, u32[]{:S(2)}) copy-start(bf16[1,128,512]{2,1,0:T(8,128)(2,1)} %param.17) | copy-start | bytes 393220
  6.5 46.2 %copy-start.1 = (bf16[1,128,512]{2,1,0:T(8,128)(2,1)S(1)}, bf16[1,128,512]{2,1,0:T(8,128)(2,1)}, u32[]{:S(2)}) copy-start(bf16[1,128,512]{2,1,0:T(8,128)(2,1)} %param.18) | copy-start | bytes 393220
  52.8 8.4 %copy-start.2 = (s32[1,1,16]{2,1,0:T(1,128)S(1)}, s32[1,1,16]{2,1,0:T(1,128)}, u32[]{:S(2)}) copy-start(s32[1,1,16]{2,1,0:T(1,128)} %route_ref.1) | copy-start | bytes 196
  55.9 24.6 %all-to-all-start.1 = ((bf16[16,16,1408]{2,1,0:T(8,128)(2,1)}), bf16[16,16,1408]{2,1,0:T(8,128)(2,1)S(1)}, u32[]{:S(2)}, u32[]{:S(2)}) async-start(bf16[16,16,1408]{2,1,0:T(8,128)(2,1)} %bitcast.10), calls=%async_computation.1 | async-start | bytes 1441792 | tf_op jit(solution)/shard_map/all_to_all | solution.py:523
  85.3 5.4 %collective-permute-start = (bf16[2048,128]{1,0:T(8,128)(2,1)S(1)}, bf16[2048,128]{1,0:T(8,128)(2,1)S(1)}, u32[]{:S(2)}, u32[]{:S(2)}) collective-permute-start(bf16[2048,128]{1,0:T(8,128)(2,1)S(1)} %get-tuple-element.34), channel_id=1, source_target_pairs={{0,1},{1,0},{2,3},{3,2},{4,5},{5,4},{6,7},{7,6},{8,9},{9,8},{10,11... | collective-permute-start | bytes 1572872 | tf_op jit(solution)/shard_map/ppermute | solution.py:473
  107.3 4.1 %collective-permute-start.1 = (f32[64,128]{1,0:T(8,128)S(1)}, f32[64,128]{1,0:T(8,128)S(1)}, u32[]{:S(2)}, u32[]{:S(2)}) collective-permute-start(f32[64,128]{1,0:T(8,128)S(1)} %convert_reduce_fusion), channel_id=1, source_target_pairs={{0,16},{16,0},{32,48},{48,32},{64,80},{80,64},{96,112},{112,96},{1... | collective-permute-start | bytes 98312 | tf_op jit(solution)/shard_map/ppermute | solution.py:493
  111.4 4.9 %collective-permute-start.2 = (f32[64,128]{1,0:T(8,128)S(1)}, f32[64,128]{1,0:T(8,128)S(1)}, u32[]{:S(2)}, u32[]{:S(2)}) collective-permute-start(f32[64,128]{1,0:T(8,128)S(1)} %add.15), channel_id=1, source_target_pairs={{0,48},{16,32},{32,16},{48,0},{64,112},{80,96},{96,80},{112,64},{1... | collective-permute-start | bytes 98312 | tf_op jit(solution)/shard_map/ppermute | solution.py:493
  129.5 6.8 %collective-permute-start.3 = (bf16[2048,128]{1,0:T(8,128)(2,1)S(1)}, bf16[2048,128]{1,0:T(8,128)(2,1)S(1)}, u32[]{:S(2)}, u32[]{:S(2)}) collective-permute-start(bf16[2048,128]{1,0:T(8,128)(2,1)S(1)} %bitcast.19), channel_id=1, source_target_pairs={{0,1},{1,0},{2,3},{3,2},{4,5},{5,4},{6,7},{7,6},{8,9},{9,8},{10,11... | collective-permute-start | bytes 1572872 | tf_op jit(solution)/shard_map/ppermute | solution.py:473

commit v7 on v6

--- a/solution.py
+++ b/solution.py
@@ -25,6 +25,8 @@
 QUERY_WIDTH = QUERY_HEADS * HEAD_SIZE
 SEND_WIDTH = 2 * HALF + 128
 X_PARTS = 4
+COST_FLOPS = 10**9
+COST_BYTES = 60 * 10**6
 X_PART = MODEL_WIDTH // X_PARTS
 BACK_WIDTH = HALF + 128
 DOWN_BLOCKS = MODEL_WIDTH // 128
@@ -193,31 +195,64 @@
         copy.wait()
 
 
-def owner_kernel(rows_ref, k_ref, v_ref, back_ref, dk_ref, dv_ref):
+def owner_kernel(
+    rows_ref, kv0_ref, kv1_ref, kv2_ref, kv3_ref,
+    back_ref, part0_ref, part1_ref, part2_ref, part3_ref,
+):
+    kv_refs = (kv0_ref, kv1_ref, kv2_ref, kv3_ref)
+    part_refs = (part0_ref, part1_ref, part2_ref, part3_ref)
+    places = [(x * 4 + k) * 16 for k in range(4) for x in range(4)]
     lower = (lax.broadcasted_iota(jnp.int32, (ROWS, HEAD_SIZE), 0) // CL % 2 == 0).astype(F32)
     lower, upper = lower.astype(BF16), (1.0 - lower).astype(BF16)
-    stats = unpack_stats(rows_ref[:, 2 * HALF :], 2 * PAIRS)
-
-    def beside(ref, h):
-        return jnp.concatenate([ref[:, m * 128 : (m + 1) * 128] for m in (h, h + 2)], axis=1)
+    even = lax.broadcasted_iota(jnp.int32, (PLEN, 128), 1) < 64
+
+    def load(at):
+        return jnp.concatenate([rows_ref[p : p + 16, at : at + 128] for p in places], axis=0)
+
+    def store(at, value):
+        for i, p in enumerate(places):
+            back_ref[p : p + 16, at : at + 128] = value[i * 16 : (i + 1) * 16]
+
+    def beside(k, at):
+        return jnp.concatenate([kv_refs[k][:, at + m : at + m + 128] for m in (0, 256)], axis=1)
 
     def apart(rows):
         return jnp.concatenate([rows * lower, rows * upper], axis=1)
 
-    sides = [(beside(k_ref, h), beside(v_ref, h)) for h in range(2)]
+    def by_prompt(rows):
+        none = jnp.zeros((64, 256), BF16)
+        return jnp.concatenate(
+            [
+                jnp.concatenate([rows[:64], none], axis=1),
+                jnp.concatenate([none, rows[64:]], axis=1),
+            ],
+            axis=0,
+        )
+
+    def against(sides, rows):
+        parts = []
+        for p in range(2):
+            two = rows[p * 128 : (p + 1) * 128]
+            parts.append(jnp.where(even, nt(sides[2 * p], two), nt(sides[2 * p + 1], two)))
+        return jnp.concatenate(parts, axis=1)
+
+    sides = [
+        ([beside(k, h * 128) for k in range(4)], [beside(k, 512 + h * 128) for k in range(4)])
+        for h in range(2)
+    ]
+    stats = unpack_stats(load(2 * HALF), 2 * PAIRS)
 
     def products(b):
-        g = apart(rows_ref[:, b * 128 : (b + 1) * 128])
-        q = apart(rows_ref[:, HALF + b * 128 : HALF + (b + 1) * 128])
+        g = apart(load(b * 128))
+        q = apart(load(HALF + b * 128))
         keys, values = sides[b // GROUP]
-        return q, g, nt(keys, q), nt(values, g)
+        return q, g, against(keys, q), against(values, g)
 
     lses, deltas = [], []
     ready = products(0)
     for h in range(2):
         keys = sides[h][0]
-        dk = jnp.zeros((PLEN, 2 * HEAD_SIZE), F32)
-        dv = jnp.zeros((PLEN, 2 * HEAD_SIZE), F32)
+        done = []
         for b in range(h * GROUP, (h + 1) * GROUP):
             q, g, scores, dprob = ready
             if b + 1 < PAIRS:
@@ -235,17 +270,35 @@
                 own_lse - lse
             )
             dscore = (probs * (dprob - delta)).astype(BF16)
-            dv = dv + nn(probs_b, g)
-            dk = dk + nn(dscore, q)
-            dq = (tn(dscore, keys) * INV_SQRT).reshape(SLOTS, 2, CL, 2 * HEAD_SIZE)
-            dq = jnp.concatenate([dq[:, :1, :, :HEAD_SIZE], dq[:, 1:, :, HEAD_SIZE:]], axis=1)
-            back_ref[:, b * 128 : (b + 1) * 128] = dq.reshape(ROWS, HEAD_SIZE).astype(BF16)
+            picks = []
+            for p in range(2):
+                both = jnp.concatenate([keys[2 * p], keys[2 * p + 1]], axis=1)
+                full = tn(dscore[:, p * 128 : (p + 1) * 128], both) * INV_SQRT
+                for k in range(2):
+                    rows = full[k * 64 : (k + 1) * 64, k * 256 : (k + 1) * 256]
+                    rows = rows.reshape(4, 2, CL, 256)
+                    rows = jnp.concatenate(
+                        [rows[:, :1, :, :HEAD_SIZE], rows[:, 1:, :, HEAD_SIZE:]], axis=1
+                    )
+                    picks.append(rows.reshape(64, HEAD_SIZE))
+            store(b * 128, jnp.concatenate(picks, axis=0).astype(BF16))
+            done.append((dscore, q, probs_b, g))
             lses.append(lse)
             deltas.append(delta)
-        for at, m in ((0, h), (HEAD_SIZE, h + 2)):
-            dk_ref[:, m * 128 : (m + 1) * 128] = (dk[:, at : at + HEAD_SIZE] * INV_SQRT).astype(BF16)
-            dv_ref[:, m * 128 : (m + 1) * 128] = dv[:, at : at + HEAD_SIZE].astype(BF16)
-    back_ref[:, HALF:] = pack_stats(lses + deltas).astype(BF16)
+        for p in range(2):
+            at = slice(p * 128, (p + 1) * 128)
+            for first, scale, base in ((0, INV_SQRT, 0), (2, 1.0, 512)):
+                left = jnp.concatenate([d[first][:, at] for d in done], axis=1)
+                right = jnp.concatenate([by_prompt(d[first + 1][at]) for d in done], axis=0)
+                grad = nn(left, right) * scale
+                for k in range(2):
+                    ref = part_refs[2 * p + k]
+                    for i, m in enumerate((h, h + 2)):
+                        column = k * 256 + i * 128
+                        ref[:, base + m * 128 : base + (m + 1) * 128] = grad[
+                            :, column : column + 128
+                        ].astype(ref.dtype)
+    store(HALF, pack_stats(lses + deltas).astype(BF16))
 
 
 def own_kernel(
@@ -378,7 +431,7 @@
 HBM = pl.BlockSpec(memory_space=pltpu.HBM)
 
 
-def call(kernel, in_specs, outs, scratch=(), out_specs=None, vmem_mib=40):
+def call(kernel, in_specs, outs, scratch=(), out_specs=None, vmem_mib=40, cost=None):
     return pl.pallas_call(
         kernel,
         out_shape=[jax.ShapeDtypeStruct(shape, dtype) for shape, dtype in outs],
@@ -386,6 +439,7 @@
         out_specs=out_specs or [VMEM] * len(outs),
         scratch_shapes=list(scratch),
         compiler_params=pltpu.CompilerParams(vmem_limit_bytes=vmem_mib * 1024 * 1024),
+        cost_estimate=cost,
     )
 
 
@@ -407,15 +461,30 @@
         ],
         [HBM],
         60,
+        pl.CostEstimate(flops=COST_FLOPS, bytes_accessed=COST_BYTES, transcendentals=0),
     )(*arrays)[0]
 
 
-def run_owner(rows, keys, values):
+def run_owner(rows, *prompts):
+    part = (PLEN, 2 * KEY_VALUE_HEADS * HEAD_SIZE)
     return call(
         owner_kernel,
-        [VMEM] * 3,
-        [((ROWS, BACK_WIDTH), BF16)] + [((PLEN, KEY_VALUE_HEADS * HEAD_SIZE), BF16)] * 2,
-    )(rows, keys, values)
+        [VMEM] * 5,
+        [((ROWS, BACK_WIDTH), BF16), (part, F32)] + [(part, BF16)] * 3,
+    )(rows, *prompts)
+
+
+def by_z(part, step):
+    pairs = [(x * 4 + z, x * 4 + (z + step) % 4) for x in range(4) for z in range(4)]
+    return lax.ppermute(part, "prompt", pairs)
+
+
+def over_x(blocks):
+    groups = [[x * 4 + z for x in range(4)] for z in range(4)]
+    shape = blocks.shape
+    blocks = blocks.reshape(4, 64, shape[-1])
+    moved = lax.all_to_all(blocks, "prompt", 0, 0, axis_index_groups=groups, tiled=True)
+    return moved.reshape(shape)
 
 
 def run_own(rank, route, core, *arrays):
@@ -481,7 +550,7 @@
     ]
 
 
-def sum_all(mine, other):
+def sum_all(mine, other, beside):
     rows = CORE_ROWS // 32
     swap = functools.partial(
         lax.all_to_all, axis_name=("prompt", "comp"), split_axis=0, concat_axis=0,
@@ -493,7 +562,8 @@
         total = total + lax.ppermute(total, "prompt", [(i, flip(i)) for i in range(16)])
     total = total.astype(BF16)
     half = swap(jnp.broadcast_to(total[None], (32, rows, 128))).reshape(CORE_ROWS, 128)
-    return half, by_core(half)
+    half, beside = lax.optimization_barrier((half, beside))
+    return half, by_core(half), beside
 
 
 def per_device(
@@ -512,21 +582,31 @@
 ):
     hidden = normed_hidden_input[0]
     keys, values = completion_keys[0], completion_values[0]
+    prompt = jnp.concatenate([owner_prompt_keys[0], owner_prompt_values[0]], axis=1)
+    prompts = [prompt] + [by_z(prompt, -k) for k in (1, 2, 3)]
+    z = lax.axis_index("prompt") % 4
+    route = route // 4 * 4 + (route - z) % 4
     send = run_prepare(
         adapter_rank, route, lengths, hidden, frozen_query_base[0], attention_output_grad[0],
         keys, values, adapter_down_weight.T, adapter_up_weight,
     )
-    arrived = lax.all_to_all(send, "prompt", 0, 0, tiled=True)
-    back, dk, dv = run_owner(
-        arrived.reshape(ROWS, SEND_WIDTH), owner_prompt_keys[0], owner_prompt_values[0]
-    )
-    back = lax.all_to_all(back.reshape(SLOTS, 16, BACK_WIDTH), "prompt", 0, 0, tiled=True)
+    send, prompts[2] = lax.optimization_barrier((send, prompts[2]))
+    arrived = over_x(send)
+    back, total, *parts = run_owner(arrived.reshape(ROWS, SEND_WIDTH), *prompts)
+    back = over_x(back.reshape(SLOTS, 16, BACK_WIDTH))
+    back, far = lax.optimization_barrier((back, by_z(parts[1], 2)))
     core = (lax.axis_index("comp") % 2).astype(jnp.int32)[None]
     own = run_own(adapter_rank, route, core, keys, values, send)
     dq, dsk, dsv, mine, other = run_finish(
         hidden, adapter_up_weight, *own, back.reshape(ROWS, BACK_WIDTH)
     )
-    down, up = run_spread(own[-1], *sum_all(mine, other))
+    near = [by_z(parts[0], 1), by_z(parts[2], 3)]
+    half, other_half, near = sum_all(mine, other, near)
+    for part in [far] + near:
+        total = total + part.astype(F32)
+    width = KEY_VALUE_HEADS * HEAD_SIZE
+    dk, dv = total[:, :width].astype(BF16), total[:, width:].astype(BF16)
+    down, up = run_spread(own[-1], half, other_half)
     return dq, dsk, dsv, dk[None], dv[None], down.T, up
 
 

time: 138 us -> 133 us (0.964)
  blocking collectives: 75.6 us -> 23.1 us
  starting transfers between devices: 15.3 us -> 41.3 us
  waiting for transfers between devices: 28.3 us -> 42.9 us
  other arithmetic: 0.23 us -> 3.49 us
  local copies, waits for them, and re-layouts: 0.13 us -> 2.33 us
    all_to_all x2 -> x0, blocking collectives: 59.3 us -> none  [the longest x1 46.2 us: per_device(): arrived = lax.all_to_all(send, 'prompt', 0, 0, tiled=True)]
    ppermute x0 -> x6, waiting for transfers between devices: none -> 34.1 us  [by_z(): return lax.ppermute(part, 'prompt', pairs)]
    ppermute x0 -> x6, starting transfers between devices: none -> 20.4 us  [by_z(): return lax.ppermute(part, 'prompt', pairs)]
    all_to_all x1 -> x3, waiting for transfers between devices: 17.1 us -> 0.01 us  [the longest x2 0.01 us: over_x(): lax.all_to_all(blocks, 'prompt', 0, 0, axis_index_groups=groups, tiled=True)]
    all_to_all x1 -> x3, starting transfers between devices: 5.24 us -> 12.5 us  [the longest x2 8.22 us: over_x(): lax.all_to_all(blocks, 'prompt', 0, 0, axis_index_groups=groups, tiled=True)]
    all_to_all x1, blocking collectives: 16.3 us -> 23.1 us  [sum_all(): total = jnp.sum(swap(pair.reshape(32, rows, 128)).astype(F32), axis=0)]
    ppermute x2, starting transfers between devices: 9.13 us -> 6.72 us  [by_core(): return lax.ppermute(part, 'comp', [(i, i ^ 1) for i in range(16)])]
    ppermute x2, waiting for transfers between devices: 3.07 us -> 1.54 us  [by_core(): return lax.ppermute(part, 'comp', [(i, i ^ 1) for i in range(16)])]
  transfers between devices with their start and end apart: 5 -> 13, of which waited for: 5 -> 6; matrix products, arithmetic and copies ran while one was open for 0% -> 2% of each run, Pallas kernels for 2% -> 6%
where the time goes in v7:
time: 133 us; the launch traced here: 132 us
  waiting for transfers between devices  42.9 us (32%)
  starting transfers between devices  41.3 us (31%)
  blocking collectives  23.1 us (17%)
  Pallas kernels  17.8 us (13%)
  other arithmetic  3.49 us (3%)
  local copies, waits for them, and re-layouts  2.33 us (2%)
  between operations  1.38 us (1%)
    ppermute x6, waiting for transfers between devices, by_z(): return lax.ppermute(part, 'prompt', pairs)  34.1 us
    all_to_all x1, blocking collectives, sum_all(): total = jnp.sum(swap(pair.reshape(32, rows, 128)).astype(F32), axis=0)  23.1 us
    ppermute x6, starting transfers between devices, by_z(): return lax.ppermute(part, 'prompt', pairs)  20.4 us
    all_to_all x2, starting transfers between devices, over_x(): lax.all_to_all(blocks, 'prompt', 0, 0, axis_index_groups=groups, tiled=True)  8.22 us
    ppermute x2, waiting for transfers between devices, sum_all(): lax.ppermute(total, 'prompt', [(i, flip(i)) for i in range(16)])  7.24 us
    ppermute x2, starting transfers between devices, by_core(): return lax.ppermute(part, 'comp', [(i, i ^ 1) for i in range(16)])  6.72 us
    pallas_call x1, Pallas kernels, run_prepare(): call(prepare_kernel, [HBM] * len(arrays), [((SLOTS, 16, SEND_WIDTH), BF16...  5.2 us
    pallas_call x1, Pallas kernels, run_finish(): call(finish_kernel, [HBM] * 2 + [VMEM] * len(arrays), [((1, TOKENS, QUERY...  4.8 us
  transfers between devices with their start and end apart: 13, of which 6 were waited for; matrix products, arithmetic and copies ran while one was open for 2% of the time, Pallas kernels for 6%

profile of v7, /device:TPU:1, one launch (start us, length us, event | category | flops | bytes accessed | tf_op | source)
XLA Modules:
  0.0 132.4 jit_solution(1577753657834962874)
XLA Ops:
  1.6 7.8 %collective-permute-start = (bf16[128,1024]{1,0:T(8,128)(2,1)S(1)}, bf16[128,1024]{1,0:T(8,128)(2,1)S(1)}, u32[]{:S(2)}, u32[]{:S(2)}) collective-permute-start(bf16[128,1024]{1,0:T(8,128)(2,1)S(1)} %pad_maximum_fusion.kv0_ref), channel_id=1, source_target_pairs={{0,32},{16,48},{32,0},{48,16},{64,96},{80,112},{96,64},{112,80},{1... | collective-permute-start | bytes 786440 | tf_op jit(solution)/shard_map/ppermute | solution.py:479
  10.1 1.2 fusion.route_hbm.route_ref
  11.3 5.2 %shard_map.171.send_hbm = bf16[16,16,2688]{2,1,0:T(8,128)(2,1)} custom-call(s32[1]{0:T(128)S(6)} %copy.19.rank_hbm.rank_ref, s32[1,1,16]{2,1,0:T(1,128)} %fusion.route_hbm.route_ref, s32[1,1,16]{2,1,0:T(1,128)} %length_hbm.1, bf16[128,5120]{1,0:T(8,128)(2,1)} %bitcast.26, bf16[128,2560]{1,0:T(8,128)(2,1)} %bitcast.29, bf16[128,2560]{1,0:T(8,128)(2,1)} %bitcast.30, ...), custom_call_target="tpu_custom_call" | custom-call | flops 1000000000 | bytes 60000000 | tf_op jit(solution)/shard_map/pallas_call | solution.py:453
  16.5 4.0 %all-to-all-start = ((bf16[4,64,2688]{2,1,0:T(8,128)(2,1)}), bf16[4,64,2688]{2,1,0:T(8,128)(2,1)S(1)}, u32[]{:S(2)}, u32[]{:S(2)}) async-start(bf16[4,64,2688]{2,1,0:T(8,128)(2,1)} %bitcast.25), calls=%async_computation | async-start | bytes 2752512 | tf_op jit(solution)/shard_map/all_to_all | solution.py:486
  20.5 6.2 %collective-permute-start.2 = (bf16[128,1024]{1,0:T(8,128)(2,1)S(1)}, bf16[128,1024]{1,0:T(8,128)(2,1)S(1)}, u32[]{:S(2)}, u32[]{:S(2)}) collective-permute-start(bf16[128,1024]{1,0:T(8,128)(2,1)S(1)} %pad_maximum_fusion.kv0_ref), channel_id=1, source_target_pairs={{0,16},{16,32},{32,48},{48,0},{64,80},{80,96},{96,112},{112,64},{1... | collective-permute-start | bytes 786440 | tf_op jit(solution)/shard_map/ppermute | solution.py:479
  26.6 2.7 %collective-permute-start.1 = (bf16[128,1024]{1,0:T(8,128)(2,1)S(1)}, bf16[128,1024]{1,0:T(8,128)(2,1)S(1)}, u32[]{:S(2)}, u32[]{:S(2)}) collective-permute-start(bf16[128,1024]{1,0:T(8,128)(2,1)S(1)} %pad_maximum_fusion.kv0_ref), channel_id=1, source_target_pairs={{0,48},{16,0},{32,16},{48,32},{64,112},{80,64},{96,80},{112,96},{1... | collective-permute-start | bytes 786440 | tf_op jit(solution)/shard_map/ppermute | solution.py:479
  29.4 11.7 %collective-permute-done.2.kv3_ref = bf16[128,1024]{1,0:T(8,128)(2,1)S(1)} collective-permute-done((bf16[128,1024]{1,0:T(8,128)(2,1)S(1)}, bf16[128,1024]{1,0:T(8,128)(2,1)S(1)}, u32[]{:S(2)}, u32[]{:S(2)}) %collective-permute-start.2) | collective-permute-done | bytes 262176 | tf_op jit(solution)/shard_map/ppermute | solution.py:479
  41.1 4.2 %shard_map.173 = (bf16[256,1408]{1,0:T(8,128)(2,1)}, f32[128,1024]{1,0:T(8,128)S(1)}, bf16[128,1024]{1,0:T(8,128)(2,1)S(1)}, bf16[128,1024]{1,0:T(8,128)(2,1)}, bf16[128,1024]{1,0:T(8,128)(2,1)S(1)}) custom-call(bf16[256,2688]{1,0:T(8,128)(2,1)S(1)} %bitcast.21, bf16[128,1024]{1,0:T(8,128)(2,1)S(1)} %pad_maximum_fusion.kv0_ref, ...), custom_call_target="tpu_custom_call" | custom-call | tf_op jit(solution)/shard_map/pallas_call | solution.py:470
  46.0 4.2 %all-to-all-start.1 = ((bf16[4,64,1408]{2,1,0:T(8,128)(2,1)}), bf16[4,64,1408]{2,1,0:T(8,128)(2,1)S(1)}, u32[]{:S(2)}, u32[]{:S(2)}) async-start(bf16[4,64,1408]{2,1,0:T(8,128)(2,1)} %bitcast.11), calls=%async_computation.1 | async-start | bytes 1441792 | tf_op jit(solution)/shard_map/all_to_all | solution.py:486
  50.2 2.2 %shard_map.172 = (bf16[256,2688]{1,0:T(8,128)(2,1)S(1)}, bf16[256,256]{1,0:T(8,128)(2,1)S(1)}, bf16[256,256]{1,0:T(8,128)(2,1)S(1)}, bf16[256,256]{1,0:T(8,128)(2,1)S(1)}, f32[3,64,128]{2,1,0:T(8,128)S(1)}) custom-call(s32[1]{0:T(128)S(6)} %copy.19.rank_hbm.rank_ref, s32[1,1,16]{2,1,0:T(1,128)S(1)} %copy-done, s32[1]{0:T(128)} %bitcast.1.core_ref, ...), custom_call_target="tpu_custom_call" | custom-call | tf_op jit(solution)/shard_map/pallas_call | solution.py:491
  52.4 8.6 %collective-permute-done.3 = bf16[128,1024]{1,0:T(8,128)(2,1)} collective-permute-done((bf16[128,1024]{1,0:T(8,128)(2,1)}, bf16[128,1024]{1,0:T(8,128)(2,1)}, u32[]{:S(2)}, u32[]{:S(2)}) %collective-permute-start.3) | collective-permute-done | bytes 262176 | tf_op jit(solution)/shard_map/ppermute | solution.py:479
  61.0 4.8 %shard_map.174 = (bf16[1,128,2560]{2,1,0:T(8,128)(2,1)}, bf16[1,128,512]{2,1,0:T(8,128)(2,1)}, bf16[1,128,512]{2,1,0:T(8,128)(2,1)}, bf16[2048,128]{1,0:T(8,128)(2,1)S(1)}, bf16[2048,128]{1,0:T(8,128)(2,1)S(1)}) custom-call(bf16[128,5120]{1,0:T(8,128)(2,1)} %bitcast.27, bf16[64,2560]{1,0:T(8,128)(2,1)} %wu_hbm.3, ...), custom_call_target="tpu_custom_call" | custom-call | tf_op jit(solution)/shard_map/pallas_call | solution.py:511
  65.8 3.6 %collective-permute-start.4 = (bf16[2048,128]{1,0:T(8,128)(2,1)S(1)}, bf16[2048,128]{1,0:T(8,128)(2,1)S(1)}, u32[]{:S(2)}, u32[]{:S(2)}) collective-permute-start(bf16[2048,128]{1,0:T(8,128)(2,1)S(1)} %get-tuple-element.47), channel_id=1, source_target_pairs={{0,1},{1,0},{2,3},{3,2},{4,5},{5,4},{6,7},{7,6},{8,9},{9,8},{10,11... | collective-permute-start | bytes 1572872 | tf_op jit(solution)/shard_map/ppermute | solution.py:542
  69.4 1.5 %collective-permute-done.4 = bf16[2048,128]{1,0:T(8,128)(2,1)S(1)} collective-permute-done((bf16[2048,128]{1,0:T(8,128)(2,1)S(1)}, bf16[2048,128]{1,0:T(8,128)(2,1)S(1)}, u32[]{:S(2)}, u32[]{:S(2)}) %collective-permute-start.4) | collective-permute-done | bytes 524320 | tf_op jit(solution)/shard_map/ppermute | solution.py:542
  71.1 23.1 %all_to_all.20 = bf16[32,64,128]{2,1,0:T(8,128)(2,1)S(1)} all-to-all(bf16[32,64,128]{2,1,0:T(8,128)(2,1)S(1)} %bitcast.28), channel_id=1, replica_groups={{0,2,4,6,8,10,12,14,64,66,68,70,72,74,76,78,128,130,132,134,136,138,140..., dimensions={0} | all-to-all | bytes 1048576 | tf_op jit(solution)/shard_map/all_to_all | solution.py:560
  94.6 3.9 %collective-permute-done.5 = f32[64,128]{1,0:T(8,128)S(1)} collective-permute-done((f32[64,128]{1,0:T(8,128)S(1)}, f32[64,128]{1,0:T(8,128)S(1)}, u32[]{:S(2)}, u32[]{:S(2)}) %collective-permute-start.5) | collective-permute-done | bytes 32800 | tf_op jit(solution)/shard_map/ppermute | solution.py:562
  98.5 1.5 %collective-permute-start.6 = (f32[64,128]{1,0:T(8,128)S(1)}, f32[64,128]{1,0:T(8,128)S(1)}, u32[]{:S(2)}, u32[]{:S(2)}) collective-permute-start(f32[64,128]{1,0:T(8,128)S(1)} %add.41), channel_id=1, source_target_pairs={{0,48},{16,32},{32,16},{48,0},{64,112},{80,96},{96,80},{112,64},{1... | collective-permute-start | bytes 98312 | tf_op jit(solution)/shard_map/ppermute | solution.py:562
  100.0 3.4 %collective-permute-done.6 = f32[64,128]{1,0:T(8,128)S(1)} collective-permute-done((f32[64,128]{1,0:T(8,128)S(1)}, f32[64,128]{1,0:T(8,128)S(1)}, u32[]{:S(2)}, u32[]{:S(2)}) %collective-permute-start.6) | collective-permute-done | bytes 32800 | tf_op jit(solution)/shard_map/ppermute | solution.py:562
  104.3 4.3 %all-to-all-start.3 = ((bf16[32,64,128]{2,1,0:T(8,128)(2,1)}), bf16[32,64,128]{2,1,0:T(8,128)(2,1)S(1)}, u32[]{:S(2)}, u32[]{:S(2)}) async-start(bf16[32,64,128]{2,1,0:T(8,128)(2,1)} %broadcast_in_dim.16), calls=%async_computation.3 | async-start | bytes 1048576 | tf_op jit(solution)/shard_map/all_to_all | solution.py:564
  109.4 2.8 %collective-permute-start.8 = (bf16[128,1024]{1,0:T(8,128)(2,1)S(1)}, bf16[128,1024]{1,0:T(8,128)(2,1)S(1)}, u32[]{:S(2)}, u32[]{:S(2)}) collective-permute-start(bf16[128,1024]{1,0:T(8,128)(2,1)S(1)} %get-tuple-element.49), channel_id=1, source_target_pairs={{0,48},{16,0},{32,16},{48,32},{64,112},{80,64},{96,80},{112,96},{1... | collective-permute-start | bytes 786440 | tf_op jit(solution)/shard_map/ppermute | solution.py:479
  112.2 13.8 %collective-permute-done.7 = bf16[128,1024]{1,0:T(8,128)(2,1)S(1)} collective-permute-done((bf16[128,1024]{1,0:T(8,128)(2,1)S(1)}, bf16[128,1024]{1,0:T(8,128)(2,1)S(1)}, u32[]{:S(2)}, u32[]{:S(2)}) %collective-permute-start.7) | collective-permute-done | bytes 262176 | tf_op jit(solution)/shard_map/ppermute | solution.py:479
  126.1 3.1 %collective-permute-start.9 = (bf16[2048,128]{1,0:T(8,128)(2,1)S(1)}, bf16[2048,128]{1,0:T(8,128)(2,1)S(1)}, u32[]{:S(2)}, u32[]{:S(2)}) collective-permute-start(bf16[2048,128]{1,0:T(8,128)(2,1)S(1)} %bitcast.23), channel_id=1, source_target_pairs={{0,1},{1,0},{2,3},{3,2},{4,5},{5,4},{6,7},{7,6},{8,9},{9,8},{10,11... | collective-permute-start | bytes 1572872 | tf_op jit(solution)/shard_map/ppermute | solution.py:542
  129.2 1.1 add_convert_fusion.1
  131.0 1.4 %shard_map.175 = (f32[64,5120]{1,0:T(8,128)}, f32[64,2560]{1,0:T(8,128)}) custom-call(f32[3,64,128]{2,1,0:T(8,128)S(1)} %get-tuple-element.36.factors_ref, bf16[2048,128]{1,0:T(8,128)(2,1)S(1)} %bitcast.24, bf16[2048,128]{1,0:T(8,128)(2,1)S(1)} %collective-permute-done.9.other_ref), custom_call_target="tpu_custom_call" | custom-call | tf_op jit(solution)/shard_map/pallas_call | solution.py:534
  (23 shorter events, 4.7 us)
Async XLA Ops:
  1.6 14.9 %collective-permute-start = (bf16[128,1024]{1,0:T(8,128)(2,1)S(1)}, bf16[128,1024]{1,0:T(8,128)(2,1)S(1)}, u32[]{:S(2)}, u32[]{:S(2)}) collective-permute-start(bf16[128,1024]{1,0:T(8,128)(2,1)S(1)} %pad_maximum_fusion.kv0_ref), channel_id=1, source_target_pairs={{0,32},{16,48},{32,0},{48,16},{64,96},{80,112},{96,64},{112,80},{1... | collective-permute-start | bytes 786440 | tf_op jit(solution)/shard_map/ppermute | solution.py:479
  16.5 24.6 %all-to-all-start = ((bf16[4,64,2688]{2,1,0:T(8,128)(2,1)}), bf16[4,64,2688]{2,1,0:T(8,128)(2,1)S(1)}, u32[]{:S(2)}, u32[]{:S(2)}) async-start(bf16[4,64,2688]{2,1,0:T(8,128)(2,1)} %bitcast.25), calls=%async_computation | async-start | bytes 2752512 | tf_op jit(solution)/shard_map/all_to_all | solution.py:486
  20.5 20.6 %collective-permute-start.2 = (bf16[128,1024]{1,0:T(8,128)(2,1)S(1)}, bf16[128,1024]{1,0:T(8,128)(2,1)S(1)}, u32[]{:S(2)}, u32[]{:S(2)}) collective-permute-start(bf16[128,1024]{1,0:T(8,128)(2,1)S(1)} %pad_maximum_fusion.kv0_ref), channel_id=1, source_target_pairs={{0,16},{16,32},{32,48},{48,0},{64,80},{80,96},{96,112},{112,64},{1... | collective-permute-start | bytes 786440 | tf_op jit(solution)/shard_map/ppermute | solution.py:479
  26.6 14.4 %collective-permute-start.1 = (bf16[128,1024]{1,0:T(8,128)(2,1)S(1)}, bf16[128,1024]{1,0:T(8,128)(2,1)S(1)}, u32[]{:S(2)}, u32[]{:S(2)}) collective-permute-start(bf16[128,1024]{1,0:T(8,128)(2,1)S(1)} %pad_maximum_fusion.kv0_ref), channel_id=1, source_target_pairs={{0,48},{16,0},{32,16},{48,32},{64,112},{80,64},{96,80},{112,96},{1... | collective-permute-start | bytes 786440 | tf_op jit(solution)/shard_map/ppermute | solution.py:479
  41.1 9.2 %copy-start = (s32[1,1,16]{2,1,0:T(1,128)S(1)}, s32[1,1,16]{2,1,0:T(1,128)}, u32[]{:S(2)}) copy-start(s32[1,1,16]{2,1,0:T(1,128)} %fusion.route_hbm.route_ref) | copy-start | bytes 196
  45.3 0.7 copy-start.1
  46.0 15.0 %all-to-all-start.1 = ((bf16[4,64,1408]{2,1,0:T(8,128)(2,1)}), bf16[4,64,1408]{2,1,0:T(8,128)(2,1)S(1)}, u32[]{:S(2)}, u32[]{:S(2)}) async-start(bf16[4,64,1408]{2,1,0:T(8,128)(2,1)} %bitcast.11), calls=%async_computation.1 | async-start | bytes 1441792 | tf_op jit(solution)/shard_map/all_to_all | solution.py:486
  50.2 10.8 %collective-permute-start.3 = (bf16[128,1024]{1,0:T(8,128)(2,1)}, bf16[128,1024]{1,0:T(8,128)(2,1)}, u32[]{:S(2)}, u32[]{:S(2)}) collective-permute-start(bf16[128,1024]{1,0:T(8,128)(2,1)} %get-tuple-element.39), channel_id=1, source_target_pairs={{0,32},{16,48},{32,0},{48,16},{64,96},{80,112},{96,64},{112,80},{1... | collective-permute-start | bytes 786440 | tf_op jit(solution)/shard_map/ppermute | solution.py:479
  65.8 5.2 %collective-permute-start.4 = (bf16[2048,128]{1,0:T(8,128)(2,1)S(1)}, bf16[2048,128]{1,0:T(8,128)(2,1)S(1)}, u32[]{:S(2)}, u32[]{:S(2)}) collective-permute-start(bf16[2048,128]{1,0:T(8,128)(2,1)S(1)} %get-tuple-element.47), channel_id=1, source_target_pairs={{0,1},{1,0},{2,3},{3,2},{4,5},{5,4},{6,7},{7,6},{8,9},{9,8},{10,11... | collective-permute-start | bytes 1572872 | tf_op jit(solution)/shard_map/ppermute | solution.py:542
  94.3 14.3 %copy-start.2 = (bf16[128,1024]{1,0:T(8,128)(2,1)S(1)}, bf16[128,1024]{1,0:T(8,128)(2,1)}, u32[]{:S(2)}) copy-start(bf16[128,1024]{1,0:T(8,128)(2,1)} %copy-done.1) | copy-start | bytes 786436
  94.4 4.1 %collective-permute-start.5 = (f32[64,128]{1,0:T(8,128)S(1)}, f32[64,128]{1,0:T(8,128)S(1)}, u32[]{:S(2)}, u32[]{:S(2)}) collective-permute-start(f32[64,128]{1,0:T(8,128)S(1)} %convert_reduce_fusion), channel_id=1, source_target_pairs={{0,16},{16,0},{32,48},{48,32},{64,80},{80,64},{96,112},{112,96},{1... | collective-permute-start | bytes 98312 | tf_op jit(solution)/shard_map/ppermute | solution.py:562
  98.5 4.9 %collective-permute-start.6 = (f32[64,128]{1,0:T(8,128)S(1)}, f32[64,128]{1,0:T(8,128)S(1)}, u32[]{:S(2)}, u32[]{:S(2)}) collective-permute-start(f32[64,128]{1,0:T(8,128)S(1)} %add.41), channel_id=1, source_target_pairs={{0,48},{16,32},{32,16},{48,0},{64,112},{80,96},{96,80},{112,64},{1... | collective-permute-start | bytes 98312 | tf_op jit(solution)/shard_map/ppermute | solution.py:562
  104.3 21.8 %all-to-all-start.3 = ((bf16[32,64,128]{2,1,0:T(8,128)(2,1)}), bf16[32,64,128]{2,1,0:T(8,128)(2,1)S(1)}, u32[]{:S(2)}, u32[]{:S(2)}) async-start(bf16[32,64,128]{2,1,0:T(8,128)(2,1)} %broadcast_in_dim.16), calls=%async_computation.3 | async-start | bytes 1048576 | tf_op jit(solution)/shard_map/all_to_all | solution.py:564
  108.6 17.5 %collective-permute-start.7 = (bf16[128,1024]{1,0:T(8,128)(2,1)S(1)}, bf16[128,1024]{1,0:T(8,128)(2,1)S(1)}, u32[]{:S(2)}, u32[]{:S(2)}) collective-permute-start(bf16[128,1024]{1,0:T(8,128)(2,1)S(1)} %copy-done.2), channel_id=1, source_target_pairs={{0,16},{16,32},{32,48},{48,0},{64,80},{80,96},{96,112},{112,64},{1... | collective-permute-start | bytes 786440 | tf_op jit(solution)/shard_map/ppermute | solution.py:479
  109.4 16.6 %collective-permute-start.8 = (bf16[128,1024]{1,0:T(8,128)(2,1)S(1)}, bf16[128,1024]{1,0:T(8,128)(2,1)S(1)}, u32[]{:S(2)}, u32[]{:S(2)}) collective-permute-start(bf16[128,1024]{1,0:T(8,128)(2,1)S(1)} %get-tuple-element.49), channel_id=1, source_target_pairs={{0,48},{16,0},{32,16},{48,32},{64,112},{80,64},{96,80},{112,96},{1... | collective-permute-start | bytes 786440 | tf_op jit(solution)/shard_map/ppermute | solution.py:479
  126.1 4.9 %collective-permute-start.9 = (bf16[2048,128]{1,0:T(8,128)(2,1)S(1)}, bf16[2048,128]{1,0:T(8,128)(2,1)S(1)}, u32[]{:S(2)}, u32[]{:S(2)}) collective-permute-start(bf16[2048,128]{1,0:T(8,128)(2,1)S(1)} %bitcast.23), channel_id=1, source_target_pairs={{0,1},{1,0},{2,3},{3,2},{4,5},{5,4},{6,7},{7,6},{8,9},{9,8},{10,11... | collective-permute-start | bytes 1572872 | tf_op jit(solution)/shard_map/ppermute | solution.py:542

commit v8 on v7

--- a/solution.py
+++ b/solution.py
@@ -196,11 +196,17 @@
 
 
 def owner_kernel(
-    rows_ref, kv0_ref, kv1_ref, kv2_ref, kv3_ref,
-    back_ref, part0_ref, part1_ref, part2_ref, part3_ref,
+    rows_ref, kv0_ref, kv1_ref, kv3_ref, k2_ref, v2_ref,
+    back_ref, part0_hbm, part1_hbm, part3_hbm, dk2_hbm, dv2_hbm,
+    part0_ref, part1_ref, part3_ref, dk2_ref, dv2_ref, sems,
 ):
-    kv_refs = (kv0_ref, kv1_ref, kv2_ref, kv3_ref)
-    part_refs = (part0_ref, part1_ref, part2_ref, part3_ref)
+    width = KEY_VALUE_HEADS * HEAD_SIZE
+
+    def halves(ref):
+        return ref.at[:, :width], ref.at[:, width:]
+
+    kv_refs = (halves(kv0_ref), halves(kv1_ref), (k2_ref, v2_ref), halves(kv3_ref))
+    part_refs = (halves(part0_ref), halves(part1_ref), (dk2_ref, dv2_ref), halves(part3_ref))
     places = [(x * 4 + k) * 16 for k in range(4) for x in range(4)]
     lower = (lax.broadcasted_iota(jnp.int32, (ROWS, HEAD_SIZE), 0) // CL % 2 == 0).astype(F32)
     lower, upper = lower.astype(BF16), (1.0 - lower).astype(BF16)
@@ -213,8 +219,8 @@
         for i, p in enumerate(places):
             back_ref[p : p + 16, at : at + 128] = value[i * 16 : (i + 1) * 16]
 
-    def beside(k, at):
-        return jnp.concatenate([kv_refs[k][:, at + m : at + m + 128] for m in (0, 256)], axis=1)
+    def beside(ref, h):
+        return jnp.concatenate([ref[:, m * 128 : (m + 1) * 128] for m in (h, h + 2)], axis=1)
 
     def apart(rows):
         return jnp.concatenate([rows * lower, rows * upper], axis=1)
@@ -237,7 +243,7 @@
         return jnp.concatenate(parts, axis=1)
 
     sides = [
-        ([beside(k, h * 128) for k in range(4)], [beside(k, 512 + h * 128) for k in range(4)])
+        ([beside(refs[0], h) for refs in kv_refs], [beside(refs[1], h) for refs in kv_refs])
         for h in range(2)
     ]
     stats = unpack_stats(load(2 * HALF), 2 * PAIRS)
@@ -287,18 +293,30 @@
             deltas.append(delta)
         for p in range(2):
             at = slice(p * 128, (p + 1) * 128)
-            for first, scale, base in ((0, INV_SQRT, 0), (2, 1.0, 512)):
+            for kind, first, scale in ((0, 0, INV_SQRT), (1, 2, 1.0)):
                 left = jnp.concatenate([d[first][:, at] for d in done], axis=1)
                 right = jnp.concatenate([by_prompt(d[first + 1][at]) for d in done], axis=0)
                 grad = nn(left, right) * scale
                 for k in range(2):
-                    ref = part_refs[2 * p + k]
+                    ref = part_refs[2 * p + k][kind]
                     for i, m in enumerate((h, h + 2)):
                         column = k * 256 + i * 128
-                        ref[:, base + m * 128 : base + (m + 1) * 128] = grad[
-                            :, column : column + 128
-                        ].astype(ref.dtype)
+                        ref[:, m * 128 : (m + 1) * 128] = grad[:, column : column + 128].astype(
+                            ref.dtype
+                        )
+    outs = [
+        (dk2_ref, dk2_hbm), (dv2_ref, dv2_hbm), (part1_ref, part1_hbm), (part3_ref, part3_hbm),
+        (part0_ref, part0_hbm),
+    ]
+    copies = [
+        pltpu.make_async_copy(source, target, sems.at[i])
+        for i, (source, target) in enumerate(outs)
+    ]
+    for copy in copies:
+        copy.start()
     store(HALF, pack_stats(lses + deltas).astype(BF16))
+    for copy in copies:
+        copy.wait()
 
 
 def own_kernel(
@@ -434,7 +452,9 @@
 def call(kernel, in_specs, outs, scratch=(), out_specs=None, vmem_mib=40, cost=None):
     return pl.pallas_call(
         kernel,
-        out_shape=[jax.ShapeDtypeStruct(shape, dtype) for shape, dtype in outs],
+        out_shape=[
+            jax.ShapeDtypeStruct(*out) if len(out) == 2 else out[0](*out[1:]) for out in outs
+        ],
         in_specs=in_specs,
         out_specs=out_specs or [VMEM] * len(outs),
         scratch_shapes=list(scratch),
@@ -466,11 +486,15 @@
 
 
 def run_owner(rows, *prompts):
+    half = (PLEN, KEY_VALUE_HEADS * HEAD_SIZE)
     part = (PLEN, 2 * KEY_VALUE_HEADS * HEAD_SIZE)
+    parts = [(part, F32)] + [(part, BF16)] * 2 + [(half, BF16)] * 2
     return call(
         owner_kernel,
-        [VMEM] * 5,
-        [((ROWS, BACK_WIDTH), BF16), (part, F32)] + [(part, BF16)] * 3,
+        [VMEM] * 6,
+        [((ROWS, BACK_WIDTH), BF16)] + [(pltpu.HBM, *p) for p in parts],
+        [pltpu.VMEM(*p) for p in parts] + [pltpu.SemaphoreType.DMA((5,))],
+        [VMEM] + [HBM] * 5,
     )(rows, *prompts)
 
 
@@ -583,28 +607,33 @@
     hidden = normed_hidden_input[0]
     keys, values = completion_keys[0], completion_values[0]
     prompt = jnp.concatenate([owner_prompt_keys[0], owner_prompt_values[0]], axis=1)
-    prompts = [prompt] + [by_z(prompt, -k) for k in (1, 2, 3)]
+    after, before = by_z(prompt, -1), by_z(prompt, 1)
     z = lax.axis_index("prompt") % 4
     route = route // 4 * 4 + (route - z) % 4
     send = run_prepare(
         adapter_rank, route, lengths, hidden, frozen_query_base[0], attention_output_grad[0],
         keys, values, adapter_down_weight.T, adapter_up_weight,
     )
-    send, prompts[2] = lax.optimization_barrier((send, prompts[2]))
+    send, after, before = lax.optimization_barrier((send, after, before))
     arrived = over_x(send)
-    back, total, *parts = run_owner(arrived.reshape(ROWS, SEND_WIDTH), *prompts)
+    width = KEY_VALUE_HEADS * HEAD_SIZE
+    far = by_z(after[:, :width], -1), by_z(before[:, width:], 1)
+    back, total, to_after, to_before, *far = run_owner(
+        arrived.reshape(ROWS, SEND_WIDTH), prompt, after, before, *far
+    )
     back = over_x(back.reshape(SLOTS, 16, BACK_WIDTH))
-    back, far = lax.optimization_barrier((back, by_z(parts[1], 2)))
+    back, *far = lax.optimization_barrier((back, by_z(far[0], 1), by_z(far[1], -1)))
+    to_after = jnp.concatenate([to_after[:, :width] + far[0], to_after[:, width:]], axis=1)
+    to_before = jnp.concatenate([to_before[:, :width], to_before[:, width:] + far[1]], axis=1)
     core = (lax.axis_index("comp") % 2).astype(jnp.int32)[None]
     own = run_own(adapter_rank, route, core, keys, values, send)
     dq, dsk, dsv, mine, other = run_finish(
         hidden, adapter_up_weight, *own, back.reshape(ROWS, BACK_WIDTH)
     )
-    near = [by_z(parts[0], 1), by_z(parts[2], 3)]
+    near = [by_z(to_after, 1), by_z(to_before, -1)]
     half, other_half, near = sum_all(mine, other, near)
-    for part in [far] + near:
+    for part in near:
         total = total + part.astype(F32)
-    width = KEY_VALUE_HEADS * HEAD_SIZE
     dk, dv = total[:, :width].astype(BF16), total[:, width:].astype(BF16)
     down, up = run_spread(own[-1], half, other_half)
     return dq, dsk, dsv, dk[None], dv[None], down.T, up

time: 133 us -> 127 us (0.955)
  blocking collectives: 23.1 us -> 16.4 us
  waiting for transfers between devices: 42.9 us -> 46.4 us
  starting transfers between devices: 41.3 us -> 39.4 us
    all_to_all x2, waiting for transfers between devices: 0.01 us -> 8.89 us  [over_x(): lax.all_to_all(blocks, 'prompt', 0, 0, axis_index_groups=groups, tiled=True)]
    all_to_all x1, blocking collectives: 23.1 us -> 16.4 us  [sum_all(): total = jnp.sum(swap(pair.reshape(32, rows, 128)).astype(F32), axis=0)]
    ppermute x6 -> x8, waiting for transfers between devices: 34.1 us -> 30.1 us  [by_z(): return lax.ppermute(part, 'prompt', pairs)]
    ppermute x6 -> x8, starting transfers between devices: 20.4 us -> 17 us  [by_z(): return lax.ppermute(part, 'prompt', pairs)]
    ppermute x2, waiting for transfers between devices: 7.24 us -> 5.17 us  [sum_all(): lax.ppermute(total, 'prompt', [(i, flip(i)) for i in range(16)])]
    ppermute x2, starting transfers between devices: 1.74 us -> 3.81 us  [sum_all(): lax.ppermute(total, 'prompt', [(i, flip(i)) for i in range(16)])]
  transfers between devices with their start and end apart: 13 -> 15, of which waited for: 6 -> 13; matrix products, arithmetic and copies ran while one was open for 2% -> 2% of each run, Pallas kernels for 6% -> 6%
where the time goes in v8:
time: 127 us
  waiting for transfers between devices  46.4 us (37%)
  starting transfers between devices  39.4 us (31%)
  Pallas kernels  18.8 us (15%)
  blocking collectives  16.4 us (13%)
  other arithmetic  2.59 us (2%)
  local copies, waits for them, and re-layouts  1.68 us (1%)
  between operations  1.46 us (1%)
    ppermute x8, waiting for transfers between devices, by_z(): return lax.ppermute(part, 'prompt', pairs)  30.1 us
    ppermute x8, starting transfers between devices, by_z(): return lax.ppermute(part, 'prompt', pairs)  17 us
    all_to_all x1, blocking collectives, sum_all(): total = jnp.sum(swap(pair.reshape(32, rows, 128)).astype(F32), axis=0)  16.4 us
    all_to_all x2, waiting for transfers between devices, over_x(): lax.all_to_all(blocks, 'prompt', 0, 0, axis_index_groups=groups, tiled=True)  8.89 us
    all_to_all x2, starting transfers between devices, over_x(): lax.all_to_all(blocks, 'prompt', 0, 0, axis_index_groups=groups, tiled=True)  7.65 us
    ppermute x2, starting transfers between devices, by_core(): return lax.ppermute(part, 'comp', [(i, i ^ 1) for i in range(16)])  6.58 us
    pallas_call x1, Pallas kernels, run_owner(): call(owner_kernel, [VMEM] * 6, [((ROWS, BACK_WIDTH), BF16)] + [(pltpu.HBM...  5.27 us
    pallas_call x1, Pallas kernels, run_prepare(): call(prepare_kernel, [HBM] * len(arrays), [((SLOTS, 16, SEND_WIDTH), BF16...  5.18 us
  transfers between devices with their start and end apart: 15, of which 13 were waited for; matrix products, arithmetic and copies ran while one was open for 2% of the time, Pallas kernels for 6%

profile of v8, /device:TPU:1, one launch (start us, length us, event | category | flops | bytes accessed | tf_op | source)
XLA Modules:
  0.0 126.7 jit_solution(8647476891881078440)
XLA Ops:
  1.6 3.9 %collective-permute-start.1 = (bf16[128,1024]{1,0:T(8,128)(2,1)S(1)}, bf16[128,1024]{1,0:T(8,128)(2,1)S(1)}, u32[]{:S(2)}, u32[]{:S(2)}) collective-permute-start(bf16[128,1024]{1,0:T(8,128)(2,1)S(1)} %pad_maximum_fusion.kv0_ref), channel_id=1, source_target_pairs={{0,16},{16,32},{32,48},{48,0},{64,80},{80,96},{96,112},{112,64},{1... | collective-permute-start | bytes 786440 | tf_op jit(solution)/shard_map/ppermute | solution.py:503
  5.5 3.1 %collective-permute-start = (bf16[128,1024]{1,0:T(8,128)(2,1)S(1)}, bf16[128,1024]{1,0:T(8,128)(2,1)S(1)}, u32[]{:S(2)}, u32[]{:S(2)}) collective-permute-start(bf16[128,1024]{1,0:T(8,128)(2,1)S(1)} %pad_maximum_fusion.kv0_ref), channel_id=1, source_target_pairs={{0,48},{16,0},{32,16},{48,32},{64,112},{80,64},{96,80},{112,96},{1... | collective-permute-start | bytes 786440 | tf_op jit(solution)/shard_map/ppermute | solution.py:503
  10.5 5.2 %shard_map.171.send_hbm = bf16[16,16,2688]{2,1,0:T(8,128)(2,1)} custom-call(s32[1]{0:T(128)S(6)} %copy.19.rank_hbm.rank_ref, s32[1,1,16]{2,1,0:T(1,128)} %fusion.route_hbm.route_ref, s32[1,1,16]{2,1,0:T(1,128)} %length_hbm.1, bf16[128,5120]{1,0:T(8,128)(2,1)} %bitcast.26, bf16[128,2560]{1,0:T(8,128)(2,1)} %bitcast.29, bf16[128,2560]{1,0:T(8,128)(2,1)} %bitcast.30, ...), custom_call_target="tpu_custom_call" | custom-call | flops 1000000000 | bytes 60000000 | tf_op jit(solution)/shard_map/pallas_call | solution.py:473
  16.2 5.5 %collective-permute-done.kv1_ref = bf16[128,1024]{1,0:T(8,128)(2,1)S(1)} collective-permute-done((bf16[128,1024]{1,0:T(8,128)(2,1)S(1)}, bf16[128,1024]{1,0:T(8,128)(2,1)S(1)}, u32[]{:S(2)}, u32[]{:S(2)}) %collective-permute-start) | collective-permute-done | bytes 262176 | tf_op jit(solution)/shard_map/ppermute | solution.py:503
  21.6 4.0 %all-to-all-start = ((bf16[4,64,2688]{2,1,0:T(8,128)(2,1)}), bf16[4,64,2688]{2,1,0:T(8,128)(2,1)S(1)}, u32[]{:S(2)}, u32[]{:S(2)}) async-start(bf16[4,64,2688]{2,1,0:T(8,128)(2,1)} %bitcast.25), calls=%async_computation | async-start | bytes 2752512 | tf_op jit(solution)/shard_map/all_to_all | solution.py:510
  25.7 3.2 %collective-permute-start.3 = (bf16[128,512]{1,0:T(8,128)(2,1)S(1)}, bf16[128,512]{1,0:T(8,128)(2,1)S(1)}, u32[]{:S(2)}, u32[]{:S(2)}) collective-permute-start(bf16[128,512]{1,0:T(8,128)(2,1)S(1)} %slice.27), channel_id=1, source_target_pairs={{0,16},{16,32},{32,48},{48,0},{64,80},{80,96},{96,112},{112,64},{1... | collective-permute-start | bytes 393224 | tf_op jit(solution)/shard_map/ppermute | solution.py:503
  29.3 5.3 %collective-permute-done.3.v2_ref = bf16[128,512]{1,0:T(8,128)(2,1)S(1)} collective-permute-done((bf16[128,512]{1,0:T(8,128)(2,1)S(1)}, bf16[128,512]{1,0:T(8,128)(2,1)S(1)}, u32[]{:S(2)}, u32[]{:S(2)}) %collective-permute-start.3) | collective-permute-done | bytes 131104 | tf_op jit(solution)/shard_map/ppermute | solution.py:503
  34.6 8.5 %all-to-all-done = bf16[4,64,2688]{2,1,0:T(8,128)(2,1)S(1)} async-done(((bf16[4,64,2688]{2,1,0:T(8,128)(2,1)}), bf16[4,64,2688]{2,1,0:T(8,128)(2,1)S(1)}, u32[]{:S(2)}, u32[]{:S(2)}) %all-to-all-start) | async-done | bytes 1376288 | tf_op jit(solution)/shard_map/all_to_all | solution.py:510
  43.0 5.3 %shard_map.173 = (bf16[256,1408]{1,0:T(8,128)(2,1)}, f32[128,1024]{1,0:T(8,128)}, bf16[128,1024]{1,0:T(8,128)(2,1)}, bf16[128,1024]{1,0:T(8,128)(2,1)}, bf16[128...) custom-call(bf16[256,2688]{1,0:T(8,128)(2,1)S(1)} %bitcast.21, bf16[128,1024]{1,0:T(8,128)(2,1)S(1)} %pad_maximum_fusion.kv0_ref, ...), custom_call_target="tpu_custom_call" | custom-call | tf_op jit(solution)/shard_map/pallas_call | solution.py:492
  48.3 3.6 %all-to-all-start.1 = ((bf16[4,64,1408]{2,1,0:T(8,128)(2,1)}), bf16[4,64,1408]{2,1,0:T(8,128)(2,1)S(1)}, u32[]{:S(2)}, u32[]{:S(2)}) async-start(bf16[4,64,1408]{2,1,0:T(8,128)(2,1)} %bitcast.11), calls=%async_computation.1 | async-start | bytes 1441792 | tf_op jit(solution)/shard_map/all_to_all | solution.py:510
  52.0 2.9 %collective-permute-start.4 = (bf16[128,512]{1,0:T(8,128)(2,1)S(1)}, bf16[128,512]{1,0:T(8,128)(2,1)S(1)}, u32[]{:S(2)}, u32[]{:S(2)}) collective-permute-start(bf16[128,512]{1,0:T(8,128)(2,1)S(1)} %copy-done.5), channel_id=1, source_target_pairs={{0,16},{16,32},{32,48},{48,0},{64,80},{80,96},{96,112},{112,64},{1... | collective-permute-start | bytes 393224 | tf_op jit(solution)/shard_map/ppermute | solution.py:503
  55.7 2.2 %shard_map.172 = (bf16[256,2688]{1,0:T(8,128)(2,1)S(1)}, bf16[256,256]{1,0:T(8,128)(2,1)S(1)}, bf16[256,256]{1,0:T(8,128)(2,1)S(1)}, bf16[256,256]{1,0:T(8,128)(2,1)S(1)}, f32[3,64,128]{2,1,0:T(8,128)S(1)}) custom-call(s32[1]{0:T(128)S(6)} %copy.19.rank_hbm.rank_ref, s32[1,1,16]{2,1,0:T(1,128)S(1)} %copy-done, s32[1]{0:T(128)} %bitcast.1.core_ref, ...), custom_call_target="tpu_custom_call" | custom-call | tf_op jit(solution)/shard_map/pallas_call | solution.py:515
  58.7 2.3 %collective-permute-done.5 = bf16[128,512]{1,0:T(8,128)(2,1)S(1)} collective-permute-done((bf16[128,512]{1,0:T(8,128)(2,1)S(1)}, bf16[128,512]{1,0:T(8,128)(2,1)S(1)}, u32[]{:S(2)}, u32[]{:S(2)}) %collective-permute-start.5) | collective-permute-done | bytes 131104 | tf_op jit(solution)/shard_map/ppermute | solution.py:503
  61.4 4.8 %shard_map.174 = (bf16[1,128,2560]{2,1,0:T(8,128)(2,1)}, bf16[1,128,512]{2,1,0:T(8,128)(2,1)}, bf16[1,128,512]{2,1,0:T(8,128)(2,1)}, bf16[2048,128]{1,0:T(8,128)(2,1)S(1)}, bf16[2048,128]{1,0:T(8,128)(2,1)S(1)}) custom-call(bf16[128,5120]{1,0:T(8,128)(2,1)} %bitcast.27, bf16[64,2560]{1,0:T(8,128)(2,1)} %wu_hbm.3, ...), custom_call_target="tpu_custom_call" | custom-call | tf_op jit(solution)/shard_map/pallas_call | solution.py:535
  66.2 3.2 %collective-permute-start.6 = (bf16[2048,128]{1,0:T(8,128)(2,1)S(1)}, bf16[2048,128]{1,0:T(8,128)(2,1)S(1)}, u32[]{:S(2)}, u32[]{:S(2)}) collective-permute-start(bf16[2048,128]{1,0:T(8,128)(2,1)S(1)} %get-tuple-element.51), channel_id=1, source_target_pairs={{0,1},{1,0},{2,3},{3,2},{4,5},{5,4},{6,7},{7,6},{8,9},{9,8},{10,11... | collective-permute-start | bytes 1572872 | tf_op jit(solution)/shard_map/ppermute | solution.py:566
  71.1 16.4 %all_to_all.20 = bf16[32,64,128]{2,1,0:T(8,128)(2,1)S(1)} all-to-all(bf16[32,64,128]{2,1,0:T(8,128)(2,1)S(1)} %bitcast.28), channel_id=1, replica_groups={{0,2,4,6,8,10,12,14,64,66,68,70,72,74,76,78,128,130,132,134,136,138,140..., dimensions={0} | all-to-all | bytes 1048576 | tf_op jit(solution)/shard_map/all_to_all | solution.py:584
  89.2 2.5 %collective-permute-done.7 = f32[64,128]{1,0:T(8,128)S(1)} collective-permute-done((f32[64,128]{1,0:T(8,128)S(1)}, f32[64,128]{1,0:T(8,128)S(1)}, u32[]{:S(2)}, u32[]{:S(2)}) %collective-permute-start.7) | collective-permute-done | bytes 32800 | tf_op jit(solution)/shard_map/ppermute | solution.py:586
  91.7 2.2 %collective-permute-start.8 = (f32[64,128]{1,0:T(8,128)S(1)}, f32[64,128]{1,0:T(8,128)S(1)}, u32[]{:S(2)}, u32[]{:S(2)}) collective-permute-start(f32[64,128]{1,0:T(8,128)S(1)} %add.43), channel_id=1, source_target_pairs={{0,48},{16,32},{32,16},{48,0},{64,112},{80,96},{96,80},{112,64},{1... | collective-permute-start | bytes 98312 | tf_op jit(solution)/shard_map/ppermute | solution.py:586
  93.9 2.7 %collective-permute-done.8 = f32[64,128]{1,0:T(8,128)S(1)} collective-permute-done((f32[64,128]{1,0:T(8,128)S(1)}, f32[64,128]{1,0:T(8,128)S(1)}, u32[]{:S(2)}, u32[]{:S(2)}) %collective-permute-start.8) | collective-permute-done | bytes 32800 | tf_op jit(solution)/shard_map/ppermute | solution.py:586
  97.5 4.3 %all-to-all-start.3 = ((bf16[32,64,128]{2,1,0:T(8,128)(2,1)}), bf16[32,64,128]{2,1,0:T(8,128)(2,1)S(1)}, u32[]{:S(2)}, u32[]{:S(2)}) async-start(bf16[32,64,128]{2,1,0:T(8,128)(2,1)} %broadcast_in_dim.16), calls=%async_computation.3 | async-start | bytes 1048576 | tf_op jit(solution)/shard_map/all_to_all | solution.py:588
  101.9 2.6 %collective-permute-start.10 = (bf16[128,1024]{1,0:T(8,128)(2,1)S(1)}, bf16[128,1024]{1,0:T(8,128)(2,1)S(1)}, u32[]{:S(2)}, u32[]{:S(2)}) collective-permute-start(bf16[128,1024]{1,0:T(8,128)(2,1)S(1)} %pad_maximum_fusion.2), channel_id=1, source_target_pairs={{0,48},{16,0},{32,16},{48,32},{64,112},{80,64},{96,80},{112,96},{1... | collective-permute-start | bytes 786440 | tf_op jit(solution)/shard_map/ppermute | solution.py:503
  104.6 3.6 %collective-permute-done.10 = bf16[128,1024]{1,0:T(8,128)(2,1)S(1)} collective-permute-done((bf16[128,1024]{1,0:T(8,128)(2,1)S(1)}, bf16[128,1024]{1,0:T(8,128)(2,1)S(1)}, u32[]{:S(2)}, u32[]{:S(2)}) %collective-permute-start.10) | collective-permute-done | bytes 262176 | tf_op jit(solution)/shard_map/ppermute | solution.py:503
  108.2 12.2 %collective-permute-done.9 = bf16[128,1024]{1,0:T(8,128)(2,1)S(1)} collective-permute-done((bf16[128,1024]{1,0:T(8,128)(2,1)S(1)}, bf16[128,1024]{1,0:T(8,128)(2,1)S(1)}, u32[]{:S(2)}, u32[]{:S(2)}) %collective-permute-start.9) | collective-permute-done | bytes 262176 | tf_op jit(solution)/shard_map/ppermute | solution.py:503
  120.4 3.4 %collective-permute-start.11 = (bf16[2048,128]{1,0:T(8,128)(2,1)S(1)}, bf16[2048,128]{1,0:T(8,128)(2,1)S(1)}, u32[]{:S(2)}, u32[]{:S(2)}) collective-permute-start(bf16[2048,128]{1,0:T(8,128)(2,1)S(1)} %bitcast.23), channel_id=1, source_target_pairs={{0,1},{1,0},{2,3},{3,2},{4,5},{5,4},{6,7},{7,6},{8,9},{9,8},{10,11... | collective-permute-start | bytes 1572872 | tf_op jit(solution)/shard_map/ppermute | solution.py:566
  (38 shorter events, 12.6 us)
Async XLA Ops:
  1.6 14.5 %collective-permute-start.1 = (bf16[128,1024]{1,0:T(8,128)(2,1)S(1)}, bf16[128,1024]{1,0:T(8,128)(2,1)S(1)}, u32[]{:S(2)}, u32[]{:S(2)}) collective-permute-start(bf16[128,1024]{1,0:T(8,128)(2,1)S(1)} %pad_maximum_fusion.kv0_ref), channel_id=1, source_target_pairs={{0,16},{16,32},{32,48},{48,0},{64,80},{80,96},{96,112},{112,64},{1... | collective-permute-start | bytes 786440 | tf_op jit(solution)/shard_map/ppermute | solution.py:503
  5.5 16.1 %collective-permute-start = (bf16[128,1024]{1,0:T(8,128)(2,1)S(1)}, bf16[128,1024]{1,0:T(8,128)(2,1)S(1)}, u32[]{:S(2)}, u32[]{:S(2)}) collective-permute-start(bf16[128,1024]{1,0:T(8,128)(2,1)S(1)} %pad_maximum_fusion.kv0_ref), channel_id=1, source_target_pairs={{0,48},{16,0},{32,16},{48,32},{64,112},{80,64},{96,80},{112,96},{1... | collective-permute-start | bytes 786440 | tf_op jit(solution)/shard_map/ppermute | solution.py:503
  21.6 21.4 %all-to-all-start = ((bf16[4,64,2688]{2,1,0:T(8,128)(2,1)}), bf16[4,64,2688]{2,1,0:T(8,128)(2,1)S(1)}, u32[]{:S(2)}, u32[]{:S(2)}) async-start(bf16[4,64,2688]{2,1,0:T(8,128)(2,1)} %bitcast.25), calls=%async_computation | async-start | bytes 2752512 | tf_op jit(solution)/shard_map/all_to_all | solution.py:510
  25.7 8.9 %collective-permute-start.3 = (bf16[128,512]{1,0:T(8,128)(2,1)S(1)}, bf16[128,512]{1,0:T(8,128)(2,1)S(1)}, u32[]{:S(2)}, u32[]{:S(2)}) collective-permute-start(bf16[128,512]{1,0:T(8,128)(2,1)S(1)} %slice.27), channel_id=1, source_target_pairs={{0,16},{16,32},{32,48},{48,0},{64,80},{80,96},{96,112},{112,64},{1... | collective-permute-start | bytes 393224 | tf_op jit(solution)/shard_map/ppermute | solution.py:503
  28.9 5.7 %collective-permute-start.2 = (bf16[128,512]{1,0:T(8,128)(2,1)S(1)}, bf16[128,512]{1,0:T(8,128)(2,1)S(1)}, u32[]{:S(2)}, u32[]{:S(2)}) collective-permute-start(bf16[128,512]{1,0:T(8,128)(2,1)S(1)} %slice.26), channel_id=1, source_target_pairs={{0,48},{16,0},{32,16},{48,32},{64,112},{80,64},{96,80},{112,96},{1... | collective-permute-start | bytes 393224 | tf_op jit(solution)/shard_map/ppermute | solution.py:503
  43.0 12.6 %copy-start = (s32[1,1,16]{2,1,0:T(1,128)S(1)}, s32[1,1,16]{2,1,0:T(1,128)}, u32[]{:S(2)}) copy-start(s32[1,1,16]{2,1,0:T(1,128)} %fusion.route_hbm.route_ref) | copy-start | bytes 196
  48.3 3.7 %copy-start.5 = (bf16[128,512]{1,0:T(8,128)(2,1)S(1)}, bf16[128,512]{1,0:T(8,128)(2,1)}, u32[]{:S(2)}) copy-start(bf16[128,512]{1,0:T(8,128)(2,1)} %get-tuple-element.43) | copy-start | bytes 393220
  48.3 6.5 %copy-start.4 = (bf16[128,512]{1,0:T(8,128)(2,1)S(1)}, bf16[128,512]{1,0:T(8,128)(2,1)}, u32[]{:S(2)}) copy-start(bf16[128,512]{1,0:T(8,128)(2,1)} %get-tuple-element.44) | copy-start | bytes 393220
  48.3 13.0 %all-to-all-start.1 = ((bf16[4,64,1408]{2,1,0:T(8,128)(2,1)}), bf16[4,64,1408]{2,1,0:T(8,128)(2,1)S(1)}, u32[]{:S(2)}, u32[]{:S(2)}) async-start(bf16[4,64,1408]{2,1,0:T(8,128)(2,1)} %bitcast.11), calls=%async_computation.1 | async-start | bytes 1441792 | tf_op jit(solution)/shard_map/all_to_all | solution.py:510
  52.0 6.7 %collective-permute-start.4 = (bf16[128,512]{1,0:T(8,128)(2,1)S(1)}, bf16[128,512]{1,0:T(8,128)(2,1)S(1)}, u32[]{:S(2)}, u32[]{:S(2)}) collective-permute-start(bf16[128,512]{1,0:T(8,128)(2,1)S(1)} %copy-done.5), channel_id=1, source_target_pairs={{0,16},{16,32},{32,48},{48,0},{64,80},{80,96},{96,112},{112,64},{1... | collective-permute-start | bytes 393224 | tf_op jit(solution)/shard_map/ppermute | solution.py:503
  54.9 6.1 %collective-permute-start.5 = (bf16[128,512]{1,0:T(8,128)(2,1)S(1)}, bf16[128,512]{1,0:T(8,128)(2,1)S(1)}, u32[]{:S(2)}, u32[]{:S(2)}) collective-permute-start(bf16[128,512]{1,0:T(8,128)(2,1)S(1)} %copy-done.4), channel_id=1, source_target_pairs={{0,48},{16,0},{32,16},{48,32},{64,112},{80,64},{96,80},{112,96},{1... | collective-permute-start | bytes 393224 | tf_op jit(solution)/shard_map/ppermute | solution.py:503
  66.2 4.7 %collective-permute-start.6 = (bf16[2048,128]{1,0:T(8,128)(2,1)S(1)}, bf16[2048,128]{1,0:T(8,128)(2,1)S(1)}, u32[]{:S(2)}, u32[]{:S(2)}) collective-permute-start(bf16[2048,128]{1,0:T(8,128)(2,1)S(1)} %get-tuple-element.51), channel_id=1, source_target_pairs={{0,1},{1,0},{2,3},{3,2},{4,5},{5,4},{6,7},{7,6},{8,9},{9,8},{10,11... | collective-permute-start | bytes 1572872 | tf_op jit(solution)/shard_map/ppermute | solution.py:566
  87.5 14.3 %copy-start.2 = (bf16[128,1024]{1,0:T(8,128)(2,1)S(1)}, bf16[128,1024]{1,0:T(8,128)(2,1)}, u32[]{:S(2)}) copy-start(bf16[128,1024]{1,0:T(8,128)(2,1)} %get-tuple-element.52) | copy-start | bytes 786436
  87.5 14.3 %copy-start.3 = (bf16[128,1024]{1,0:T(8,128)(2,1)S(1)}, bf16[128,1024]{1,0:T(8,128)(2,1)}, u32[]{:S(2)}) copy-start(bf16[128,1024]{1,0:T(8,128)(2,1)} %get-tuple-element.54) | copy-start | bytes 786436
  87.6 4.1 %collective-permute-start.7 = (f32[64,128]{1,0:T(8,128)S(1)}, f32[64,128]{1,0:T(8,128)S(1)}, u32[]{:S(2)}, u32[]{:S(2)}) collective-permute-start(f32[64,128]{1,0:T(8,128)S(1)} %convert_reduce_fusion), channel_id=1, source_target_pairs={{0,16},{16,0},{32,48},{48,32},{64,80},{80,64},{96,112},{112,96},{1... | collective-permute-start | bytes 98312 | tf_op jit(solution)/shard_map/ppermute | solution.py:586
  91.7 4.9 %collective-permute-start.8 = (f32[64,128]{1,0:T(8,128)S(1)}, f32[64,128]{1,0:T(8,128)S(1)}, u32[]{:S(2)}, u32[]{:S(2)}) collective-permute-start(f32[64,128]{1,0:T(8,128)S(1)} %add.43), channel_id=1, source_target_pairs={{0,48},{16,32},{32,16},{48,0},{64,112},{80,96},{96,80},{112,64},{1... | collective-permute-start | bytes 98312 | tf_op jit(solution)/shard_map/ppermute | solution.py:586
  97.5 22.9 %all-to-all-start.3 = ((bf16[32,64,128]{2,1,0:T(8,128)(2,1)}), bf16[32,64,128]{2,1,0:T(8,128)(2,1)S(1)}, u32[]{:S(2)}, u32[]{:S(2)}) async-start(bf16[32,64,128]{2,1,0:T(8,128)(2,1)} %broadcast_in_dim.16), calls=%async_computation.3 | async-start | bytes 1048576 | tf_op jit(solution)/shard_map/all_to_all | solution.py:588
  101.8 22.0 %copy-start.1 = (f32[128,1024]{1,0:T(8,128)S(1)}, f32[128,1024]{1,0:T(8,128)}, u32[]{:S(2)}) copy-start(f32[128,1024]{1,0:T(8,128)} %get-tuple-element.49) | copy-start | bytes 1572868
  101.9 6.3 %collective-permute-start.10 = (bf16[128,1024]{1,0:T(8,128)(2,1)S(1)}, bf16[128,1024]{1,0:T(8,128)(2,1)S(1)}, u32[]{:S(2)}, u32[]{:S(2)}) collective-permute-start(bf16[128,1024]{1,0:T(8,128)(2,1)S(1)} %pad_maximum_fusion.2), channel_id=1, source_target_pairs={{0,48},{16,0},{32,16},{48,32},{64,112},{80,64},{96,80},{112,96},{1... | collective-permute-start | bytes 786440 | tf_op jit(solution)/shard_map/ppermute | solution.py:503
  104.6 15.9 %collective-permute-start.9 = (bf16[128,1024]{1,0:T(8,128)(2,1)S(1)}, bf16[128,1024]{1,0:T(8,128)(2,1)S(1)}, u32[]{:S(2)}, u32[]{:S(2)}) collective-permute-start(bf16[128,1024]{1,0:T(8,128)(2,1)S(1)} %pad_maximum_fusion.1), channel_id=1, source_target_pairs={{0,16},{16,32},{32,48},{48,0},{64,80},{80,96},{96,112},{112,64},{1... | collective-permute-start | bytes 786440 | tf_op jit(solution)/shard_map/ppermute | solution.py:503
  120.4 4.9 %collective-permute-start.11 = (bf16[2048,128]{1,0:T(8,128)(2,1)S(1)}, bf16[2048,128]{1,0:T(8,128)(2,1)S(1)}, u32[]{:S(2)}, u32[]{:S(2)}) collective-permute-start(bf16[2048,128]{1,0:T(8,128)(2,1)S(1)} %bitcast.23), channel_id=1, source_target_pairs={{0,1},{1,0},{2,3},{3,2},{4,5},{5,4},{6,7},{7,6},{8,9},{9,8},{10,11... | collective-permute-start | bytes 1572872 | tf_op jit(solution)/shard_map/ppermute | solution.py:566

commit v9 on v8

--- a/solution.py
+++ b/solution.py
@@ -196,7 +196,7 @@
 
 
 def owner_kernel(
-    rows_ref, kv0_ref, kv1_ref, kv3_ref, k2_ref, v2_ref,
+    rows_ref, k0_ref, v0_ref, k1_ref, v1_ref, k2_ref, v2_ref, k3_ref, v3_ref,
     back_ref, part0_hbm, part1_hbm, part3_hbm, dk2_hbm, dv2_hbm,
     part0_ref, part1_ref, part3_ref, dk2_ref, dv2_ref, sems,
 ):
@@ -205,7 +205,7 @@
     def halves(ref):
         return ref.at[:, :width], ref.at[:, width:]
 
-    kv_refs = (halves(kv0_ref), halves(kv1_ref), (k2_ref, v2_ref), halves(kv3_ref))
+    kv_refs = ((k0_ref, v0_ref), (k1_ref, v1_ref), (k2_ref, v2_ref), (k3_ref, v3_ref))
     part_refs = (halves(part0_ref), halves(part1_ref), (dk2_ref, dv2_ref), halves(part3_ref))
     places = [(x * 4 + k) * 16 for k in range(4) for x in range(4)]
     lower = (lax.broadcasted_iota(jnp.int32, (ROWS, HEAD_SIZE), 0) // CL % 2 == 0).astype(F32)
@@ -491,7 +491,7 @@
     parts = [(part, F32)] + [(part, BF16)] * 2 + [(half, BF16)] * 2
     return call(
         owner_kernel,
-        [VMEM] * 6,
+        [VMEM] * 9,
         [((ROWS, BACK_WIDTH), BF16)] + [(pltpu.HBM, *p) for p in parts],
         [pltpu.VMEM(*p) for p in parts] + [pltpu.SemaphoreType.DMA((5,))],
         [VMEM] + [HBM] * 5,
@@ -606,20 +606,21 @@
 ):
     hidden = normed_hidden_input[0]
     keys, values = completion_keys[0], completion_values[0]
-    prompt = jnp.concatenate([owner_prompt_keys[0], owner_prompt_values[0]], axis=1)
-    after, before = by_z(prompt, -1), by_z(prompt, 1)
+    k0, v0 = owner_prompt_keys[0], owner_prompt_values[0]
+    k1, v3 = by_z(k0, -1), by_z(v0, 1)
     z = lax.axis_index("prompt") % 4
     route = route // 4 * 4 + (route - z) % 4
     send = run_prepare(
         adapter_rank, route, lengths, hidden, frozen_query_base[0], attention_output_grad[0],
         keys, values, adapter_down_weight.T, adapter_up_weight,
     )
-    send, after, before = lax.optimization_barrier((send, after, before))
+    send, k1, v3 = lax.optimization_barrier((send, k1, v3))
     arrived = over_x(send)
+    k2, v2 = by_z(k1, -1), by_z(v3, 1)
+    k3, v1 = by_z(k0, 1), by_z(v0, -1)
     width = KEY_VALUE_HEADS * HEAD_SIZE
-    far = by_z(after[:, :width], -1), by_z(before[:, width:], 1)
     back, total, to_after, to_before, *far = run_owner(
-        arrived.reshape(ROWS, SEND_WIDTH), prompt, after, before, *far
+        arrived.reshape(ROWS, SEND_WIDTH), k0, v0, k1, v1, k2, v2, k3, v3
     )
     back = over_x(back.reshape(SLOTS, 16, BACK_WIDTH))
     back, *far = lax.optimization_barrier((back, by_z(far[0], 1), by_z(far[1], -1)))

time: 127 us -> 123 us (0.969)
  waiting for transfers between devices: 46.4 us -> 36.9 us
  starting transfers between devices: 39.4 us -> 43.1 us
  blocking collectives: 16.4 us -> 18.6 us
    all_to_all x2, waiting for transfers between devices: 8.89 us -> 3 us  [over_x(): lax.all_to_all(blocks, 'prompt', 0, 0, axis_index_groups=groups, tiled=True)]
    ppermute x8 -> x10, waiting for transfers between devices: 30.1 us -> 26.6 us  [by_z(): return lax.ppermute(part, 'prompt', pairs)]
    ppermute x8 -> x10, starting transfers between devices: 17 us -> 19.3 us  [by_z(): return lax.ppermute(part, 'prompt', pairs)]
    all_to_all x1, blocking collectives: 16.4 us -> 18.6 us  [sum_all(): total = jnp.sum(swap(pair.reshape(32, rows, 128)).astype(F32), axis=0)]
  transfers between devices with their start and end apart: 15 -> 17, of which waited for: 13 -> 12; matrix products, arithmetic and copies ran while one was open for 2% -> 2% of each run, Pallas kernels for 6% -> 6%
where the time goes in v9:
time: 123 us; the launch traced here: 122 us
  starting transfers between devices  43.1 us (35%)
  waiting for transfers between devices  36.9 us (30%)
  Pallas kernels  18.9 us (15%)
  blocking collectives  18.6 us (15%)
  local copies, waits for them, and re-layouts  1.67 us (1%)
  other arithmetic  1.6 us (1%)
  between operations  1.43 us (1%)
    ppermute x10, waiting for transfers between devices, by_z(): return lax.ppermute(part, 'prompt', pairs)  26.6 us
    ppermute x10, starting transfers between devices, by_z(): return lax.ppermute(part, 'prompt', pairs)  19.3 us
    all_to_all x1, blocking collectives, sum_all(): total = jnp.sum(swap(pair.reshape(32, rows, 128)).astype(F32), axis=0)  18.6 us
    all_to_all x2, starting transfers between devices, over_x(): lax.all_to_all(blocks, 'prompt', 0, 0, axis_index_groups=groups, tiled=True)  8.57 us
    ppermute x2, starting transfers between devices, by_core(): return lax.ppermute(part, 'comp', [(i, i ^ 1) for i in range(16)])  6.94 us
    pallas_call x1, Pallas kernels, run_owner(): call(owner_kernel, [VMEM] * 9, [((ROWS, BACK_WIDTH), BF16)] + [(pltpu.HBM...  5.29 us
    pallas_call x1, Pallas kernels, run_prepare(): call(prepare_kernel, [HBM] * len(arrays), [((SLOTS, 16, SEND_WIDTH), BF16...  5.23 us
    ppermute x2, waiting for transfers between devices, sum_all(): lax.ppermute(total, 'prompt', [(i, flip(i)) for i in range(16)])  5.06 us
  transfers between devices with their start and end apart: 17, of which 12 were waited for; matrix products, arithmetic and copies ran while one was open for 2% of the time, Pallas kernels for 6%

profile of v9, /device:TPU:1, one launch (start us, length us, event | category | flops | bytes accessed | tf_op | source)
XLA Modules:
  0.0 122.2 jit_solution(14615647481480837203)
XLA Ops:
  0.6 6.9 %collective-permute-start = (bf16[128,512]{1,0:T(8,128)(2,1)}, bf16[128,512]{1,0:T(8,128)(2,1)S(1)}, u32[]{:S(2)}, u32[]{:S(2)}) collective-permute-start(bf16[128,512]{1,0:T(8,128)(2,1)} %bitcast.25), channel_id=1, source_target_pairs={{0,48},{16,0},{32,16},{48,32},{64,112},{80,64},{96,80},{112,96},{1... | collective-permute-start | bytes 393224 | tf_op jit(solution)/shard_map/ppermute | solution.py:503
  9.4 5.2 %shard_map.171.send_hbm = bf16[16,16,2688]{2,1,0:T(8,128)(2,1)} custom-call(s32[1]{0:T(128)S(6)} %copy.19.rank_hbm.rank_ref, s32[1,1,16]{2,1,0:T(1,128)} %fusion.route_hbm.route_ref, s32[1,1,16]{2,1,0:T(1,128)} %length_hbm.1, bf16[128,5120]{1,0:T(8,128)(2,1)} %bitcast.32, bf16[128,2560]{1,0:T(8,128)(2,1)} %bitcast.35, bf16[128,2560]{1,0:T(8,128)(2,1)} %bitcast.36, ...), custom_call_target="tpu_custom_call" | custom-call | flops 1000000000 | bytes 60000000 | tf_op jit(solution)/shard_map/pallas_call | solution.py:473
  15.0 4.1 %all-to-all-start = ((bf16[4,64,2688]{2,1,0:T(8,128)(2,1)}), bf16[4,64,2688]{2,1,0:T(8,128)(2,1)S(1)}, u32[]{:S(2)}, u32[]{:S(2)}) async-start(bf16[4,64,2688]{2,1,0:T(8,128)(2,1)} %bitcast.31), calls=%async_computation | async-start | bytes 2752512 | tf_op jit(solution)/shard_map/all_to_all | solution.py:510
  20.1 2.7 %collective-permute-start.2 = (bf16[128,512]{1,0:T(8,128)(2,1)S(1)}, bf16[128,512]{1,0:T(8,128)(2,1)S(1)}, u32[]{:S(2)}, u32[]{:S(2)}) collective-permute-start(bf16[128,512]{1,0:T(8,128)(2,1)S(1)} %bitcast.29), channel_id=1, source_target_pairs={{0,48},{16,0},{32,16},{48,32},{64,112},{80,64},{96,80},{112,96},{1... | collective-permute-start | bytes 393224 | tf_op jit(solution)/shard_map/ppermute | solution.py:503
  22.8 2.0 %collective-permute-start.3 = (bf16[128,512]{1,0:T(8,128)(2,1)S(1)}, bf16[128,512]{1,0:T(8,128)(2,1)S(1)}, u32[]{:S(2)}, u32[]{:S(2)}) collective-permute-start(bf16[128,512]{1,0:T(8,128)(2,1)S(1)} %collective-permute-done.k1_ref), channel_id=1, source_target_pairs={{0,48},{16,0},{32,16},{48,32},{64,112},{80,64},{96,80},{112,96},{1... | collective-permute-start | bytes 393224 | tf_op jit(solution)/shard_map/ppermute | solution.py:503
  25.6 4.9 %collective-permute-done.3.k2_ref = bf16[128,512]{1,0:T(8,128)(2,1)S(1)} collective-permute-done((bf16[128,512]{1,0:T(8,128)(2,1)S(1)}, bf16[128,512]{1,0:T(8,128)(2,1)S(1)}, u32[]{:S(2)}, u32[]{:S(2)}) %collective-permute-start.3) | collective-permute-done | bytes 131104 | tf_op jit(solution)/shard_map/ppermute | solution.py:503
  30.5 4.9 %collective-permute-done.4.v2_ref = bf16[128,512]{1,0:T(8,128)(2,1)S(1)} collective-permute-done((bf16[128,512]{1,0:T(8,128)(2,1)S(1)}, bf16[128,512]{1,0:T(8,128)(2,1)S(1)}, u32[]{:S(2)}, u32[]{:S(2)}) %collective-permute-start.4) | collective-permute-done | bytes 131104 | tf_op jit(solution)/shard_map/ppermute | solution.py:503
  35.4 5.3 %shard_map.173 = (bf16[256,1408]{1,0:T(8,128)(2,1)}, f32[128,1024]{1,0:T(8,128)}, bf16[128,1024]{1,0:T(8,128)(2,1)}, bf16[128,1024]{1,0:T(8,128)(2,1)}, bf16[128...) custom-call(bf16[256,2688]{1,0:T(8,128)(2,1)S(1)} %bitcast.21, bf16[128,512]{1,0:T(8,128)(2,1)S(1)} %bitcast.27, ...), custom_call_target="tpu_custom_call" | custom-call | tf_op jit(solution)/shard_map/pallas_call | solution.py:492
  40.7 4.4 %all-to-all-start.1 = ((bf16[4,64,1408]{2,1,0:T(8,128)(2,1)}), bf16[4,64,1408]{2,1,0:T(8,128)(2,1)S(1)}, u32[]{:S(2)}, u32[]{:S(2)}) async-start(bf16[4,64,1408]{2,1,0:T(8,128)(2,1)} %bitcast.11), calls=%async_computation.1 | async-start | bytes 1441792 | tf_op jit(solution)/shard_map/all_to_all | solution.py:510
  46.5 2.3 %collective-permute-start.7 = (bf16[128,512]{1,0:T(8,128)(2,1)S(1)}, bf16[128,512]{1,0:T(8,128)(2,1)S(1)}, u32[]{:S(2)}, u32[]{:S(2)}) collective-permute-start(bf16[128,512]{1,0:T(8,128)(2,1)S(1)} %copy-done.6), channel_id=1, source_target_pairs={{0,48},{16,0},{32,16},{48,32},{64,112},{80,64},{96,80},{112,96},{1... | collective-permute-start | bytes 393224 | tf_op jit(solution)/shard_map/ppermute | solution.py:503
  48.8 2.2 %shard_map.172 = (bf16[256,2688]{1,0:T(8,128)(2,1)S(1)}, bf16[256,256]{1,0:T(8,128)(2,1)S(1)}, bf16[256,256]{1,0:T(8,128)(2,1)S(1)}, bf16[256,256]{1,0:T(8,128)(2,1)S(1)}, f32[3,64,128]{2,1,0:T(8,128)S(1)}) custom-call(s32[1]{0:T(128)S(6)} %copy.19.rank_hbm.rank_ref, s32[1,1,16]{2,1,0:T(1,128)S(1)} %copy-done.2, s32[1]{0:T(128)} %bitcast.1.core_ref, ...), custom_call_target="tpu_custom_call" | custom-call | tf_op jit(solution)/shard_map/pallas_call | solution.py:515
  51.3 3.0 %all-to-all-done.1 = bf16[4,64,1408]{2,1,0:T(8,128)(2,1)S(1)} async-done(((bf16[4,64,1408]{2,1,0:T(8,128)(2,1)}), bf16[4,64,1408]{2,1,0:T(8,128)(2,1)S(1)}, u32[]{:S(2)}, u32[]{:S(2)}) %all-to-all-start.1) | async-done | bytes 720928 | tf_op jit(solution)/shard_map/all_to_all | solution.py:510
  54.3 4.8 %shard_map.174 = (bf16[1,128,2560]{2,1,0:T(8,128)(2,1)}, bf16[1,128,512]{2,1,0:T(8,128)(2,1)}, bf16[1,128,512]{2,1,0:T(8,128)(2,1)}, bf16[2048,128]{1,0:T(8,128)(2,1)S(1)}, bf16[2048,128]{1,0:T(8,128)(2,1)S(1)}) custom-call(bf16[128,5120]{1,0:T(8,128)(2,1)} %bitcast.33, bf16[64,2560]{1,0:T(8,128)(2,1)} %wu_hbm.3, ...), custom_call_target="tpu_custom_call" | custom-call | tf_op jit(solution)/shard_map/pallas_call | solution.py:535
  59.1 3.5 %collective-permute-start.8 = (bf16[2048,128]{1,0:T(8,128)(2,1)S(1)}, bf16[2048,128]{1,0:T(8,128)(2,1)S(1)}, u32[]{:S(2)}, u32[]{:S(2)}) collective-permute-start(bf16[2048,128]{1,0:T(8,128)(2,1)S(1)} %get-tuple-element.51), channel_id=1, source_target_pairs={{0,1},{1,0},{2,3},{3,2},{4,5},{5,4},{6,7},{7,6},{8,9},{9,8},{10,11... | collective-permute-start | bytes 1572872 | tf_op jit(solution)/shard_map/ppermute | solution.py:566
  64.3 18.6 %all_to_all.20 = bf16[32,64,128]{2,1,0:T(8,128)(2,1)S(1)} all-to-all(bf16[32,64,128]{2,1,0:T(8,128)(2,1)S(1)} %bitcast.34), channel_id=1, replica_groups={{0,2,4,6,8,10,12,14,64,66,68,70,72,74,76,78,128,130,132,134,136,138,140..., dimensions={0} | all-to-all | bytes 1048576 | tf_op jit(solution)/shard_map/all_to_all | solution.py:584
  83.0 1.6 %collective-permute-start.9 = (f32[64,128]{1,0:T(8,128)S(1)}, f32[64,128]{1,0:T(8,128)S(1)}, u32[]{:S(2)}, u32[]{:S(2)}) collective-permute-start(f32[64,128]{1,0:T(8,128)S(1)} %convert_reduce_fusion), channel_id=1, source_target_pairs={{0,16},{16,0},{32,48},{48,32},{64,80},{80,64},{96,112},{112,96},{1... | collective-permute-start | bytes 98312 | tf_op jit(solution)/shard_map/ppermute | solution.py:586
  84.6 2.5 %collective-permute-done.9 = f32[64,128]{1,0:T(8,128)S(1)} collective-permute-done((f32[64,128]{1,0:T(8,128)S(1)}, f32[64,128]{1,0:T(8,128)S(1)}, u32[]{:S(2)}, u32[]{:S(2)}) %collective-permute-start.9) | collective-permute-done | bytes 32800 | tf_op jit(solution)/shard_map/ppermute | solution.py:586
  87.1 2.3 %collective-permute-start.10 = (f32[64,128]{1,0:T(8,128)S(1)}, f32[64,128]{1,0:T(8,128)S(1)}, u32[]{:S(2)}, u32[]{:S(2)}) collective-permute-start(f32[64,128]{1,0:T(8,128)S(1)} %add.43), channel_id=1, source_target_pairs={{0,48},{16,32},{32,16},{48,0},{64,112},{80,96},{96,80},{112,64},{1... | collective-permute-start | bytes 98312 | tf_op jit(solution)/shard_map/ppermute | solution.py:586
  89.4 2.6 %collective-permute-done.10 = f32[64,128]{1,0:T(8,128)S(1)} collective-permute-done((f32[64,128]{1,0:T(8,128)S(1)}, f32[64,128]{1,0:T(8,128)S(1)}, u32[]{:S(2)}, u32[]{:S(2)}) %collective-permute-start.10) | collective-permute-done | bytes 32800 | tf_op jit(solution)/shard_map/ppermute | solution.py:586
  92.9 4.3 %all-to-all-start.3 = ((bf16[32,64,128]{2,1,0:T(8,128)(2,1)}), bf16[32,64,128]{2,1,0:T(8,128)(2,1)S(1)}, u32[]{:S(2)}, u32[]{:S(2)}) async-start(bf16[32,64,128]{2,1,0:T(8,128)(2,1)} %broadcast_in_dim.16), calls=%async_computation.3 | async-start | bytes 1048576 | tf_op jit(solution)/shard_map/all_to_all | solution.py:588
  97.3 2.7 %collective-permute-start.12 = (bf16[128,1024]{1,0:T(8,128)(2,1)S(1)}, bf16[128,1024]{1,0:T(8,128)(2,1)S(1)}, u32[]{:S(2)}, u32[]{:S(2)}) collective-permute-start(bf16[128,1024]{1,0:T(8,128)(2,1)S(1)} %pad_maximum_fusion.1), channel_id=1, source_target_pairs={{0,48},{16,0},{32,16},{48,32},{64,112},{80,64},{96,80},{112,96},{1... | collective-permute-start | bytes 786440 | tf_op jit(solution)/shard_map/ppermute | solution.py:503
  100.2 3.5 %collective-permute-done.12 = bf16[128,1024]{1,0:T(8,128)(2,1)S(1)} collective-permute-done((bf16[128,1024]{1,0:T(8,128)(2,1)S(1)}, bf16[128,1024]{1,0:T(8,128)(2,1)S(1)}, u32[]{:S(2)}, u32[]{:S(2)}) %collective-permute-start.12) | collective-permute-done | bytes 262176 | tf_op jit(solution)/shard_map/ppermute | solution.py:503
  103.6 12.3 %collective-permute-done.11 = bf16[128,1024]{1,0:T(8,128)(2,1)S(1)} collective-permute-done((bf16[128,1024]{1,0:T(8,128)(2,1)S(1)}, bf16[128,1024]{1,0:T(8,128)(2,1)S(1)}, u32[]{:S(2)}, u32[]{:S(2)}) %collective-permute-start.11) | collective-permute-done | bytes 262176 | tf_op jit(solution)/shard_map/ppermute | solution.py:503
  115.9 3.4 %collective-permute-start.13 = (bf16[2048,128]{1,0:T(8,128)(2,1)S(1)}, bf16[2048,128]{1,0:T(8,128)(2,1)S(1)}, u32[]{:S(2)}, u32[]{:S(2)}) collective-permute-start(bf16[2048,128]{1,0:T(8,128)(2,1)S(1)} %bitcast.23), channel_id=1, source_target_pairs={{0,1},{1,0},{2,3},{3,2},{4,5},{5,4},{6,7},{7,6},{8,9},{9,8},{10,11... | collective-permute-start | bytes 1572872 | tf_op jit(solution)/shard_map/ppermute | solution.py:566
  (43 shorter events, 10.8 us)
Async XLA Ops:
  0.6 14.0 %collective-permute-start = (bf16[128,512]{1,0:T(8,128)(2,1)}, bf16[128,512]{1,0:T(8,128)(2,1)S(1)}, u32[]{:S(2)}, u32[]{:S(2)}) collective-permute-start(bf16[128,512]{1,0:T(8,128)(2,1)} %bitcast.25), channel_id=1, source_target_pairs={{0,48},{16,0},{32,16},{48,32},{64,112},{80,64},{96,80},{112,96},{1... | collective-permute-start | bytes 393224 | tf_op jit(solution)/shard_map/ppermute | solution.py:503
  7.6 7.5 %collective-permute-start.1 = (bf16[128,512]{1,0:T(8,128)(2,1)}, bf16[128,512]{1,0:T(8,128)(2,1)S(1)}, u32[]{:S(2)}, u32[]{:S(2)}) collective-permute-start(bf16[128,512]{1,0:T(8,128)(2,1)} %bitcast.28), channel_id=1, source_target_pairs={{0,16},{16,32},{32,48},{48,0},{64,80},{80,96},{96,112},{112,64},{1... | collective-permute-start | bytes 393224 | tf_op jit(solution)/shard_map/ppermute | solution.py:503
  15.0 5.1 %copy-start.1 = (bf16[1,128,512]{2,1,0:T(8,128)(2,1)S(1)}, bf16[1,128,512]{2,1,0:T(8,128)(2,1)}, u32[]{:S(2)}) copy-start(bf16[1,128,512]{2,1,0:T(8,128)(2,1)} %param.18) | copy-start | bytes 393220
  15.0 20.4 %all-to-all-start = ((bf16[4,64,2688]{2,1,0:T(8,128)(2,1)}), bf16[4,64,2688]{2,1,0:T(8,128)(2,1)S(1)}, u32[]{:S(2)}, u32[]{:S(2)}) async-start(bf16[4,64,2688]{2,1,0:T(8,128)(2,1)} %bitcast.31), calls=%async_computation | async-start | bytes 2752512 | tf_op jit(solution)/shard_map/all_to_all | solution.py:510
  19.2 6.5 %collective-permute-start.5 = (bf16[128,512]{1,0:T(8,128)(2,1)S(1)}, bf16[128,512]{1,0:T(8,128)(2,1)S(1)}, u32[]{:S(2)}, u32[]{:S(2)}) collective-permute-start(bf16[128,512]{1,0:T(8,128)(2,1)S(1)} %bitcast.26), channel_id=1, source_target_pairs={{0,16},{16,32},{32,48},{48,0},{64,80},{80,96},{96,112},{112,64},{1... | collective-permute-start | bytes 393224 | tf_op jit(solution)/shard_map/ppermute | solution.py:503
  20.1 5.5 %collective-permute-start.2 = (bf16[128,512]{1,0:T(8,128)(2,1)S(1)}, bf16[128,512]{1,0:T(8,128)(2,1)S(1)}, u32[]{:S(2)}, u32[]{:S(2)}) collective-permute-start(bf16[128,512]{1,0:T(8,128)(2,1)S(1)} %bitcast.29), channel_id=1, source_target_pairs={{0,48},{16,0},{32,16},{48,32},{64,112},{80,64},{96,80},{112,96},{1... | collective-permute-start | bytes 393224 | tf_op jit(solution)/shard_map/ppermute | solution.py:503
  22.8 7.8 %collective-permute-start.3 = (bf16[128,512]{1,0:T(8,128)(2,1)S(1)}, bf16[128,512]{1,0:T(8,128)(2,1)S(1)}, u32[]{:S(2)}, u32[]{:S(2)}) collective-permute-start(bf16[128,512]{1,0:T(8,128)(2,1)S(1)} %collective-permute-done.k1_ref), channel_id=1, source_target_pairs={{0,48},{16,0},{32,16},{48,32},{64,112},{80,64},{96,80},{112,96},{1... | collective-permute-start | bytes 393224 | tf_op jit(solution)/shard_map/ppermute | solution.py:503
  24.8 10.6 %collective-permute-start.4 = (bf16[128,512]{1,0:T(8,128)(2,1)S(1)}, bf16[128,512]{1,0:T(8,128)(2,1)S(1)}, u32[]{:S(2)}, u32[]{:S(2)}) collective-permute-start(bf16[128,512]{1,0:T(8,128)(2,1)S(1)} %collective-permute-done.1.v3_ref), channel_id=1, source_target_pairs={{0,16},{16,32},{32,48},{48,0},{64,80},{80,96},{96,112},{112,64},{1... | collective-permute-start | bytes 393224 | tf_op jit(solution)/shard_map/ppermute | solution.py:503
  35.4 13.4 %copy-start.2 = (s32[1,1,16]{2,1,0:T(1,128)S(1)}, s32[1,1,16]{2,1,0:T(1,128)}, u32[]{:S(2)}) copy-start(s32[1,1,16]{2,1,0:T(1,128)} %fusion.route_hbm.route_ref) | copy-start | bytes 196
  40.7 4.4 %copy-start.7 = (bf16[128,512]{1,0:T(8,128)(2,1)S(1)}, bf16[128,512]{1,0:T(8,128)(2,1)}, u32[]{:S(2)}) copy-start(bf16[128,512]{1,0:T(8,128)(2,1)} %get-tuple-element.43) | copy-start | bytes 393220
  40.7 5.8 %copy-start.6 = (bf16[128,512]{1,0:T(8,128)(2,1)S(1)}, bf16[128,512]{1,0:T(8,128)(2,1)}, u32[]{:S(2)}) copy-start(bf16[128,512]{1,0:T(8,128)(2,1)} %get-tuple-element.44) | copy-start | bytes 393220
  40.7 13.5 %all-to-all-start.1 = ((bf16[4,64,1408]{2,1,0:T(8,128)(2,1)}), bf16[4,64,1408]{2,1,0:T(8,128)(2,1)S(1)}, u32[]{:S(2)}, u32[]{:S(2)}) async-start(bf16[4,64,1408]{2,1,0:T(8,128)(2,1)} %bitcast.11), calls=%async_computation.1 | async-start | bytes 1441792 | tf_op jit(solution)/shard_map/all_to_all | solution.py:510
  45.2 5.9 %collective-permute-start.6 = (bf16[128,512]{1,0:T(8,128)(2,1)S(1)}, bf16[128,512]{1,0:T(8,128)(2,1)S(1)}, u32[]{:S(2)}, u32[]{:S(2)}) collective-permute-start(bf16[128,512]{1,0:T(8,128)(2,1)S(1)} %copy-done.7), channel_id=1, source_target_pairs={{0,16},{16,32},{32,48},{48,0},{64,80},{80,96},{96,112},{112,64},{1... | collective-permute-start | bytes 393224 | tf_op jit(solution)/shard_map/ppermute | solution.py:503
  46.5 4.7 %collective-permute-start.7 = (bf16[128,512]{1,0:T(8,128)(2,1)S(1)}, bf16[128,512]{1,0:T(8,128)(2,1)S(1)}, u32[]{:S(2)}, u32[]{:S(2)}) collective-permute-start(bf16[128,512]{1,0:T(8,128)(2,1)S(1)} %copy-done.6), channel_id=1, source_target_pairs={{0,48},{16,0},{32,16},{48,32},{64,112},{80,64},{96,80},{112,96},{1... | collective-permute-start | bytes 393224 | tf_op jit(solution)/shard_map/ppermute | solution.py:503
  59.1 5.1 %collective-permute-start.8 = (bf16[2048,128]{1,0:T(8,128)(2,1)S(1)}, bf16[2048,128]{1,0:T(8,128)(2,1)S(1)}, u32[]{:S(2)}, u32[]{:S(2)}) collective-permute-start(bf16[2048,128]{1,0:T(8,128)(2,1)S(1)} %get-tuple-element.51), channel_id=1, source_target_pairs={{0,1},{1,0},{2,3},{3,2},{4,5},{5,4},{6,7},{7,6},{8,9},{9,8},{10,11... | collective-permute-start | bytes 1572872 | tf_op jit(solution)/shard_map/ppermute | solution.py:566
  82.9 14.3 %copy-start.4 = (bf16[128,1024]{1,0:T(8,128)(2,1)S(1)}, bf16[128,1024]{1,0:T(8,128)(2,1)}, u32[]{:S(2)}) copy-start(bf16[128,1024]{1,0:T(8,128)(2,1)} %get-tuple-element.52) | copy-start | bytes 786436
  82.9 14.3 %copy-start.5 = (bf16[128,1024]{1,0:T(8,128)(2,1)S(1)}, bf16[128,1024]{1,0:T(8,128)(2,1)}, u32[]{:S(2)}) copy-start(bf16[128,1024]{1,0:T(8,128)(2,1)} %get-tuple-element.54) | copy-start | bytes 786436
  83.0 4.1 %collective-permute-start.9 = (f32[64,128]{1,0:T(8,128)S(1)}, f32[64,128]{1,0:T(8,128)S(1)}, u32[]{:S(2)}, u32[]{:S(2)}) collective-permute-start(f32[64,128]{1,0:T(8,128)S(1)} %convert_reduce_fusion), channel_id=1, source_target_pairs={{0,16},{16,0},{32,48},{48,32},{64,80},{80,64},{96,112},{112,96},{1... | collective-permute-start | bytes 98312 | tf_op jit(solution)/shard_map/ppermute | solution.py:586
  87.1 4.9 %collective-permute-start.10 = (f32[64,128]{1,0:T(8,128)S(1)}, f32[64,128]{1,0:T(8,128)S(1)}, u32[]{:S(2)}, u32[]{:S(2)}) collective-permute-start(f32[64,128]{1,0:T(8,128)S(1)} %add.43), channel_id=1, source_target_pairs={{0,48},{16,32},{32,16},{48,0},{64,112},{80,96},{96,80},{112,64},{1... | collective-permute-start | bytes 98312 | tf_op jit(solution)/shard_map/ppermute | solution.py:586
  92.9 23.0 %all-to-all-start.3 = ((bf16[32,64,128]{2,1,0:T(8,128)(2,1)}), bf16[32,64,128]{2,1,0:T(8,128)(2,1)S(1)}, u32[]{:S(2)}, u32[]{:S(2)}) async-start(bf16[32,64,128]{2,1,0:T(8,128)(2,1)} %broadcast_in_dim.16), calls=%async_computation.3 | async-start | bytes 1048576 | tf_op jit(solution)/shard_map/all_to_all | solution.py:588
  97.2 22.1 %copy-start.3 = (f32[128,1024]{1,0:T(8,128)S(1)}, f32[128,1024]{1,0:T(8,128)}, u32[]{:S(2)}) copy-start(f32[128,1024]{1,0:T(8,128)} %get-tuple-element.49) | copy-start | bytes 1572868
  97.3 6.3 %collective-permute-start.12 = (bf16[128,1024]{1,0:T(8,128)(2,1)S(1)}, bf16[128,1024]{1,0:T(8,128)(2,1)S(1)}, u32[]{:S(2)}, u32[]{:S(2)}) collective-permute-start(bf16[128,1024]{1,0:T(8,128)(2,1)S(1)} %pad_maximum_fusion.1), channel_id=1, source_target_pairs={{0,48},{16,0},{32,16},{48,32},{64,112},{80,64},{96,80},{112,96},{1... | collective-permute-start | bytes 786440 | tf_op jit(solution)/shard_map/ppermute | solution.py:503
  100.1 15.8 %collective-permute-start.11 = (bf16[128,1024]{1,0:T(8,128)(2,1)S(1)}, bf16[128,1024]{1,0:T(8,128)(2,1)S(1)}, u32[]{:S(2)}, u32[]{:S(2)}) collective-permute-start(bf16[128,1024]{1,0:T(8,128)(2,1)S(1)} %pad_maximum_fusion), channel_id=1, source_target_pairs={{0,16},{16,32},{32,48},{48,0},{64,80},{80,96},{96,112},{112,64},{1... | collective-permute-start | bytes 786440 | tf_op jit(solution)/shard_map/ppermute | solution.py:503
  115.9 4.9 %collective-permute-start.13 = (bf16[2048,128]{1,0:T(8,128)(2,1)S(1)}, bf16[2048,128]{1,0:T(8,128)(2,1)S(1)}, u32[]{:S(2)}, u32[]{:S(2)}) collective-permute-start(bf16[2048,128]{1,0:T(8,128)(2,1)S(1)} %bitcast.23), channel_id=1, source_target_pairs={{0,1},{1,0},{2,3},{3,2},{4,5},{5,4},{6,7},{7,6},{8,9},{9,8},{10,11... | collective-permute-start | bytes 1572872 | tf_op jit(solution)/shard_map/ppermute | solution.py:566
  (1 other events, 4.2 us)

commit v10 on v9

--- a/solution.py
+++ b/solution.py
@@ -197,8 +197,8 @@
 
 def owner_kernel(
     rows_ref, k0_ref, v0_ref, k1_ref, v1_ref, k2_ref, v2_ref, k3_ref, v3_ref,
-    back_ref, part0_hbm, part1_hbm, part3_hbm, dk2_hbm, dv2_hbm,
-    part0_ref, part1_ref, part3_ref, dk2_ref, dv2_ref, sems,
+    back_hbm, part0_hbm, part1_hbm, part3_hbm, dk2_hbm, dv2_hbm,
+    back_ref, part0_ref, part1_ref, part3_ref, dk2_ref, dv2_ref, sems,
 ):
     width = KEY_VALUE_HEADS * HEAD_SIZE
 
@@ -291,6 +291,10 @@
             done.append((dscore, q, probs_b, g))
             lses.append(lse)
             deltas.append(delta)
+        if h == 0:
+            ahead = pl.ds(0, HALF // 2)
+            early = pltpu.make_async_copy(back_ref.at[:, ahead], back_hbm.at[:, ahead], sems.at[5])
+            early.start()
         for p in range(2):
             at = slice(p * 128, (p + 1) * 128)
             for kind, first, scale in ((0, 0, INV_SQRT), (1, 2, 1.0)):
@@ -315,6 +319,12 @@
     for copy in copies:
         copy.start()
     store(HALF, pack_stats(lses + deltas).astype(BF16))
+    last = pl.ds(HALF // 2, BACK_WIDTH - HALF // 2)
+    copies += [
+        early,
+        pltpu.make_async_copy(back_ref.at[:, last], back_hbm.at[:, last], sems.at[6]),
+    ]
+    copies[-1].start()
     for copy in copies:
         copy.wait()
 
@@ -488,13 +498,13 @@
 def run_owner(rows, *prompts):
     half = (PLEN, KEY_VALUE_HEADS * HEAD_SIZE)
     part = (PLEN, 2 * KEY_VALUE_HEADS * HEAD_SIZE)
-    parts = [(part, F32)] + [(part, BF16)] * 2 + [(half, BF16)] * 2
+    parts = [((ROWS, BACK_WIDTH), BF16), (part, F32)] + [(part, BF16)] * 2 + [(half, BF16)] * 2
     return call(
         owner_kernel,
         [VMEM] * 9,
-        [((ROWS, BACK_WIDTH), BF16)] + [(pltpu.HBM, *p) for p in parts],
-        [pltpu.VMEM(*p) for p in parts] + [pltpu.SemaphoreType.DMA((5,))],
-        [VMEM] + [HBM] * 5,
+        [(pltpu.HBM, *p) for p in parts],
+        [pltpu.VMEM(*p) for p in parts] + [pltpu.SemaphoreType.DMA((7,))],
+        [HBM] * 6,
     )(rows, *prompts)
 
 

time: 123 us -> 122 us (level)
  transfers between devices with their start and end apart: 17 -> 17, of which waited for: 12 -> 11; matrix products, arithmetic and copies ran while one was open for 2% -> 2% of each run, Pallas kernels for 6% -> 6%
where the time goes in v10:
time: 122 us
  starting transfers between devices  43 us (35%)
  waiting for transfers between devices  36.9 us (30%)
  blocking collectives  18.6 us (15%)
  Pallas kernels  18.2 us (15%)
  local copies, waits for them, and re-layouts  1.67 us (1%)
  other arithmetic  1.6 us (1%)
  between operations  1.43 us (1%)
    ppermute x10, waiting for transfers between devices, by_z(): return lax.ppermute(part, 'prompt', pairs)  26.6 us
    ppermute x10, starting transfers between devices, by_z(): return lax.ppermute(part, 'prompt', pairs)  19.3 us
    all_to_all x1, blocking collectives, sum_all(): total = jnp.sum(swap(pair.reshape(32, rows, 128)).astype(F32), axis=0)  18.6 us
    all_to_all x2, starting transfers between devices, over_x(): lax.all_to_all(blocks, 'prompt', 0, 0, axis_index_groups=groups, tiled=True)  8.55 us
    ppermute x2, starting transfers between devices, by_core(): return lax.ppermute(part, 'comp', [(i, i ^ 1) for i in range(16)])  6.93 us
    pallas_call x1, Pallas kernels, run_prepare(): call(prepare_kernel, [HBM] * len(arrays), [((SLOTS, 16, SEND_WIDTH), BF16...  5.24 us
    ppermute x2, waiting for transfers between devices, sum_all(): lax.ppermute(total, 'prompt', [(i, flip(i)) for i in range(16)])  5.09 us
    pallas_call x1, Pallas kernels, run_finish(): call(finish_kernel, [HBM] * 2 + [VMEM] * len(arrays), [((1, TOKENS, QUERY...  4.81 us
  transfers between devices with their start and end apart: 17, of which 11 were waited for; matrix products, arithmetic and copies ran while one was open for 2% of the time, Pallas kernels for 6%

profile of v10, /device:TPU:1, one launch (start us, length us, event | category | flops | bytes accessed | tf_op | source)
XLA Modules:
  0.0 121.5 jit_solution(6056206174082104373)
XLA Ops:
  0.6 6.9 %collective-permute-start = (bf16[128,512]{1,0:T(8,128)(2,1)}, bf16[128,512]{1,0:T(8,128)(2,1)S(1)}, u32[]{:S(2)}, u32[]{:S(2)}) collective-permute-start(bf16[128,512]{1,0:T(8,128)(2,1)} %bitcast.25), channel_id=1, source_target_pairs={{0,48},{16,0},{32,16},{48,32},{64,112},{80,64},{96,80},{112,96},{1... | collective-permute-start | bytes 393224 | tf_op jit(solution)/shard_map/ppermute | solution.py:513
  9.4 5.2 %shard_map.171.send_hbm = bf16[16,16,2688]{2,1,0:T(8,128)(2,1)} custom-call(s32[1]{0:T(128)S(6)} %copy.19.rank_hbm.rank_ref, s32[1,1,16]{2,1,0:T(1,128)} %fusion.route_hbm.route_ref, s32[1,1,16]{2,1,0:T(1,128)} %length_hbm.1, bf16[128,5120]{1,0:T(8,128)(2,1)} %bitcast.32, bf16[128,2560]{1,0:T(8,128)(2,1)} %bitcast.36, bf16[128,2560]{1,0:T(8,128)(2,1)} %bitcast.37, ...), custom_call_target="tpu_custom_call" | custom-call | flops 1000000000 | bytes 60000000 | tf_op jit(solution)/shard_map/pallas_call | solution.py:483
  15.0 4.1 %all-to-all-start = ((bf16[4,64,2688]{2,1,0:T(8,128)(2,1)}), bf16[4,64,2688]{2,1,0:T(8,128)(2,1)S(1)}, u32[]{:S(2)}, u32[]{:S(2)}) async-start(bf16[4,64,2688]{2,1,0:T(8,128)(2,1)} %bitcast.31), calls=%async_computation | async-start | bytes 2752512 | tf_op jit(solution)/shard_map/all_to_all | solution.py:520
  20.1 2.7 %collective-permute-start.2 = (bf16[128,512]{1,0:T(8,128)(2,1)S(1)}, bf16[128,512]{1,0:T(8,128)(2,1)S(1)}, u32[]{:S(2)}, u32[]{:S(2)}) collective-permute-start(bf16[128,512]{1,0:T(8,128)(2,1)S(1)} %bitcast.29), channel_id=1, source_target_pairs={{0,48},{16,0},{32,16},{48,32},{64,112},{80,64},{96,80},{112,96},{1... | collective-permute-start | bytes 393224 | tf_op jit(solution)/shard_map/ppermute | solution.py:513
  22.8 2.0 %collective-permute-start.3 = (bf16[128,512]{1,0:T(8,128)(2,1)S(1)}, bf16[128,512]{1,0:T(8,128)(2,1)S(1)}, u32[]{:S(2)}, u32[]{:S(2)}) collective-permute-start(bf16[128,512]{1,0:T(8,128)(2,1)S(1)} %collective-permute-done.k1_ref), channel_id=1, source_target_pairs={{0,48},{16,0},{32,16},{48,32},{64,112},{80,64},{96,80},{112,96},{1... | collective-permute-start | bytes 393224 | tf_op jit(solution)/shard_map/ppermute | solution.py:513
  25.1 5.4 %collective-permute-done.3.k2_ref = bf16[128,512]{1,0:T(8,128)(2,1)S(1)} collective-permute-done((bf16[128,512]{1,0:T(8,128)(2,1)S(1)}, bf16[128,512]{1,0:T(8,128)(2,1)S(1)}, u32[]{:S(2)}, u32[]{:S(2)}) %collective-permute-start.3) | collective-permute-done | bytes 131104 | tf_op jit(solution)/shard_map/ppermute | solution.py:513
  30.5 4.9 %collective-permute-done.4.v2_ref = bf16[128,512]{1,0:T(8,128)(2,1)S(1)} collective-permute-done((bf16[128,512]{1,0:T(8,128)(2,1)S(1)}, bf16[128,512]{1,0:T(8,128)(2,1)S(1)}, u32[]{:S(2)}, u32[]{:S(2)}) %collective-permute-start.4) | collective-permute-done | bytes 131104 | tf_op jit(solution)/shard_map/ppermute | solution.py:513
  35.4 4.6 %shard_map.173 = (bf16[256,1408]{1,0:T(8,128)(2,1)}, f32[128,1024]{1,0:T(8,128)}, bf16[128,1024]{1,0:T(8,128)(2,1)}, bf16[128,1024]{1,0:T(8,128)(2,1)}, bf16[128...) custom-call(bf16[256,2688]{1,0:T(8,128)(2,1)S(1)} %bitcast.21, bf16[128,512]{1,0:T(8,128)(2,1)S(1)} %bitcast.27, ...), custom_call_target="tpu_custom_call" | custom-call | tf_op jit(solution)/shard_map/pallas_call | solution.py:502
  40.0 4.4 %all-to-all-start.1 = ((bf16[4,64,1408]{2,1,0:T(8,128)(2,1)}), bf16[4,64,1408]{2,1,0:T(8,128)(2,1)S(1)}, u32[]{:S(2)}, u32[]{:S(2)}) async-start(bf16[4,64,1408]{2,1,0:T(8,128)(2,1)} %bitcast.35), calls=%async_computation.1 | async-start | bytes 1441792 | tf_op jit(solution)/shard_map/all_to_all | solution.py:520
  45.8 2.3 %collective-permute-start.7 = (bf16[128,512]{1,0:T(8,128)(2,1)S(1)}, bf16[128,512]{1,0:T(8,128)(2,1)S(1)}, u32[]{:S(2)}, u32[]{:S(2)}) collective-permute-start(bf16[128,512]{1,0:T(8,128)(2,1)S(1)} %copy-done.6), channel_id=1, source_target_pairs={{0,48},{16,0},{32,16},{48,32},{64,112},{80,64},{96,80},{112,96},{1... | collective-permute-start | bytes 393224 | tf_op jit(solution)/shard_map/ppermute | solution.py:513
  48.1 2.2 %shard_map.172 = (bf16[256,2688]{1,0:T(8,128)(2,1)S(1)}, bf16[256,256]{1,0:T(8,128)(2,1)S(1)}, bf16[256,256]{1,0:T(8,128)(2,1)S(1)}, bf16[256,256]{1,0:T(8,128)(2,1)S(1)}, f32[3,64,128]{2,1,0:T(8,128)S(1)}) custom-call(s32[1]{0:T(128)S(6)} %copy.19.rank_hbm.rank_ref, s32[1,1,16]{2,1,0:T(1,128)S(1)} %copy-done.2, s32[1]{0:T(128)} %bitcast.1.core_ref, ...), custom_call_target="tpu_custom_call" | custom-call | tf_op jit(solution)/shard_map/pallas_call | solution.py:525
  50.5 3.0 %all-to-all-done.1 = bf16[4,64,1408]{2,1,0:T(8,128)(2,1)S(1)} async-done(((bf16[4,64,1408]{2,1,0:T(8,128)(2,1)}), bf16[4,64,1408]{2,1,0:T(8,128)(2,1)S(1)}, u32[]{:S(2)}, u32[]{:S(2)}) %all-to-all-start.1) | async-done | bytes 720928 | tf_op jit(solution)/shard_map/all_to_all | solution.py:520
  53.5 4.8 %shard_map.174 = (bf16[1,128,2560]{2,1,0:T(8,128)(2,1)}, bf16[1,128,512]{2,1,0:T(8,128)(2,1)}, bf16[1,128,512]{2,1,0:T(8,128)(2,1)}, bf16[2048,128]{1,0:T(8,128)(2,1)S(1)}, bf16[2048,128]{1,0:T(8,128)(2,1)S(1)}) custom-call(bf16[128,5120]{1,0:T(8,128)(2,1)} %bitcast.33, bf16[64,2560]{1,0:T(8,128)(2,1)} %wu_hbm.3, ...), custom_call_target="tpu_custom_call" | custom-call | tf_op jit(solution)/shard_map/pallas_call | solution.py:545
  58.3 3.5 %collective-permute-start.8 = (bf16[2048,128]{1,0:T(8,128)(2,1)S(1)}, bf16[2048,128]{1,0:T(8,128)(2,1)S(1)}, u32[]{:S(2)}, u32[]{:S(2)}) collective-permute-start(bf16[2048,128]{1,0:T(8,128)(2,1)S(1)} %get-tuple-element.51), channel_id=1, source_target_pairs={{0,1},{1,0},{2,3},{3,2},{4,5},{5,4},{6,7},{7,6},{8,9},{9,8},{10,11... | collective-permute-start | bytes 1572872 | tf_op jit(solution)/shard_map/ppermute | solution.py:576
  63.5 18.6 %all_to_all.20 = bf16[32,64,128]{2,1,0:T(8,128)(2,1)S(1)} all-to-all(bf16[32,64,128]{2,1,0:T(8,128)(2,1)S(1)} %bitcast.34), channel_id=1, replica_groups={{0,2,4,6,8,10,12,14,64,66,68,70,72,74,76,78,128,130,132,134,136,138,140..., dimensions={0} | all-to-all | bytes 1048576 | tf_op jit(solution)/shard_map/all_to_all | solution.py:594
  82.3 1.6 %collective-permute-start.9 = (f32[64,128]{1,0:T(8,128)S(1)}, f32[64,128]{1,0:T(8,128)S(1)}, u32[]{:S(2)}, u32[]{:S(2)}) collective-permute-start(f32[64,128]{1,0:T(8,128)S(1)} %convert_reduce_fusion), channel_id=1, source_target_pairs={{0,16},{16,0},{32,48},{48,32},{64,80},{80,64},{96,112},{112,96},{1... | collective-permute-start | bytes 98312 | tf_op jit(solution)/shard_map/ppermute | solution.py:596
  83.9 2.5 %collective-permute-done.9 = f32[64,128]{1,0:T(8,128)S(1)} collective-permute-done((f32[64,128]{1,0:T(8,128)S(1)}, f32[64,128]{1,0:T(8,128)S(1)}, u32[]{:S(2)}, u32[]{:S(2)}) %collective-permute-start.9) | collective-permute-done | bytes 32800 | tf_op jit(solution)/shard_map/ppermute | solution.py:596
  86.4 2.3 %collective-permute-start.10 = (f32[64,128]{1,0:T(8,128)S(1)}, f32[64,128]{1,0:T(8,128)S(1)}, u32[]{:S(2)}, u32[]{:S(2)}) collective-permute-start(f32[64,128]{1,0:T(8,128)S(1)} %add.43), channel_id=1, source_target_pairs={{0,48},{16,32},{32,16},{48,0},{64,112},{80,96},{96,80},{112,64},{1... | collective-permute-start | bytes 98312 | tf_op jit(solution)/shard_map/ppermute | solution.py:596
  88.7 2.6 %collective-permute-done.10 = f32[64,128]{1,0:T(8,128)S(1)} collective-permute-done((f32[64,128]{1,0:T(8,128)S(1)}, f32[64,128]{1,0:T(8,128)S(1)}, u32[]{:S(2)}, u32[]{:S(2)}) %collective-permute-start.10) | collective-permute-done | bytes 32800 | tf_op jit(solution)/shard_map/ppermute | solution.py:596
  92.2 4.3 %all-to-all-start.3 = ((bf16[32,64,128]{2,1,0:T(8,128)(2,1)}), bf16[32,64,128]{2,1,0:T(8,128)(2,1)S(1)}, u32[]{:S(2)}, u32[]{:S(2)}) async-start(bf16[32,64,128]{2,1,0:T(8,128)(2,1)} %broadcast_in_dim.16), calls=%async_computation.3 | async-start | bytes 1048576 | tf_op jit(solution)/shard_map/all_to_all | solution.py:598
  96.6 2.7 %collective-permute-start.12 = (bf16[128,1024]{1,0:T(8,128)(2,1)S(1)}, bf16[128,1024]{1,0:T(8,128)(2,1)S(1)}, u32[]{:S(2)}, u32[]{:S(2)}) collective-permute-start(bf16[128,1024]{1,0:T(8,128)(2,1)S(1)} %pad_maximum_fusion.1), channel_id=1, source_target_pairs={{0,48},{16,0},{32,16},{48,32},{64,112},{80,64},{96,80},{112,96},{1... | collective-permute-start | bytes 786440 | tf_op jit(solution)/shard_map/ppermute | solution.py:513
  99.4 3.5 %collective-permute-done.12 = bf16[128,1024]{1,0:T(8,128)(2,1)S(1)} collective-permute-done((bf16[128,1024]{1,0:T(8,128)(2,1)S(1)}, bf16[128,1024]{1,0:T(8,128)(2,1)S(1)}, u32[]{:S(2)}, u32[]{:S(2)}) %collective-permute-start.12) | collective-permute-done | bytes 262176 | tf_op jit(solution)/shard_map/ppermute | solution.py:513
  102.9 12.3 %collective-permute-done.11 = bf16[128,1024]{1,0:T(8,128)(2,1)S(1)} collective-permute-done((bf16[128,1024]{1,0:T(8,128)(2,1)S(1)}, bf16[128,1024]{1,0:T(8,128)(2,1)S(1)}, u32[]{:S(2)}, u32[]{:S(2)}) %collective-permute-start.11) | collective-permute-done | bytes 262176 | tf_op jit(solution)/shard_map/ppermute | solution.py:513
  115.2 3.4 %collective-permute-start.13 = (bf16[2048,128]{1,0:T(8,128)(2,1)S(1)}, bf16[2048,128]{1,0:T(8,128)(2,1)S(1)}, u32[]{:S(2)}, u32[]{:S(2)}) collective-permute-start(bf16[2048,128]{1,0:T(8,128)(2,1)S(1)} %bitcast.23), channel_id=1, source_target_pairs={{0,1},{1,0},{2,3},{3,2},{4,5},{5,4},{6,7},{7,6},{8,9},{9,8},{10,11... | collective-permute-start | bytes 1572872 | tf_op jit(solution)/shard_map/ppermute | solution.py:576
  (43 shorter events, 10.2 us)
Async XLA Ops:
  0.6 14.0 %collective-permute-start = (bf16[128,512]{1,0:T(8,128)(2,1)}, bf16[128,512]{1,0:T(8,128)(2,1)S(1)}, u32[]{:S(2)}, u32[]{:S(2)}) collective-permute-start(bf16[128,512]{1,0:T(8,128)(2,1)} %bitcast.25), channel_id=1, source_target_pairs={{0,48},{16,0},{32,16},{48,32},{64,112},{80,64},{96,80},{112,96},{1... | collective-permute-start | bytes 393224 | tf_op jit(solution)/shard_map/ppermute | solution.py:513
  7.6 7.5 %collective-permute-start.1 = (bf16[128,512]{1,0:T(8,128)(2,1)}, bf16[128,512]{1,0:T(8,128)(2,1)S(1)}, u32[]{:S(2)}, u32[]{:S(2)}) collective-permute-start(bf16[128,512]{1,0:T(8,128)(2,1)} %bitcast.28), channel_id=1, source_target_pairs={{0,16},{16,32},{32,48},{48,0},{64,80},{80,96},{96,112},{112,64},{1... | collective-permute-start | bytes 393224 | tf_op jit(solution)/shard_map/ppermute | solution.py:513
  15.0 5.1 %copy-start.1 = (bf16[1,128,512]{2,1,0:T(8,128)(2,1)S(1)}, bf16[1,128,512]{2,1,0:T(8,128)(2,1)}, u32[]{:S(2)}) copy-start(bf16[1,128,512]{2,1,0:T(8,128)(2,1)} %param.18) | copy-start | bytes 393220
  15.0 20.4 %all-to-all-start = ((bf16[4,64,2688]{2,1,0:T(8,128)(2,1)}), bf16[4,64,2688]{2,1,0:T(8,128)(2,1)S(1)}, u32[]{:S(2)}, u32[]{:S(2)}) async-start(bf16[4,64,2688]{2,1,0:T(8,128)(2,1)} %bitcast.31), calls=%async_computation | async-start | bytes 2752512 | tf_op jit(solution)/shard_map/all_to_all | solution.py:520
  19.2 5.9 %collective-permute-start.5 = (bf16[128,512]{1,0:T(8,128)(2,1)S(1)}, bf16[128,512]{1,0:T(8,128)(2,1)S(1)}, u32[]{:S(2)}, u32[]{:S(2)}) collective-permute-start(bf16[128,512]{1,0:T(8,128)(2,1)S(1)} %bitcast.26), channel_id=1, source_target_pairs={{0,16},{16,32},{32,48},{48,0},{64,80},{80,96},{96,112},{112,64},{1... | collective-permute-start | bytes 393224 | tf_op jit(solution)/shard_map/ppermute | solution.py:513
  20.1 5.0 %collective-permute-start.2 = (bf16[128,512]{1,0:T(8,128)(2,1)S(1)}, bf16[128,512]{1,0:T(8,128)(2,1)S(1)}, u32[]{:S(2)}, u32[]{:S(2)}) collective-permute-start(bf16[128,512]{1,0:T(8,128)(2,1)S(1)} %bitcast.29), channel_id=1, source_target_pairs={{0,48},{16,0},{32,16},{48,32},{64,112},{80,64},{96,80},{112,96},{1... | collective-permute-start | bytes 393224 | tf_op jit(solution)/shard_map/ppermute | solution.py:513
  22.8 7.8 %collective-permute-start.3 = (bf16[128,512]{1,0:T(8,128)(2,1)S(1)}, bf16[128,512]{1,0:T(8,128)(2,1)S(1)}, u32[]{:S(2)}, u32[]{:S(2)}) collective-permute-start(bf16[128,512]{1,0:T(8,128)(2,1)S(1)} %collective-permute-done.k1_ref), channel_id=1, source_target_pairs={{0,48},{16,0},{32,16},{48,32},{64,112},{80,64},{96,80},{112,96},{1... | collective-permute-start | bytes 393224 | tf_op jit(solution)/shard_map/ppermute | solution.py:513
  24.8 10.6 %collective-permute-start.4 = (bf16[128,512]{1,0:T(8,128)(2,1)S(1)}, bf16[128,512]{1,0:T(8,128)(2,1)S(1)}, u32[]{:S(2)}, u32[]{:S(2)}) collective-permute-start(bf16[128,512]{1,0:T(8,128)(2,1)S(1)} %collective-permute-done.1.v3_ref), channel_id=1, source_target_pairs={{0,16},{16,32},{32,48},{48,0},{64,80},{80,96},{96,112},{112,64},{1... | collective-permute-start | bytes 393224 | tf_op jit(solution)/shard_map/ppermute | solution.py:513
  35.4 12.7 %copy-start.2 = (s32[1,1,16]{2,1,0:T(1,128)S(1)}, s32[1,1,16]{2,1,0:T(1,128)}, u32[]{:S(2)}) copy-start(s32[1,1,16]{2,1,0:T(1,128)} %fusion.route_hbm.route_ref) | copy-start | bytes 196
  40.0 4.4 %copy-start.7 = (bf16[128,512]{1,0:T(8,128)(2,1)S(1)}, bf16[128,512]{1,0:T(8,128)(2,1)}, u32[]{:S(2)}) copy-start(bf16[128,512]{1,0:T(8,128)(2,1)} %get-tuple-element.43) | copy-start | bytes 393220
  40.0 5.8 %copy-start.6 = (bf16[128,512]{1,0:T(8,128)(2,1)S(1)}, bf16[128,512]{1,0:T(8,128)(2,1)}, u32[]{:S(2)}) copy-start(bf16[128,512]{1,0:T(8,128)(2,1)} %get-tuple-element.44) | copy-start | bytes 393220
  40.0 13.5 %all-to-all-start.1 = ((bf16[4,64,1408]{2,1,0:T(8,128)(2,1)}), bf16[4,64,1408]{2,1,0:T(8,128)(2,1)S(1)}, u32[]{:S(2)}, u32[]{:S(2)}) async-start(bf16[4,64,1408]{2,1,0:T(8,128)(2,1)} %bitcast.35), calls=%async_computation.1 | async-start | bytes 1441792 | tf_op jit(solution)/shard_map/all_to_all | solution.py:520
  44.4 5.9 %collective-permute-start.6 = (bf16[128,512]{1,0:T(8,128)(2,1)S(1)}, bf16[128,512]{1,0:T(8,128)(2,1)S(1)}, u32[]{:S(2)}, u32[]{:S(2)}) collective-permute-start(bf16[128,512]{1,0:T(8,128)(2,1)S(1)} %copy-done.7), channel_id=1, source_target_pairs={{0,16},{16,32},{32,48},{48,0},{64,80},{80,96},{96,112},{112,64},{1... | collective-permute-start | bytes 393224 | tf_op jit(solution)/shard_map/ppermute | solution.py:513
  45.8 4.7 %collective-permute-start.7 = (bf16[128,512]{1,0:T(8,128)(2,1)S(1)}, bf16[128,512]{1,0:T(8,128)(2,1)S(1)}, u32[]{:S(2)}, u32[]{:S(2)}) collective-permute-start(bf16[128,512]{1,0:T(8,128)(2,1)S(1)} %copy-done.6), channel_id=1, source_target_pairs={{0,48},{16,0},{32,16},{48,32},{64,112},{80,64},{96,80},{112,96},{1... | collective-permute-start | bytes 393224 | tf_op jit(solution)/shard_map/ppermute | solution.py:513
  58.3 5.1 %collective-permute-start.8 = (bf16[2048,128]{1,0:T(8,128)(2,1)S(1)}, bf16[2048,128]{1,0:T(8,128)(2,1)S(1)}, u32[]{:S(2)}, u32[]{:S(2)}) collective-permute-start(bf16[2048,128]{1,0:T(8,128)(2,1)S(1)} %get-tuple-element.51), channel_id=1, source_target_pairs={{0,1},{1,0},{2,3},{3,2},{4,5},{5,4},{6,7},{7,6},{8,9},{9,8},{10,11... | collective-permute-start | bytes 1572872 | tf_op jit(solution)/shard_map/ppermute | solution.py:576
  82.2 14.3 %copy-start.4 = (bf16[128,1024]{1,0:T(8,128)(2,1)S(1)}, bf16[128,1024]{1,0:T(8,128)(2,1)}, u32[]{:S(2)}) copy-start(bf16[128,1024]{1,0:T(8,128)(2,1)} %get-tuple-element.52) | copy-start | bytes 786436
  82.2 14.3 %copy-start.5 = (bf16[128,1024]{1,0:T(8,128)(2,1)S(1)}, bf16[128,1024]{1,0:T(8,128)(2,1)}, u32[]{:S(2)}) copy-start(bf16[128,1024]{1,0:T(8,128)(2,1)} %get-tuple-element.54) | copy-start | bytes 786436
  82.3 4.1 %collective-permute-start.9 = (f32[64,128]{1,0:T(8,128)S(1)}, f32[64,128]{1,0:T(8,128)S(1)}, u32[]{:S(2)}, u32[]{:S(2)}) collective-permute-start(f32[64,128]{1,0:T(8,128)S(1)} %convert_reduce_fusion), channel_id=1, source_target_pairs={{0,16},{16,0},{32,48},{48,32},{64,80},{80,64},{96,112},{112,96},{1... | collective-permute-start | bytes 98312 | tf_op jit(solution)/shard_map/ppermute | solution.py:596
  86.4 4.9 %collective-permute-start.10 = (f32[64,128]{1,0:T(8,128)S(1)}, f32[64,128]{1,0:T(8,128)S(1)}, u32[]{:S(2)}, u32[]{:S(2)}) collective-permute-start(f32[64,128]{1,0:T(8,128)S(1)} %add.43), channel_id=1, source_target_pairs={{0,48},{16,32},{32,16},{48,0},{64,112},{80,96},{96,80},{112,64},{1... | collective-permute-start | bytes 98312 | tf_op jit(solution)/shard_map/ppermute | solution.py:596
  92.2 23.0 %all-to-all-start.3 = ((bf16[32,64,128]{2,1,0:T(8,128)(2,1)}), bf16[32,64,128]{2,1,0:T(8,128)(2,1)S(1)}, u32[]{:S(2)}, u32[]{:S(2)}) async-start(bf16[32,64,128]{2,1,0:T(8,128)(2,1)} %broadcast_in_dim.16), calls=%async_computation.3 | async-start | bytes 1048576 | tf_op jit(solution)/shard_map/all_to_all | solution.py:598
  96.5 22.1 %copy-start.3 = (f32[128,1024]{1,0:T(8,128)S(1)}, f32[128,1024]{1,0:T(8,128)}, u32[]{:S(2)}) copy-start(f32[128,1024]{1,0:T(8,128)} %get-tuple-element.49) | copy-start | bytes 1572868
  96.6 6.3 %collective-permute-start.12 = (bf16[128,1024]{1,0:T(8,128)(2,1)S(1)}, bf16[128,1024]{1,0:T(8,128)(2,1)S(1)}, u32[]{:S(2)}, u32[]{:S(2)}) collective-permute-start(bf16[128,1024]{1,0:T(8,128)(2,1)S(1)} %pad_maximum_fusion.1), channel_id=1, source_target_pairs={{0,48},{16,0},{32,16},{48,32},{64,112},{80,64},{96,80},{112,96},{1... | collective-permute-start | bytes 786440 | tf_op jit(solution)/shard_map/ppermute | solution.py:513
  99.3 15.8 %collective-permute-start.11 = (bf16[128,1024]{1,0:T(8,128)(2,1)S(1)}, bf16[128,1024]{1,0:T(8,128)(2,1)S(1)}, u32[]{:S(2)}, u32[]{:S(2)}) collective-permute-start(bf16[128,1024]{1,0:T(8,128)(2,1)S(1)} %pad_maximum_fusion), channel_id=1, source_target_pairs={{0,16},{16,32},{32,48},{48,0},{64,80},{80,96},{96,112},{112,64},{1... | collective-permute-start | bytes 786440 | tf_op jit(solution)/shard_map/ppermute | solution.py:513
  115.2 4.9 %collective-permute-start.13 = (bf16[2048,128]{1,0:T(8,128)(2,1)S(1)}, bf16[2048,128]{1,0:T(8,128)(2,1)S(1)}, u32[]{:S(2)}, u32[]{:S(2)}) collective-permute-start(bf16[2048,128]{1,0:T(8,128)(2,1)S(1)} %bitcast.23), channel_id=1, source_target_pairs={{0,1},{1,0},{2,3},{3,2},{4,5},{5,4},{6,7},{7,6},{8,9},{9,8},{10,11... | collective-permute-start | bytes 1572872 | tf_op jit(solution)/shard_map/ppermute | solution.py:576
  (1 other events, 4.2 us)
